TPU v7x, 128 devices: a whole 4x4x4 slice. The times are simulated.
128 devices in a mesh: row: 8 (over z, core), col: 16 (over y, x).
Axes of the slice: x: 4, y: 4, z: 4, core: 2. Of those that a mesh axis runs over, the one named last changes fastest.
Arguments:
- orbitals: bfloat16 [262144, 1920], P(('row', 'col')), may hold values from -6 to 6
- point_cell: int32 [8, 16, 128], P('row', 'col'), may hold values from 0 to 262143, as said below
- point_count: int32 [8, 16], P('row', 'col'), may hold values from 64 to 128, as said below
- kernel: bfloat16 [8, 16, 128, 8, 16, 128], P('row', None, None, None, 'col'), may hold values from -0.0009765625 to 0.0009765625
Outputs:
- exchange_points: float32 [8, 16, 128, 1920], P('row', 'col')
Inputs may be any that keep to these rules, and one draw needn't show every extreme that they name: `point_cell`: the slots of block (r, c) name distinct cells of slab 16 r + c, that is of [(16 r + c) * 2048, (16 r + c + 1) * 2048); slots at or past the block's count are drawn the same way and not used. `point_count`: some block holds 128 live points in every draw.
All inputs are finite; a program needn't handle non-finite values.
Results may differ from a plain program's by a relative error of at most 0.0029.
Values may be sent and summed in bfloat16 or wider, within the bound.
No kernel may reach another device: no remote copies, remote signals or barrier semaphores. Data moves between devices by JAX's collectives and lax.ppermute only.
A program may use at most 128 MiB of HBM per device.

v0:
```python
import jax
import jax.numpy as jnp
from jax import lax
from jax.sharding import PartitionSpec as P


def point_terms(rows, column_entries, kern):
    gram = lax.dot_general(
        rows, column_entries, (((1,), (1,)), ((), ())), preferred_element_type=jnp.float32
    )
    weighted = (gram * kern.astype(jnp.float32)).astype(jnp.bfloat16)
    return jnp.dot(weighted, column_entries, preferred_element_type=jnp.float32)


def on_device(orbitals, point_cell, point_count, kernel):
    slab = orbitals.shape[0]
    orbital_count = orbitals.shape[1]
    slots = point_cell.shape[2]
    local_cells = point_cell.reshape(slots) % slab
    live = jnp.arange(slots, dtype=jnp.int32) < point_count.reshape(())
    picked = jnp.take(orbitals, local_cells, axis=0)
    orbital_values = jnp.where(live[:, None], picked, jnp.zeros((), picked.dtype))
    phi_block = orbital_values.reshape(1, 1, slots, orbital_count)
    rows_panel = lax.all_gather(phi_block, "col", axis=1, tiled=True).reshape(-1, orbital_count)
    panel_rows = rows_panel.shape[0]
    tile = kernel.reshape(panel_rows, -1)
    cols_panel = lax.all_gather(phi_block, "row", axis=0, tiled=True).reshape(-1, orbital_count)
    terms = point_terms(rows_panel, cols_panel, tile)
    result = lax.psum_scatter(terms, "col", scatter_dimension=0, tiled=True)
    return result.reshape(1, 1, slots, orbital_count)


def solution(mesh):
    in_specs = (
        P(("row", "col"), None),
        P("row", "col", None),
        P("row", "col"),
        P("row", None, None, None, "col", None),
    )
    out_specs = P("row", "col", None, None)
    return jax.shard_map(
        on_device, mesh=mesh, in_specs=in_specs, out_specs=out_specs, check_vma=False
    )
```

profile of v0, /device:TPU:6, one launch (start us, length us, event | category | flops | bytes accessed | tf_op | source)
XLA Modules:
  0.0 260.9 jit_solution(10875046451515075995)
XLA Ops:
  6.5 0.0 all-gather.5.cloned.1.call-start
  7.2 0.7 fusion.5
  7.9 0.7 compare_and_fusion
  8.5 5.7 %gather_fusion = bf16[128,1920]{1,0:T(8,128)(2,1)S(1)} fusion(bf16[2048,1920]{1,0:T(8,128)(2,1)} %param.4, s32[1024]{0:T(1024)S(1)} %pad_clamp_fusion), kind=kCustom, calls=%fused_computation | custom fusion | bytes 983552 | tf_op jit(solution)/shard_map/jit(_take)/gather | solution.py:21
  14.2 0.9 fusion.2
  15.1 0.0 all-gather.5.cloned.1.call-update
  15.2 0.0 all-gather.3.cloned.1.call-start
  15.2 0.9 fusion.9
  16.2 0.0 all-gather.3.cloned.1.call-update
  16.2 0.0 reduce-scatter.2.cloned.1.call-start
  16.2 6.5 %convert.2 = f32[256,8,8,128]{3,2,1,0:T(8,128)} convert(bf16[256,8,8,128]{3,2,1,0:T(8,128)(2,1)} %bitcast.32) | non-fusion elementwise | flops 2097152 | bytes 12582912
  22.7 26.2 %all-gather.5.cloned.1.call-done = bf16[8,1,128,1920]{3,2,1,0:T(8,128)(2,1)} async-done(((bf16[1,1,128,1920]{3,2,1,0:T(8,128)(2,1)}), bf16[8,1,128,1920]{3,2,1,0:T(8,128)(2,1)}) %all-gather.5.cloned.1.call-update) | async-done | bytes 3932176 | tf_op jit(solution)/shard_map/all_gather | solution.py:27
  48.9 70.4 %all-gather.3.cloned.1.call-done = bf16[1,16,128,1920]{3,2,0,1:T(8,128)(2,1)} async-done(((bf16[1,1,128,1920]{3,2,0,1:T(8,128)(2,1)}), bf16[1,16,128,1920]{3,2,0,1:T(8,128)(2,1)}) %all-gather.3.cloned.1.call-update) | async-done | bytes 7864336 | tf_op jit(solution)/shard_map/all_gather | solution.py:24
  119.2 30.3 %fusion.1 = f32[2048,1920]{1,0:T(8,128)} fusion(bf16[1024,1920]{1,0:T(8,128)(2,1)} %bitcast.34, f32[256,8,8,128]{3,2,1,0:T(8,128)} %convert.2, bf16[2048,1920]{1,0:T(8,128)(2,1)} %bitcast.33), kind=kOutput, calls=%fused_computation.3 | convolution fusion | flops 16110321664 | bytes 35913728 | tf_op jit(solution)/shard_map/dot_general | solution.py:12
  149.6 0.0 reduce-scatter.2.cloned.1.call-update
  149.6 104.8 %reduce-scatter.2.cloned.1.call-done = f32[128,1920]{1,0:T(8,128)} async-done(((f32[2048,1920]{1,0:T(8,128)}), f32[128,1920]{1,0:T(8,128)}) %reduce-scatter.2.cloned.1.call-update) | async-done | bytes 983056 | tf_op jit(solution)/shard_map/reduce_scatter | solution.py:29
  (1 shorter events, 0.0 us)
Async XLA Ops:
  6.5 42.4 %all-gather.5.cloned.1.call-start = ((), (), s32[]{:S(2)}) async-start(), calls=%async_computation.2 | async-start | bytes 4423680 | tf_op jit(solution)/shard_map/all_gather | solution.py:27
  15.2 104.1 %all-gather.3.cloned.1.call-start = ((), (), s32[]{:S(2)}) async-start(), calls=%async_computation.1 | async-start | bytes 8355840 | tf_op jit(solution)/shard_map/all_gather | solution.py:24
  16.2 238.2 %reduce-scatter.2.cloned.1.call-start = ((), (), s32[]{:S(2)}) async-start(), calls=%async_computation.3 | async-start | bytes 16711680 | tf_op jit(solution)/shard_map/reduce_scatter | solution.py:29
Sparse Core Ops, SparseCore 0:
  15.3 33.5 all-gather.4
  51.0 68.1 all-gather.2
  149.7 104.6 reduce-scatter.1
where the time goes:
time: 262 us; the launch traced here: 261 us
  waiting for transfers between devices  201 us (77%)
  matrix products  30.3 us (12%)
  between operations  13.8 us (5%)
  other arithmetic  9.7 us (4%)
  local copies, waits for them, and re-layouts  5.67 us (2%)
    reduce_scatter x1, waiting for transfers between devices, on_device(): result = lax.psum_scatter(terms, 'col', scatter_dimension=0, tiled=True)  105 us
    all_gather x1, waiting for transfers between devices, on_device(): lax.all_gather(phi_block, 'col', axis=1, tiled=True)  70.4 us
    dot_general x1, matrix products, point_terms(): return jnp.dot(weighted, column_entries, preferred_element_type=jnp.float32)  30.3 us
    all_gather x1, waiting for transfers between devices, on_device(): lax.all_gather(phi_block, 'row', axis=0, tiled=True)  26.2 us
    unnamed x1, other arithmetic  6.49 us
    gather x1, local copies, waits for them, and re-layouts, on_device(): picked = jnp.take(orbitals, local_cells, axis=0)  5.67 us
  transfers between devices with their start and end apart: 3, of which 3 were waited for; matrix products, arithmetic and copies ran while one was open for 3% of the time, Pallas kernels for 0%

commit v1 on v0

v1 whole, which is shorter than its diff:
```python
import jax
import jax.numpy as jnp
from jax import lax
from jax.experimental import pallas as pl
from jax.experimental.pallas import tpu as pltpu
from jax.sharding import PartitionSpec as P

SIDE = 4
VMEM = 60 * 1024 * 1024


def pick_body(count_ref, cell_ref, orb_ref, out_ref, acc_ref):
    step = pl.program_id(0)
    part = orb_ref.shape[0]
    slots = out_ref.shape[0]
    wanted = jnp.transpose(jnp.broadcast_to(cell_ref[...], (slots, slots)))
    slot = lax.broadcasted_iota(jnp.int32, (slots, slots), 0)
    lane = lax.broadcasted_iota(jnp.int32, (slots, slots), 1)
    wanted = jnp.where(slot < count_ref[0], wanted, -1)
    hits = [
        (wanted == lane + (step * part + k * slots)).astype(jnp.float32).astype(jnp.bfloat16)
        for k in range(part // slots)
    ]
    term = jnp.dot(
        jnp.concatenate(hits, axis=1), orb_ref[...], preferred_element_type=jnp.float32
    )

    @pl.when(step == 0)
    def _():
        acc_ref[...] = term

    @pl.when(step > 0)
    def _():
        acc_ref[...] += term

    @pl.when(step == pl.num_programs(0) - 1)
    def _():
        out_ref[...] = acc_ref[...].astype(out_ref.dtype)


def pick(orbitals, cells, count):
    slab, width = orbitals.shape
    slots = cells.shape[1]
    part = 512
    return pl.pallas_call(
        pick_body,
        grid_spec=pltpu.PrefetchScalarGridSpec(
            num_scalar_prefetch=1,
            grid=(slab // part,),
            in_specs=[
                pl.BlockSpec((1, slots), lambda i, n: (0, 0)),
                pl.BlockSpec((part, width), lambda i, n: (i, 0)),
            ],
            out_specs=pl.BlockSpec((slots, width), lambda i, n: (0, 0)),
            scratch_shapes=[pltpu.VMEM((slots, width), jnp.float32)],
        ),
        out_shape=jax.ShapeDtypeStruct((slots, width), orbitals.dtype),
        compiler_params=pltpu.CompilerParams(vmem_limit_bytes=VMEM),
        name="pick",
    )(count, cells, orbitals)


def terms(groups, order, panel, tile, sizes, dtypes):
    rows = sum(g.shape[0] for g in groups)
    width = panel.shape[1]
    cols = panel.shape[0]
    slots = tile.shape[1]
    blocks = rows // slots
    col_part, out_part = 256, 640
    n_groups = len(groups)

    def body(order_ref, *refs):
        ins, rest = refs[:n_groups], refs[n_groups:]
        panel_ref, tiles, rest = rest[0], rest[1 : 1 + blocks], rest[1 + blocks :]
        outs, stacked, weighted = rest[: len(sizes)], rest[-2], rest[-1]
        at = 0
        for ref in ins:
            stacked[pl.ds(at, ref.shape[0]), :] = ref[...]
            at += ref.shape[0]
        for k in range(cols // col_part):
            span = pl.ds(k * col_part, col_part)
            gram = lax.dot_general(
                stacked[...],
                panel_ref[span, :],
                (((1,), (1,)), ((), ())),
                preferred_element_type=jnp.float32,
            )
            for j in range(blocks):
                part = gram[j * slots : (j + 1) * slots, :]
                weighted[pl.ds(j * slots, slots), span] = (
                    part * tiles[j][0, :, span].astype(jnp.float32)
                ).astype(jnp.bfloat16)
        for k in range(width // out_part):
            span = pl.ds(k * out_part, out_part)
            term = jnp.dot(weighted[...], panel_ref[:, span], preferred_element_type=jnp.float32)
            at = 0
            for ref, size in zip(outs, sizes):
                ref[:, span] = term[at : at + size, :].astype(ref.dtype)
                at += size

    def whole(shape):
        return pl.BlockSpec(shape, lambda i, o: (0, 0))

    def block_spec(j):
        return pl.BlockSpec((1, slots, cols), lambda i, o: (o[j], 0, 0))

    return pl.pallas_call(
        body,
        grid_spec=pltpu.PrefetchScalarGridSpec(
            num_scalar_prefetch=1,
            grid=(1,),
            in_specs=[whole(g.shape) for g in groups]
            + [whole(panel.shape)]
            + [block_spec(j) for j in range(blocks)],
            out_specs=[whole((size, width)) for size in sizes],
            scratch_shapes=[
                pltpu.VMEM((rows, width), jnp.bfloat16),
                pltpu.VMEM((rows, cols), jnp.bfloat16),
            ],
        ),
        out_shape=[jax.ShapeDtypeStruct((s, width), d) for s, d in zip(sizes, dtypes)],
        compiler_params=pltpu.CompilerParams(vmem_limit_bytes=VMEM),
        cost_estimate=pl.CostEstimate(
            flops=4 * rows * cols * width, bytes_accessed=8 * 1024 * 1024, transcendentals=0
        ),
        name="terms",
    )(order, *groups, panel, *([tile] * blocks))


def plane_perm(n_row, n_col, first, second):
    pairs = []
    for r in range(n_row):
        dx, dy = (first, second) if r % 2 == 0 else (second, first)
        for c in range(n_col):
            y, x = c // SIDE, c % SIDE
            to = ((y + dy) % SIDE) * SIDE + (x + dx) % SIDE
            pairs.append((r * n_col + c, r * n_col + to))
    return pairs


def solution(mesh):
    n_row, n_col = mesh.shape["row"], mesh.shape["col"]

    def first(a, by):
        return lax.ppermute(a, ("row", "col"), plane_perm(n_row, n_col, by, 0))

    def second(a, by):
        return lax.ppermute(a, ("row", "col"), plane_perm(n_row, n_col, 0, by))

    def on_device(orbitals, point_cell, point_count, kernel):
        slab, width = orbitals.shape
        slots = point_cell.shape[2]
        cells = lax.rem(point_cell.reshape(1, slots), slab)
        own = pick(orbitals, cells, point_count.reshape(1))

        panel = lax.all_gather(own, "row", axis=0, tiled=True)
        tile = kernel.reshape(n_col, slots, -1)

        core = lax.axis_index("row") % 2
        col = lax.axis_index("col")
        y, x = col // SIDE, col % SIDE

        def block_at(a, b):
            dx = jnp.where(core == 0, a, b)
            dy = jnp.where(core == 0, b, a)
            return ((y + dy) % SIDE) * SIDE + (x + dx) % SIDE

        def order_of(b, offsets=(0, -1, 1, 2)):
            return jnp.stack([block_at(a, b) for a in offsets]).astype(jnp.int32)

        low, high, far = first(own, 1), first(own, -1), first(own, 2)
        near = jnp.concatenate([own, low], axis=0)
        wide = jnp.concatenate([high, far], axis=0)
        near_low, wide_high = second(near, 1), second(wide, -1)
        wide_low, near_high = second(wide, 1), second(near, -1)
        near_far, wide_far = second(near_low, 1), second(wide_high, -1)

        bf, f32 = jnp.bfloat16, jnp.float32

        def reduced(group, b):
            mine, to_low, to_high, to_far = terms(
                group, order_of(b), panel, tile, (slots,) * 4, (f32, bf, bf, bf)
            )
            got = first(to_low, -1), first(to_high, 1), first(to_far, 2)
            return mine + got[0].astype(f32) + got[1].astype(f32) + got[2].astype(f32)

        here = reduced((near, wide), 0)
        to_low = reduced((near_low, wide_low), -1).astype(bf)
        to_high = reduced((near_high, wide_high), 1).astype(bf)
        to_far = reduced((near_far, wide_far), 2).astype(bf)
        got = second(to_low, -1), second(to_high, 1), second(to_far, 2)
        result = here + got[0].astype(f32) + got[1].astype(f32) + got[2].astype(f32)
        return result.reshape(1, 1, slots, width)

    in_specs = (
        P(("row", "col"), None),
        P("row", "col", None),
        P("row", "col"),
        P("row", None, None, None, "col", None),
    )
    out_specs = P("row", "col", None, None)
    return jax.shard_map(
        on_device, mesh=mesh, in_specs=in_specs, out_specs=out_specs, check_vma=False
    )
```

time: 262 us -> 164 us (0.63)
  waiting for transfers between devices: 201 us -> 59.1 us
  Pallas kernels: 0 us -> 45.3 us
  matrix products: 30.3 us -> 0 us
  starting transfers between devices: 0.09 us -> 29.9 us
    reduce_scatter x1 -> x0, waiting for transfers between devices: 105 us -> none  [on_device(): result = lax.psum_scatter(terms, 'col', scatter_dimension=0, tiled=True)]
    all_gather x2 -> x1, waiting for transfers between devices: 96.5 us -> 0.01 us  [on_device(): panel = lax.all_gather(own, 'row', axis=0, tiled=True)]
    ppermute x0 -> x24, waiting for transfers between devices: none -> 59 us  [the longest x15 42.1 us: first(): return lax.ppermute(a, ('row', 'col'), plane_perm(n_row, n_col, by, 0))]
    pallas_call x0 -> x5, Pallas kernels: none -> 45.3 us  [the longest x4 39.5 us: terms(): pl.pallas_call(body, grid_spec=pltpu.PrefetchScalarGridSpec(num_scalar_pr...]
    dot_general x1 -> x0, matrix products: 30.3 us -> none  [point_terms(): return jnp.dot(weighted, column_entries, preferred_element_type=jnp.float32)]
    ppermute x0 -> x24, starting transfers between devices: none -> 29.9 us  [the longest x15 18.4 us: first(): return lax.ppermute(a, ('row', 'col'), plane_perm(n_row, n_col, by, 0))]
    reshape x0 -> x1, local copies, waits for them, and re-layouts: none -> 7.32 us  [on_device(): tile = kernel.reshape(n_col, slots, -1)]
    unnamed x1 -> x0, other arithmetic: 6.49 us -> none
  transfers between devices with their start and end apart: 3 -> 25, of which waited for: 3 -> 8; matrix products, arithmetic and copies ran while one was open for 3% -> 8% of each run, Pallas kernels for 0% -> 24%
where the time goes in v1:
time: 164 us
  waiting for transfers between devices  59.1 us (36%)
  Pallas kernels  45.3 us (28%)
  starting transfers between devices  29.9 us (18%)
  between operations  14.2 us (9%)
  other arithmetic  7.94 us (5%)
  local copies, waits for them, and re-layouts  7.44 us (5%)
    ppermute x15, waiting for transfers between devices, first(): return lax.ppermute(a, ('row', 'col'), plane_perm(n_row, n_col, by, 0))  42.1 us
    pallas_call x4, Pallas kernels, terms(): pl.pallas_call(body, grid_spec=pltpu.PrefetchScalarGridSpec(num_scalar_pr...  39.5 us
    ppermute x15, starting transfers between devices, first(): return lax.ppermute(a, ('row', 'col'), plane_perm(n_row, n_col, by, 0))  18.4 us
    ppermute x9, waiting for transfers between devices, second(): return lax.ppermute(a, ('row', 'col'), plane_perm(n_row, n_col, 0, by))  16.9 us
    ppermute x9, starting transfers between devices, second(): return lax.ppermute(a, ('row', 'col'), plane_perm(n_row, n_col, 0, by))  11.5 us
    reshape x1, local copies, waits for them, and re-layouts, on_device(): tile = kernel.reshape(n_col, slots, -1)  7.32 us
    pallas_call x1, Pallas kernels, pick(): pl.pallas_call(pick_body, grid_spec=pltpu.PrefetchScalarGridSpec(num_scal...  5.87 us
  transfers between devices with their start and end apart: 25, of which 8 were waited for; matrix products, arithmetic and copies ran while one was open for 8% of the time, Pallas kernels for 24%

profile of v1, /device:TPU:6, one launch (start us, length us, event | category | flops | bytes accessed | tf_op | source)
XLA Modules:
  0.0 163.8 jit_solution(14554817266054463468)
XLA Ops:
  8.4 5.9 %pick.1 = bf16[128,1920]{1,0:T(8,128)(2,1)} custom-call(s32[1]{0:T(128)} %bitcast.25.count_ref, s32[1,128]{1,0:T(1,128)} %compare_select_fusion.cell_ref, bf16[2048,1920]{1,0:T(8,128)(2,1)} %orb_ref.1), custom_call_target="tpu_custom_call" | custom-call | tf_op jit(solution)/shard_map/pick/pallas_call | solution.py:45
  16.2 2.2 %collective-permute-start = (bf16[128,1920]{1,0:T(8,128)(2,1)}, bf16[128,1920]{1,0:T(8,128)(2,1)S(1)}, u32[]{:S(2)}, u32[]{:S(2)}) collective-permute-start(bf16[128,1920]{1,0:T(8,128)(2,1)} %pick.1), channel_id=1, source_target_pairs={{0,1},{1,2},{2,3},{3,0},{4,5},{5,6},{6,7},{7,4},{8,9},{9,10},{10,1... | collective-permute-start | bytes 1474568 | tf_op jit(solution)/shard_map/ppermute | solution.py:145
  18.4 11.5 %collective-permute-done.1 = bf16[128,1920]{1,0:T(8,128)(2,1)S(1)} collective-permute-done((bf16[128,1920]{1,0:T(8,128)(2,1)}, bf16[128,1920]{1,0:T(8,128)(2,1)S(1)}, u32[]{:S(2)}, u32[]{:S(2)}) %collective-permute-start.1) | collective-permute-done | bytes 491552 | tf_op jit(solution)/shard_map/ppermute | solution.py:145
  29.9 3.1 %collective-permute-start.13 = (bf16[256,1920]{1,0:T(8,128)(2,1)S(1)}, bf16[256,1920]{1,0:T(8,128)(2,1)S(1)}, u32[]{:S(2)}, u32[]{:S(2)}) collective-permute-start(bf16[256,1920]{1,0:T(8,128)(2,1)S(1)} %constant_dynamic-update-slice_fusion.refs_1_), channel_id=1, source_target_pairs={{0,12},{1,13},{2,14},{3,15},{4,0},{5,1},{6,2},{7,3},{8,4},{9,5},{1... | collective-permute-start | bytes 2949128 | tf_op jit(solution)/shard_map/ppermute | solution.py:148
  36.5 2.3 %collective-permute-start.12 = (bf16[256,1920]{1,0:T(8,128)(2,1)S(1)}, bf16[256,1920]{1,0:T(8,128)(2,1)}, u32[]{:S(2)}, u32[]{:S(2)}) collective-permute-start(bf16[256,1920]{1,0:T(8,128)(2,1)S(1)} %pad_maximum_fusion.refs_0_), channel_id=1, source_target_pairs={{0,12},{1,13},{2,14},{3,15},{4,0},{5,1},{6,2},{7,3},{8,4},{9,5},{1... | collective-permute-start | bytes 2949128 | tf_op jit(solution)/shard_map/ppermute | solution.py:148
  38.8 7.3 %reshape.62.refs_3_.refs_4_.refs_5_.refs_6_ = bf16[16,128,1024]{2,1,0:T(8,128)(2,1)} reshape(bf16[1,16,128,8,1,128]{5,3,4,2,1,0:T(8,128)(2,1)} %param.7) | data formatting | bytes 8388608 | tf_op jit(solution)/shard_map/reshape | solution.py:157
  47.4 2.0 %collective-permute-start.19 = (bf16[256,1920]{1,0:T(8,128)(2,1)S(1)}, bf16[256,1920]{1,0:T(8,128)(2,1)}, u32[]{:S(2)}, u32[]{:S(2)}) collective-permute-start(bf16[256,1920]{1,0:T(8,128)(2,1)S(1)} %collective-permute-done.13.refs_1_), channel_id=1, source_target_pairs={{0,12},{1,13},{2,14},{3,15},{4,0},{5,1},{6,2},{7,3},{8,4},{9,5},{1... | collective-permute-start | bytes 2949128 | tf_op jit(solution)/shard_map/ppermute | solution.py:148
  49.6 10.5 %collective-permute-done.7.refs_1_ = bf16[256,1920]{1,0:T(8,128)(2,1)} collective-permute-done((bf16[256,1920]{1,0:T(8,128)(2,1)S(1)}, bf16[256,1920]{1,0:T(8,128)(2,1)}, u32[]{:S(2)}, u32[]{:S(2)}) %collective-permute-start.7) | collective-permute-done | bytes 983072 | tf_op jit(solution)/shard_map/ppermute | solution.py:148
  60.2 9.9 %terms.5 = (f32[128,1920]{1,0:T(8,128)}, bf16[128,1920]{1,0:T(8,128)(2,1)}, bf16[128,1920]{1,0:T(8,128)(2,1)}, bf16[128,1920]{1,0:T(8,128)(2,1)}) custom-call(s32[4]{0:T(128)} %pad_add_fusion.1.order_ref, bf16[256,1920]{1,0:T(8,128)(2,1)} %collective-permute-done.6.refs_0_, bf16[256,1920]{1,0:T(8,128)(2,1)} %collective-permute-done.7.refs_1_, ...), custom_call_target="tpu_custom_call" | custom-call | flops 4026531840 | bytes 8388608 | tf_op jit(solution)/shard_map/terms/pallas_call | solution.py:107
  71.2 9.9 %terms.4 = (f32[128,1920]{1,0:T(8,128)}, bf16[128,1920]{1,0:T(8,128)(2,1)}, bf16[128,1920]{1,0:T(8,128)(2,1)}, bf16[128,1920]{1,0:T(8,128)(2,1)}) custom-call(s32[4]{0:T(128)} %pad_add_fusion.order_ref, bf16[256,1920]{1,0:T(8,128)(2,1)} %copy-done, bf16[256,1920]{1,0:T(8,128)(2,1)} %copy-done.1, bf16[1024,1920]{1,0:T(8,128)(2,1)} %all-gather.2.cloned.1.call-done.refs_2_, ...), custom_call_target="tpu_custom_call" | custom-call | flops 4026531840 | bytes 8388608 | tf_op jit(solution)/shard_map/terms/pallas_call | solution.py:107
  81.1 3.1 %collective-permute-start.9 = (bf16[128,1920]{1,0:T(8,128)(2,1)}, bf16[128,1920]{1,0:T(8,128)(2,1)}, u32[]{:S(2)}, u32[]{:S(2)}) collective-permute-start(bf16[128,1920]{1,0:T(8,128)(2,1)} %get-tuple-element.27), channel_id=1, source_target_pairs={{0,1},{1,2},{2,3},{3,0},{4,5},{5,6},{6,7},{7,4},{8,9},{9,10},{10,1... | collective-permute-start | bytes 1474568 | tf_op jit(solution)/shard_map/ppermute | solution.py:145
  84.3 9.9 %terms.6 = (f32[128,1920]{1,0:T(8,128)}, bf16[128,1920]{1,0:T(8,128)(2,1)}, bf16[128,1920]{1,0:T(8,128)(2,1)}, bf16[128,1920]{1,0:T(8,128)(2,1)}) custom-call(s32[4]{0:T(128)} %pad_add_fusion.2.order_ref, bf16[256,1920]{1,0:T(8,128)(2,1)} %collective-permute-done.12.refs_0_, bf16[256,1920]{1,0:T(8,128)(2,1)} %copy-done.3, ...), custom_call_target="tpu_custom_call" | custom-call | flops 4026531840 | bytes 8388608 | tf_op jit(solution)/shard_map/terms/pallas_call | solution.py:107
  94.2 3.2 %collective-permute-start.15 = (bf16[128,1920]{1,0:T(8,128)(2,1)}, bf16[128,1920]{1,0:T(8,128)(2,1)S(1)}, u32[]{:S(2)}, u32[]{:S(2)}) collective-permute-start(bf16[128,1920]{1,0:T(8,128)(2,1)} %get-tuple-element.31), channel_id=1, source_target_pairs={{0,1},{1,2},{2,3},{3,0},{4,5},{5,6},{6,7},{7,4},{8,9},{9,10},{10,1... | collective-permute-start | bytes 1474568 | tf_op jit(solution)/shard_map/ppermute | solution.py:145
  97.4 9.8 %terms.7 = (f32[128,1920]{1,0:T(8,128)}, bf16[128,1920]{1,0:T(8,128)(2,1)}, bf16[128,1920]{1,0:T(8,128)(2,1)}, bf16[128,1920]{1,0:T(8,128)(2,1)}) custom-call(s32[4]{0:T(128)} %pad_add_fusion.3.order_ref, bf16[256,1920]{1,0:T(8,128)(2,1)} %collective-permute-done.18.refs_0_, bf16[256,1920]{1,0:T(8,128)(2,1)} %collective-permute-done.19.refs_1_, ...), custom_call_target="tpu_custom_call" | custom-call | flops 4026531840 | bytes 8388608 | tf_op jit(solution)/shard_map/terms/pallas_call | solution.py:107
  108.3 2.3 %collective-permute-start.4 = (bf16[128,1920]{1,0:T(8,128)(2,1)}, bf16[128,1920]{1,0:T(8,128)(2,1)S(1)}, u32[]{:S(2)}, u32[]{:S(2)}) collective-permute-start(bf16[128,1920]{1,0:T(8,128)(2,1)} %get-tuple-element.23), channel_id=1, source_target_pairs={{0,1},{1,2},{2,3},{3,0},{4,5},{5,6},{6,7},{7,4},{8,9},{9,10},{10,1... | collective-permute-start | bytes 1474568 | tf_op jit(solution)/shard_map/ppermute | solution.py:145
  110.6 1.3 add_convert_fusion.2
  112.2 3.1 %collective-permute-start.21 = (bf16[128,1920]{1,0:T(8,128)(2,1)}, bf16[128,1920]{1,0:T(8,128)(2,1)S(1)}, u32[]{:S(2)}, u32[]{:S(2)}) collective-permute-start(bf16[128,1920]{1,0:T(8,128)(2,1)} %get-tuple-element.35), channel_id=1, source_target_pairs={{0,1},{1,2},{2,3},{3,0},{4,5},{5,6},{6,7},{7,4},{8,9},{9,10},{10,1... | collective-permute-start | bytes 1474568 | tf_op jit(solution)/shard_map/ppermute | solution.py:145
  115.3 2.7 %collective-permute-done.16 = bf16[128,1920]{1,0:T(8,128)(2,1)S(1)} collective-permute-done((bf16[128,1920]{1,0:T(8,128)(2,1)}, bf16[128,1920]{1,0:T(8,128)(2,1)S(1)}, u32[]{:S(2)}, u32[]{:S(2)}) %collective-permute-start.16) | collective-permute-done | bytes 491552 | tf_op jit(solution)/shard_map/ppermute | solution.py:145
  118.2 12.9 %collective-permute-done.20 = bf16[128,1920]{1,0:T(8,128)(2,1)S(1)} collective-permute-done((bf16[128,1920]{1,0:T(8,128)(2,1)}, bf16[128,1920]{1,0:T(8,128)(2,1)S(1)}, u32[]{:S(2)}, u32[]{:S(2)}) %collective-permute-start.20) | collective-permute-done | bytes 491552 | tf_op jit(solution)/shard_map/ppermute | solution.py:145
  132.0 8.4 %collective-permute-done.22 = bf16[128,1920]{1,0:T(8,128)(2,1)S(1)} collective-permute-done((bf16[128,1920]{1,0:T(8,128)(2,1)}, bf16[128,1920]{1,0:T(8,128)(2,1)S(1)}, u32[]{:S(2)}, u32[]{:S(2)}) %collective-permute-start.22) | collective-permute-done | bytes 491552 | tf_op jit(solution)/shard_map/ppermute | solution.py:145
  140.6 2.2 %collective-permute-start.23 = (bf16[128,1920]{1,0:T(8,128)(2,1)S(1)}, bf16[128,1920]{1,0:T(8,128)(2,1)S(1)}, u32[]{:S(2)}, u32[]{:S(2)}) collective-permute-start(bf16[128,1920]{1,0:T(8,128)(2,1)S(1)} %add_convert_fusion), channel_id=1, source_target_pairs={{0,8},{1,9},{2,10},{3,11},{4,12},{5,13},{6,14},{7,15},{8,0},{9,1},... | collective-permute-start | bytes 1474568 | tf_op jit(solution)/shard_map/ppermute | solution.py:148
  142.9 6.6 %collective-permute-done.5 = bf16[128,1920]{1,0:T(8,128)(2,1)S(1)} collective-permute-done((bf16[128,1920]{1,0:T(8,128)(2,1)S(1)}, bf16[128,1920]{1,0:T(8,128)(2,1)S(1)}, u32[]{:S(2)}, u32[]{:S(2)}) %collective-permute-start.5) | collective-permute-done | bytes 491552 | tf_op jit(solution)/shard_map/ppermute | solution.py:145
  149.5 6.2 %collective-permute-done.17 = bf16[128,1920]{1,0:T(8,128)(2,1)S(1)} collective-permute-done((bf16[128,1920]{1,0:T(8,128)(2,1)S(1)}, bf16[128,1920]{1,0:T(8,128)(2,1)S(1)}, u32[]{:S(2)}, u32[]{:S(2)}) %collective-permute-start.17) | collective-permute-done | bytes 491552 | tf_op jit(solution)/shard_map/ppermute | solution.py:148
  155.6 1.3 add_bitcast_fusion
  (61 shorter events, 12.0 us)
Async XLA Ops:
  6.5 53.6 %all-gather.2.cloned.1.call-start = ((), (), s32[]{:S(2)}) async-start(), calls=%async_computation | async-start | bytes 4423680 | tf_op jit(solution)/shard_map/all_gather | solution.py:156
  14.2 15.6 %collective-permute-start.1 = (bf16[128,1920]{1,0:T(8,128)(2,1)}, bf16[128,1920]{1,0:T(8,128)(2,1)S(1)}, u32[]{:S(2)}, u32[]{:S(2)}) collective-permute-start(bf16[128,1920]{1,0:T(8,128)(2,1)} %pick.1), channel_id=1, source_target_pairs={{0,3},{1,0},{2,1},{3,2},{4,7},{5,4},{6,5},{7,6},{8,11},{9,8},{10,9... | collective-permute-start | bytes 1474568 | tf_op jit(solution)/shard_map/ppermute | solution.py:145
  15.1 14.7 %collective-permute-start.2 = (bf16[128,1920]{1,0:T(8,128)(2,1)}, bf16[128,1920]{1,0:T(8,128)(2,1)S(1)}, u32[]{:S(2)}, u32[]{:S(2)}) collective-permute-start(bf16[128,1920]{1,0:T(8,128)(2,1)} %pick.1), channel_id=1, source_target_pairs={{0,2},{1,3},{2,0},{3,1},{4,6},{5,7},{6,4},{7,5},{8,10},{9,11},{10,... | collective-permute-start | bytes 1474568 | tf_op jit(solution)/shard_map/ppermute | solution.py:145
  16.2 16.9 %collective-permute-start = (bf16[128,1920]{1,0:T(8,128)(2,1)}, bf16[128,1920]{1,0:T(8,128)(2,1)S(1)}, u32[]{:S(2)}, u32[]{:S(2)}) collective-permute-start(bf16[128,1920]{1,0:T(8,128)(2,1)} %pick.1), channel_id=1, source_target_pairs={{0,1},{1,2},{2,3},{3,0},{4,5},{5,6},{6,7},{7,4},{8,9},{9,10},{10,1... | collective-permute-start | bytes 1474568 | tf_op jit(solution)/shard_map/ppermute | solution.py:145
  29.9 17.5 %collective-permute-start.13 = (bf16[256,1920]{1,0:T(8,128)(2,1)S(1)}, bf16[256,1920]{1,0:T(8,128)(2,1)S(1)}, u32[]{:S(2)}, u32[]{:S(2)}) collective-permute-start(bf16[256,1920]{1,0:T(8,128)(2,1)S(1)} %constant_dynamic-update-slice_fusion.refs_1_), channel_id=1, source_target_pairs={{0,12},{1,13},{2,14},{3,15},{4,0},{5,1},{6,2},{7,3},{8,4},{9,5},{1... | collective-permute-start | bytes 2949128 | tf_op jit(solution)/shard_map/ppermute | solution.py:148
  34.2 15.5 %collective-permute-start.6 = (bf16[256,1920]{1,0:T(8,128)(2,1)S(1)}, bf16[256,1920]{1,0:T(8,128)(2,1)}, u32[]{:S(2)}, u32[]{:S(2)}) collective-permute-start(bf16[256,1920]{1,0:T(8,128)(2,1)S(1)} %pad_maximum_fusion.refs_0_), channel_id=1, source_target_pairs={{0,4},{1,5},{2,6},{3,7},{4,8},{5,9},{6,10},{7,11},{8,12},{9,13},{1... | collective-permute-start | bytes 2949128 | tf_op jit(solution)/shard_map/ppermute | solution.py:148
  34.2 25.9 %collective-permute-start.7 = (bf16[256,1920]{1,0:T(8,128)(2,1)S(1)}, bf16[256,1920]{1,0:T(8,128)(2,1)}, u32[]{:S(2)}, u32[]{:S(2)}) collective-permute-start(bf16[256,1920]{1,0:T(8,128)(2,1)S(1)} %constant_dynamic-update-slice_fusion.refs_1_), channel_id=1, source_target_pairs={{0,4},{1,5},{2,6},{3,7},{4,8},{5,9},{6,10},{7,11},{8,12},{9,13},{1... | collective-permute-start | bytes 2949128 | tf_op jit(solution)/shard_map/ppermute | solution.py:148
  36.5 44.7 %collective-permute-start.12 = (bf16[256,1920]{1,0:T(8,128)(2,1)S(1)}, bf16[256,1920]{1,0:T(8,128)(2,1)}, u32[]{:S(2)}, u32[]{:S(2)}) collective-permute-start(bf16[256,1920]{1,0:T(8,128)(2,1)S(1)} %pad_maximum_fusion.refs_0_), channel_id=1, source_target_pairs={{0,12},{1,13},{2,14},{3,15},{4,0},{5,1},{6,2},{7,3},{8,4},{9,5},{1... | collective-permute-start | bytes 2949128 | tf_op jit(solution)/shard_map/ppermute | solution.py:148
  47.4 46.7 %collective-permute-start.19 = (bf16[256,1920]{1,0:T(8,128)(2,1)S(1)}, bf16[256,1920]{1,0:T(8,128)(2,1)}, u32[]{:S(2)}, u32[]{:S(2)}) collective-permute-start(bf16[256,1920]{1,0:T(8,128)(2,1)S(1)} %collective-permute-done.13.refs_1_), channel_id=1, source_target_pairs={{0,12},{1,13},{2,14},{3,15},{4,0},{5,1},{6,2},{7,3},{8,4},{9,5},{1... | collective-permute-start | bytes 2949128 | tf_op jit(solution)/shard_map/ppermute | solution.py:148
  49.6 44.5 %collective-permute-start.18 = (bf16[256,1920]{1,0:T(8,128)(2,1)}, bf16[256,1920]{1,0:T(8,128)(2,1)}, u32[]{:S(2)}, u32[]{:S(2)}) collective-permute-start(bf16[256,1920]{1,0:T(8,128)(2,1)} %collective-permute-done.6.refs_0_), channel_id=1, source_target_pairs={{0,4},{1,5},{2,6},{3,7},{4,8},{5,9},{6,10},{7,11},{8,12},{9,13},{1... | collective-permute-start | bytes 2949128 | tf_op jit(solution)/shard_map/ppermute | solution.py:148
  70.0 37.2 %collective-permute-start.10 = (bf16[128,1920]{1,0:T(8,128)(2,1)}, bf16[128,1920]{1,0:T(8,128)(2,1)S(1)}, u32[]{:S(2)}, u32[]{:S(2)}) collective-permute-start(bf16[128,1920]{1,0:T(8,128)(2,1)} %get-tuple-element.28), channel_id=1, source_target_pairs={{0,2},{1,3},{2,0},{3,1},{4,6},{5,7},{6,4},{7,5},{8,10},{9,11},{10,... | collective-permute-start | bytes 1474568 | tf_op jit(solution)/shard_map/ppermute | solution.py:145
  71.1 36.2 %collective-permute-start.8 = (bf16[128,1920]{1,0:T(8,128)(2,1)}, bf16[128,1920]{1,0:T(8,128)(2,1)S(1)}, u32[]{:S(2)}, u32[]{:S(2)}) collective-permute-start(bf16[128,1920]{1,0:T(8,128)(2,1)} %get-tuple-element.26), channel_id=1, source_target_pairs={{0,3},{1,0},{2,1},{3,2},{4,7},{5,4},{6,5},{7,6},{8,11},{9,8},{10,9... | collective-permute-start | bytes 1474568 | tf_op jit(solution)/shard_map/ppermute | solution.py:145
  81.1 27.2 %collective-permute-start.9 = (bf16[128,1920]{1,0:T(8,128)(2,1)}, bf16[128,1920]{1,0:T(8,128)(2,1)}, u32[]{:S(2)}, u32[]{:S(2)}) collective-permute-start(bf16[128,1920]{1,0:T(8,128)(2,1)} %get-tuple-element.27), channel_id=1, source_target_pairs={{0,1},{1,2},{2,3},{3,0},{4,5},{5,6},{6,7},{7,4},{8,9},{9,10},{10,1... | collective-permute-start | bytes 1474568 | tf_op jit(solution)/shard_map/ppermute | solution.py:145
  94.1 17.8 %collective-permute-start.14 = (bf16[128,1920]{1,0:T(8,128)(2,1)}, bf16[128,1920]{1,0:T(8,128)(2,1)S(1)}, u32[]{:S(2)}, u32[]{:S(2)}) collective-permute-start(bf16[128,1920]{1,0:T(8,128)(2,1)} %get-tuple-element.30), channel_id=1, source_target_pairs={{0,3},{1,0},{2,1},{3,2},{4,7},{5,4},{6,5},{7,6},{8,11},{9,8},{10,9... | collective-permute-start | bytes 1474568 | tf_op jit(solution)/shard_map/ppermute | solution.py:145
  94.2 18.1 %collective-permute-start.15 = (bf16[128,1920]{1,0:T(8,128)(2,1)}, bf16[128,1920]{1,0:T(8,128)(2,1)S(1)}, u32[]{:S(2)}, u32[]{:S(2)}) collective-permute-start(bf16[128,1920]{1,0:T(8,128)(2,1)} %get-tuple-element.31), channel_id=1, source_target_pairs={{0,1},{1,2},{2,3},{3,0},{4,5},{5,6},{6,7},{7,4},{8,9},{9,10},{10,1... | collective-permute-start | bytes 1474568 | tf_op jit(solution)/shard_map/ppermute | solution.py:145
  107.3 33.2 %collective-permute-start.3 = (bf16[128,1920]{1,0:T(8,128)(2,1)}, bf16[128,1920]{1,0:T(8,128)(2,1)S(1)}, u32[]{:S(2)}, u32[]{:S(2)}) collective-permute-start(bf16[128,1920]{1,0:T(8,128)(2,1)} %get-tuple-element.22), channel_id=1, source_target_pairs={{0,3},{1,0},{2,1},{3,2},{4,7},{5,4},{6,5},{7,6},{8,11},{9,8},{10,9... | collective-permute-start | bytes 1474568 | tf_op jit(solution)/shard_map/ppermute | solution.py:145
  108.3 34.6 %collective-permute-start.4 = (bf16[128,1920]{1,0:T(8,128)(2,1)}, bf16[128,1920]{1,0:T(8,128)(2,1)S(1)}, u32[]{:S(2)}, u32[]{:S(2)}) collective-permute-start(bf16[128,1920]{1,0:T(8,128)(2,1)} %get-tuple-element.23), channel_id=1, source_target_pairs={{0,1},{1,2},{2,3},{3,0},{4,5},{5,6},{6,7},{7,4},{8,9},{9,10},{10,1... | collective-permute-start | bytes 1474568 | tf_op jit(solution)/shard_map/ppermute | solution.py:145
  112.0 19.2 %collective-permute-start.20 = (bf16[128,1920]{1,0:T(8,128)(2,1)}, bf16[128,1920]{1,0:T(8,128)(2,1)S(1)}, u32[]{:S(2)}, u32[]{:S(2)}) collective-permute-start(bf16[128,1920]{1,0:T(8,128)(2,1)} %get-tuple-element.34), channel_id=1, source_target_pairs={{0,3},{1,0},{2,1},{3,2},{4,7},{5,4},{6,5},{7,6},{8,11},{9,8},{10,9... | collective-permute-start | bytes 1474568 | tf_op jit(solution)/shard_map/ppermute | solution.py:145
  112.2 19.0 %collective-permute-start.21 = (bf16[128,1920]{1,0:T(8,128)(2,1)}, bf16[128,1920]{1,0:T(8,128)(2,1)S(1)}, u32[]{:S(2)}, u32[]{:S(2)}) collective-permute-start(bf16[128,1920]{1,0:T(8,128)(2,1)} %get-tuple-element.35), channel_id=1, source_target_pairs={{0,1},{1,2},{2,3},{3,0},{4,5},{5,6},{6,7},{7,4},{8,9},{9,10},{10,1... | collective-permute-start | bytes 1474568 | tf_op jit(solution)/shard_map/ppermute | solution.py:145
  117.9 22.4 %collective-permute-start.22 = (bf16[128,1920]{1,0:T(8,128)(2,1)}, bf16[128,1920]{1,0:T(8,128)(2,1)S(1)}, u32[]{:S(2)}, u32[]{:S(2)}) collective-permute-start(bf16[128,1920]{1,0:T(8,128)(2,1)} %get-tuple-element.36), channel_id=1, source_target_pairs={{0,2},{1,3},{2,0},{3,1},{4,6},{5,7},{6,4},{7,5},{8,10},{9,11},{10,... | collective-permute-start | bytes 1474568 | tf_op jit(solution)/shard_map/ppermute | solution.py:145
  131.2 18.3 %collective-permute-start.5 = (bf16[128,1920]{1,0:T(8,128)(2,1)S(1)}, bf16[128,1920]{1,0:T(8,128)(2,1)S(1)}, u32[]{:S(2)}, u32[]{:S(2)}) collective-permute-start(bf16[128,1920]{1,0:T(8,128)(2,1)S(1)} %copy-done.7), channel_id=1, source_target_pairs={{0,2},{1,3},{2,0},{3,1},{4,6},{5,7},{6,4},{7,5},{8,10},{9,11},{10,... | collective-permute-start | bytes 1474568 | tf_op jit(solution)/shard_map/ppermute | solution.py:145
  131.2 18.3 %collective-permute-start.11 = (bf16[128,1920]{1,0:T(8,128)(2,1)S(1)}, bf16[128,1920]{1,0:T(8,128)(2,1)S(1)}, u32[]{:S(2)}, u32[]{:S(2)}) collective-permute-start(bf16[128,1920]{1,0:T(8,128)(2,1)S(1)} %add_convert_fusion.2), channel_id=1, source_target_pairs={{0,12},{1,13},{2,14},{3,15},{4,0},{5,1},{6,2},{7,3},{8,4},{9,5},{1... | collective-permute-start | bytes 1474568 | tf_op jit(solution)/shard_map/ppermute | solution.py:148
  140.3 15.3 %collective-permute-start.17 = (bf16[128,1920]{1,0:T(8,128)(2,1)S(1)}, bf16[128,1920]{1,0:T(8,128)(2,1)S(1)}, u32[]{:S(2)}, u32[]{:S(2)}) collective-permute-start(bf16[128,1920]{1,0:T(8,128)(2,1)S(1)} %add_convert_fusion.1), channel_id=1, source_target_pairs={{0,4},{1,5},{2,6},{3,7},{4,8},{5,9},{6,10},{7,11},{8,12},{9,13},{1... | collective-permute-start | bytes 1474568 | tf_op jit(solution)/shard_map/ppermute | solution.py:148
  140.6 15.0 %collective-permute-start.23 = (bf16[128,1920]{1,0:T(8,128)(2,1)S(1)}, bf16[128,1920]{1,0:T(8,128)(2,1)S(1)}, u32[]{:S(2)}, u32[]{:S(2)}) collective-permute-start(bf16[128,1920]{1,0:T(8,128)(2,1)S(1)} %add_convert_fusion), channel_id=1, source_target_pairs={{0,8},{1,9},{2,10},{3,11},{4,12},{5,13},{6,14},{7,15},{8,0},{9,1},... | collective-permute-start | bytes 1474568 | tf_op jit(solution)/shard_map/ppermute | solution.py:148
  (9 other events, 204.0 us)
Sparse Core Ops, SparseCore 0:
  14.4 33.5 all-gather.1

commit v2 on v1

v2 whole, which is shorter than its diff:
```python
import functools

import jax
import jax.numpy as jnp
from jax import lax
from jax.experimental import pallas as pl
from jax.experimental.pallas import tpu as pltpu
from jax.sharding import PartitionSpec as P

SIDE = 4
VMEM = 60 * 1024 * 1024


def pick_body(slab, count_ref, cell_ref, orb_ref, out_ref, acc_ref):
    step = pl.program_id(0)
    part = orb_ref.shape[0]
    slots = out_ref.shape[0]
    local = cell_ref[...] & (slab - 1)
    wanted = jnp.transpose(jnp.broadcast_to(local, (slots, slots)))
    slot = lax.broadcasted_iota(jnp.int32, (slots, slots), 0)
    lane = lax.broadcasted_iota(jnp.int32, (slots, slots), 1)
    wanted = jnp.where(slot < count_ref[0, 0], wanted, -1)
    hits = [
        (wanted == lane + (step * part + k * slots)).astype(jnp.float32).astype(jnp.bfloat16)
        for k in range(part // slots)
    ]
    term = jnp.dot(
        jnp.concatenate(hits, axis=1), orb_ref[...], preferred_element_type=jnp.float32
    )

    @pl.when(step == 0)
    def _():
        acc_ref[...] = term

    @pl.when(step > 0)
    def _():
        acc_ref[...] += term

    @pl.when(step == pl.num_programs(0) - 1)
    def _():
        out_ref[...] = acc_ref[...].astype(out_ref.dtype)


def pick(orbitals, cells, count):
    slab, width = orbitals.shape
    slots = cells.shape[1]
    part = 512
    assert slab & (slab - 1) == 0
    return pl.pallas_call(
        functools.partial(pick_body, slab),
        grid_spec=pltpu.PrefetchScalarGridSpec(
            num_scalar_prefetch=1,
            grid=(slab // part,),
            in_specs=[
                pl.BlockSpec((1, slots), lambda i, n: (0, 0)),
                pl.BlockSpec((part, width), lambda i, n: (i, 0)),
            ],
            out_specs=pl.BlockSpec((slots, width), lambda i, n: (0, 0)),
            scratch_shapes=[pltpu.VMEM((slots, width), jnp.float32)],
        ),
        out_shape=jax.ShapeDtypeStruct((slots, width), orbitals.dtype),
        compiler_params=pltpu.CompilerParams(vmem_limit_bytes=VMEM),
        name="pick",
    )(count, cells, orbitals)


def whole_arrays(body, ins, outs, after=(), behind=(), scalars=(), scratch=(), flops=0, name=None):
    vmem = pl.BlockSpec(memory_space=pltpu.VMEM)
    smem = pl.BlockSpec(memory_space=pltpu.SMEM)
    held = pl.BlockSpec(memory_space=pl.ANY)

    def run(*refs):
        n, m = len(scalars) + len(ins), len(after) + len(behind)
        mark = refs[n + m + len(outs)]
        mark[...] = jnp.zeros_like(mark)
        body(*refs[:n], *refs[n + m : n + m + len(outs)], *refs[n + m + len(outs) + 1 :])

    outs = list(outs)
    marks = [((8, 128), jnp.int32)]

    return pl.pallas_call(
        run,
        in_specs=[smem] * len(scalars) + [vmem] * (len(ins) + len(after)) + [held] * len(behind),
        out_specs=[vmem] * (len(outs) + 1),
        out_shape=[jax.ShapeDtypeStruct(shape, dtype) for shape, dtype in outs + marks],
        scratch_shapes=scratch,
        compiler_params=pltpu.CompilerParams(vmem_limit_bytes=30 * 1024 * 1024),
        cost_estimate=pl.CostEstimate(flops=flops, bytes_accessed=1024, transcendentals=0),
        name=name,
    )(*scalars, *ins, *after, *behind)


def terms(groups, order, panels, tile, outs, after=()):
    width = panels[0].shape[1]
    depth = panels[0].shape[0]
    cols = depth * len(panels)
    slots = tile.shape[1]
    sizes = [g.shape[0] for g in groups]
    blocks = sum(sizes) // slots
    col_part, out_part = 256, 640
    n_groups, n_panels = len(groups), len(panels)
    batch = 512

    def body(order_ref, *refs):
        ins, refs = refs[:n_groups], refs[n_groups:]
        panel_refs, refs = refs[:n_panels], refs[n_panels:]
        tile_ref, refs = refs[0], refs[1:]
        out_refs, (weighted, rows) = refs[: len(outs)], refs[len(outs) :]
        top = 0
        for ref, size in zip(ins, sizes):
            rows[pl.ds(top, size), :] = ref[...]
            top += size
        for k in range(cols // col_part):
            panel_ref = panel_refs[k * col_part // depth]
            for top in range(0, sum(sizes), batch):
                gram = lax.dot_general(
                    rows[pl.ds(top, batch), :],
                    panel_ref[pl.ds(k * col_part % depth, col_part), :],
                    (((1,), (1,)), ((), ())),
                    preferred_element_type=jnp.float32,
                )
                for j in range(batch // slots):
                    span = pl.ds(k * col_part, col_part)
                    part = gram[j * slots : (j + 1) * slots, :]
                    kern = tile_ref[order_ref[top // slots + j], :, span].astype(jnp.float32)
                    weighted[pl.ds(top + j * slots, slots), span] = (part * kern).astype(
                        jnp.bfloat16
                    )
        for k in range(width // out_part):
            span = pl.ds(k * out_part, out_part)
            term = None
            for i, panel_ref in enumerate(panel_refs):
                more = jnp.dot(
                    weighted[:, pl.ds(i * depth, depth)],
                    panel_ref[:, span],
                    preferred_element_type=jnp.float32,
                )
                term = more if term is None else term + more
            for ref, (dtype, parts) in zip(out_refs, outs):
                at = 0
                for block, start, size in parts:
                    top = block * slots + start
                    ref[pl.ds(at, size), span] = term[top : top + size, :].astype(dtype)
                    at += size

    return whole_arrays(
        body,
        (*groups, *panels, tile),
        [((sum(p[2] for p in parts), width), dtype) for dtype, parts in outs],
        after=after,
        scalars=(order,),
        scratch=[pltpu.VMEM((sum(sizes), n), jnp.bfloat16) for n in (cols, width)],
        flops=4 * sum(sizes) * cols * width,
        name="terms",
    )


def stack(*ins, after=()):
    rows, width = sum(a.shape[0] for a in ins), ins[0].shape[1]

    def body(*refs):
        top = 0
        for ref in refs[: len(ins)]:
            refs[len(ins)][pl.ds(top, ref.shape[0]), :] = ref[...]
            top += ref.shape[0]

    return whole_arrays(body, ins, [((rows, width), ins[0].dtype)], after=after, name="stack")


def sums(mine, got, cuts, dtype, after=(), behind=()):
    rows, width = mine.shape
    size = rows // cuts

    def body(*refs):
        ins, outs = refs[: 1 + len(got)], refs[1 + len(got) :]
        for k, out in enumerate(outs):
            span = pl.ds(k * size, size)
            total = ins[0][span, :].astype(jnp.float32)
            for ref in ins[1:]:
                total = total + ref[span, :].astype(jnp.float32)
            out[...] = total.astype(dtype)

    outs = [((size, width), dtype)] * cuts
    return whole_arrays(body, (mine, *got), outs, after=after, behind=behind, name="sums")


def plane_perm(n_row, n_col, first, second):
    pairs = []
    for r in range(n_row):
        dx, dy = (first, second) if r % 2 == 0 else (second, first)
        for c in range(n_col):
            y, x = c // SIDE, c % SIDE
            to = ((y + dy) % SIDE) * SIDE + (x + dx) % SIDE
            pairs.append((r * n_col + c, r * n_col + to))
    return pairs


def solution(mesh):
    n_row, n_col = mesh.shape["row"], mesh.shape["col"]
    bf, f32 = jnp.bfloat16, jnp.float32

    def first(a, by):
        return lax.ppermute(a, ("row", "col"), plane_perm(n_row, n_col, by, 0))

    def second(a, by):
        return lax.ppermute(a, ("row", "col"), plane_perm(n_row, n_col, 0, by))

    def on_device(orbitals, point_cell, point_count, kernel):
        slab, width = orbitals.shape
        slots = point_cell.shape[2]
        own = pick(orbitals, point_cell.reshape(1, slots), point_count)
        tile = kernel.reshape(n_col, slots, -1)

        offsets = (0, -1, 1, 2)
        low, high, far = first(own, 1), first(own, -1), first(own, 2)
        near, mark = stack(own, low)
        near_low, near_high = second(near, 1), second(near, -1)
        wide, _ = stack(high, far, after=(mark,))
        wide_low, wide_high = second(wide, 1), second(wide, -1)
        panels = (lax.all_gather(own, "row", axis=0, tiled=True),)

        row, col = lax.axis_index("row"), lax.axis_index("col")
        core, y, x = row % 2, col // SIDE, col % SIDE

        def terms_of(groups, bs, after=()):
            blocks = []
            for b in bs:
                for a in offsets:
                    dx, dy = jnp.where(core == 0, a, b), jnp.where(core == 0, b, a)
                    blocks.append(((y + dy) % SIDE) * SIDE + (x + dx) % SIDE)
            order = jnp.stack(blocks).astype(jnp.int32)
            outs = [
                (f32 if k == 0 else bf, [(4 * i + k, 0, slots) for i in range(len(bs))])
                for k in range(4)
            ]
            return terms(groups, order, panels, tile, outs, after=after)

        def over_first(t):
            return first(t[1], -1), first(t[2], 1), first(t[3], 2)

        def total(mine, got):
            return mine + sum(a.astype(f32) for a in got)

        *t_here, mark = terms_of((near, wide), (0,))
        got_here = over_first(t_here)
        near_far, wide_far = second(near_low, 1), second(wide_high, -1)
        *t_near, mark = terms_of((near_low, wide_low, near_high, wide_high), (-1, 1), after=(mark,))
        here, mark = sums(t_here[0], got_here, 1, f32, after=(mark,))
        got_near = over_first(t_near)
        *t_far, mark = terms_of((near_far, wide_far), (2,), after=(mark,))
        got_far = over_first(t_far)
        to_low, to_high, mark = sums(t_near[0], got_near, 2, bf, after=(mark,))
        got = second(to_low, -1), second(to_high, 1)
        to_far, _ = sums(t_far[0], got_far, 1, bf, after=(mark,), behind=got)
        result = total(here, (*got, second(to_far, 2)))
        return result.reshape(1, 1, slots, width)

    in_specs = (
        P(("row", "col"), None),
        P("row", "col", None),
        P("row", "col"),
        P("row", None, None, None, "col", None),
    )
    out_specs = P("row", "col", None, None)
    return jax.shard_map(
        on_device, mesh=mesh, in_specs=in_specs, out_specs=out_specs, check_vma=False
    )
```

time: 164 us -> 144 us (0.88)
  the two profiles are of different devices: /device:TPU:6 before, /device:TPU:96 now
where the time goes in v2:
time: 144 us; the launch traced here: 143 us
  waiting for transfers between devices  39.2 us (27%)
  Pallas kernels  35.7 us (25%)
  starting transfers between devices  29.8 us (21%)
  local copies, waits for them, and re-layouts  22.8 us (16%)
  between operations  14.2 us (10%)
    pallas_call x8, Pallas kernels, whole_arrays(): pl.pallas_call(run, in_specs=[smem] * len(scalars) + [vmem] * (len(ins) +...  29.8 us
    ppermute x12, waiting for transfers between devices, first(): return lax.ppermute(a, ('row', 'col'), plane_perm(n_row, n_col, by, 0))  27.6 us
    unnamed x24, local copies, waits for them, and re-layouts  15.4 us
    ppermute x9, starting transfers between devices, second(): return lax.ppermute(a, ('row', 'col'), plane_perm(n_row, n_col, 0, by))  15 us
    ppermute x12, starting transfers between devices, first(): return lax.ppermute(a, ('row', 'col'), plane_perm(n_row, n_col, by, 0))  14.8 us
    ppermute x9, waiting for transfers between devices, second(): return lax.ppermute(a, ('row', 'col'), plane_perm(n_row, n_col, 0, by))  11.6 us
    reshape x1, local copies, waits for them, and re-layouts, on_device(): tile = kernel.reshape(n_col, slots, -1)  7.29 us
    pallas_call x1, Pallas kernels, pick(): pl.pallas_call(functools.partial(pick_body, slab), grid_spec=pltpu.Prefet...  5.91 us
  transfers between devices with their start and end apart: 22, of which 10 were waited for; matrix products, arithmetic and copies ran while one was open for 5% of the time, Pallas kernels for 20%

profile of v2, /device:TPU:96, one launch (start us, length us, event | category | flops | bytes accessed | tf_op | source)
XLA Modules:
  0.0 142.9 jit_solution(12179961183039801765)
XLA Ops:
  7.2 5.9 %pick.1.refs_0_ = bf16[128,1920]{1,0:T(8,128)(2,1)} custom-call(s32[1,1]{1,0:T(1,128)S(6)} %copy.5.count_ref, s32[1,128]{1,0:T(1,128)} %bitcast.23, bf16[2048,1920]{1,0:T(8,128)(2,1)} %orb_ref.1), custom_call_target="tpu_custom_call" | custom-call | tf_op jit(solution)/shard_map/pick/pallas_call | solution.py:49
  18.2 5.2 %collective-permute-done.refs_1_ = bf16[128,1920]{1,0:T(8,128)(2,1)S(1)} collective-permute-done((bf16[128,1920]{1,0:T(8,128)(2,1)}, bf16[128,1920]{1,0:T(8,128)(2,1)S(1)}, u32[]{:S(2)}, u32[]{:S(2)}) %collective-permute-start) | collective-permute-done | bytes 491552 | tf_op jit(solution)/shard_map/ppermute | solution.py:203
  26.2 2.2 %collective-permute-done.1.refs_0_ = bf16[128,1920]{1,0:T(8,128)(2,1)S(1)} collective-permute-done((bf16[128,1920]{1,0:T(8,128)(2,1)}, bf16[128,1920]{1,0:T(8,128)(2,1)S(1)}, u32[]{:S(2)}, u32[]{:S(2)}) %collective-permute-start.1) | collective-permute-done | bytes 491552 | tf_op jit(solution)/shard_map/ppermute | solution.py:203
  28.4 2.4 %collective-permute-done.2.refs_1_ = bf16[128,1920]{1,0:T(8,128)(2,1)S(1)} collective-permute-done((bf16[128,1920]{1,0:T(8,128)(2,1)}, bf16[128,1920]{1,0:T(8,128)(2,1)S(1)}, u32[]{:S(2)}, u32[]{:S(2)}) %collective-permute-start.2) | collective-permute-done | bytes 491552 | tf_op jit(solution)/shard_map/ppermute | solution.py:203
  31.9 4.3 %collective-permute-start.9 = (bf16[256,1920]{1,0:T(8,128)(2,1)}, bf16[256,1920]{1,0:T(8,128)(2,1)}, u32[]{:S(2)}, u32[]{:S(2)}) collective-permute-start(bf16[256,1920]{1,0:T(8,128)(2,1)} %get-tuple-element.31.refs_2_), channel_id=1, source_target_pairs={{0,12},{1,13},{2,14},{3,15},{4,0},{5,1},{6,2},{7,3},{8,4},{9,5},{1... | collective-permute-start | bytes 2949128 | tf_op jit(solution)/shard_map/ppermute | solution.py:206
  36.2 3.2 %collective-permute-start.8 = (bf16[256,1920]{1,0:T(8,128)(2,1)S(1)}, bf16[256,1920]{1,0:T(8,128)(2,1)}, u32[]{:S(2)}, u32[]{:S(2)}) collective-permute-start(bf16[256,1920]{1,0:T(8,128)(2,1)S(1)} %get-tuple-element.29.refs_1_), channel_id=1, source_target_pairs={{0,12},{1,13},{2,14},{3,15},{4,0},{5,1},{6,2},{7,3},{8,4},{9,5},{1... | collective-permute-start | bytes 2949128 | tf_op jit(solution)/shard_map/ppermute | solution.py:206
  39.4 7.3 %reshape.10.refs_4_.refs_6_ = bf16[16,128,1024]{2,1,0:T(8,128)(2,1)} reshape(bf16[1,16,128,8,1,128]{5,3,4,2,1,0:T(8,128)(2,1)} %param.7) | data formatting | bytes 8388608 | tf_op jit(solution)/shard_map/reshape | solution.py:212
  48.1 3.7 %collective-permute-start.14 = (bf16[256,1920]{1,0:T(8,128)(2,1)}, bf16[256,1920]{1,0:T(8,128)(2,1)}, u32[]{:S(2)}, u32[]{:S(2)}) collective-permute-start(bf16[256,1920]{1,0:T(8,128)(2,1)} %collective-permute-done.9.refs_4_), channel_id=1, source_target_pairs={{0,12},{1,13},{2,14},{3,15},{4,0},{5,1},{6,2},{7,3},{8,4},{9,5},{1... | collective-permute-start | bytes 2949128 | tf_op jit(solution)/shard_map/ppermute | solution.py:206
  51.8 2.2 %copy-done.1 = bf16[16,128,1024]{2,1,0:T(8,128)(2,1)S(1)} copy-done((bf16[16,128,1024]{2,1,0:T(8,128)(2,1)S(1)}, bf16[16,128,1024]{2,1,0:T(8,128)(2,1)}, u32[]{:S(2)}) %copy-start.1) | copy-done | bytes 4194328
  54.0 2.1 %copy-done.10 = bf16[1024,1920]{1,0:T(8,128)(2,1)S(1)} copy-done((bf16[1024,1920]{1,0:T(8,128)(2,1)S(1)}, bf16[1024,1920]{1,0:T(8,128)(2,1)}, u32[]{:S(2)}) %copy-start.10) | copy-done | bytes 3932184
  56.1 6.3 %terms.3 = (f32[128,1920]{1,0:T(8,128)S(1)}, bf16[128,1920]{1,0:T(8,128)(2,1)S(1)}, bf16[128,1920]{1,0:T(8,128)(2,1)S(1)}, bf16[128,1920]{1,0:T(8,128)(2,1)S(1)}, s32[8,128]{1,0:T(8,128)S(1)}) custom-call(s32[4]{0:T(128)S(1)} %pad_add_fusion.refs_0_, bf16[256,1920]{1,0:T(8,128)(2,1)S(1)} %get-tuple-element.29.refs_1_, ...), custom_call_target="tpu_custom_call" | custom-call | flops 4026531840 | bytes 1024 | tf_op jit(solution)/shard_map/terms/pallas_call | solution.py:81
  63.4 2.0 %collective-permute-start.4 = (bf16[128,1920]{1,0:T(8,128)(2,1)S(1)}, bf16[128,1920]{1,0:T(8,128)(2,1)S(1)}, u32[]{:S(2)}, u32[]{:S(2)}) collective-permute-start(bf16[128,1920]{1,0:T(8,128)(2,1)S(1)} %get-tuple-element.34), channel_id=1, source_target_pairs={{0,1},{1,2},{2,3},{3,0},{4,5},{5,6},{6,7},{7,4},{8,9},{9,10},{10,1... | collective-permute-start | bytes 1474568 | tf_op jit(solution)/shard_map/ppermute | solution.py:203
  66.2 13.1 %terms.4 = (f32[256,1920]{1,0:T(8,128)S(1)}, bf16[256,1920]{1,0:T(8,128)(2,1)}, bf16[256,1920]{1,0:T(8,128)(2,1)}, bf16[256,1920]{1,0:T(8,128)(2,1)}, s32[8,128]{1,0:T(8,128)S(1)}) custom-call(s32[8]{0:T(128)S(1)} %stack.72.refs_0_, bf16[256,1920]{1,0:T(8,128)(2,1)} %collective-permute-done.6.refs_1_, bf16[256,1920]{1,0:T(8,128)(2,1)} %collective-permute-done.7.refs_2_, ...), custom_call_target="tpu_custom_call" | custom-call | flops 8053063680 | bytes 1024 | tf_op jit(solution)/shard_map/terms/pallas_call | solution.py:81
  79.3 2.1 %collective-permute-start.10 = (bf16[256,1920]{1,0:T(8,128)(2,1)}, bf16[256,1920]{1,0:T(8,128)(2,1)S(1)}, u32[]{:S(2)}, u32[]{:S(2)}) collective-permute-start(bf16[256,1920]{1,0:T(8,128)(2,1)} %get-tuple-element.40), channel_id=1, source_target_pairs={{0,3},{1,0},{2,1},{3,2},{4,7},{5,4},{6,5},{7,6},{8,11},{9,8},{10,9... | collective-permute-start | bytes 2949128 | tf_op jit(solution)/shard_map/ppermute | solution.py:203
  83.0 2.6 %collective-permute-start.12 = (bf16[256,1920]{1,0:T(8,128)(2,1)}, bf16[256,1920]{1,0:T(8,128)(2,1)}, u32[]{:S(2)}, u32[]{:S(2)}) collective-permute-start(bf16[256,1920]{1,0:T(8,128)(2,1)} %get-tuple-element.42), channel_id=1, source_target_pairs={{0,2},{1,3},{2,0},{3,1},{4,6},{5,7},{6,4},{7,5},{8,10},{9,11},{10,... | collective-permute-start | bytes 2949128 | tf_op jit(solution)/shard_map/ppermute | solution.py:203
  89.2 2.2 %copy-done.3 = bf16[16,128,1024]{2,1,0:T(8,128)(2,1)S(1)} copy-done((bf16[16,128,1024]{2,1,0:T(8,128)(2,1)S(1)}, bf16[16,128,1024]{2,1,0:T(8,128)(2,1)}, u32[]{:S(2)}) %copy-start.3) | copy-done | bytes 4194328
  91.4 2.1 %copy-done.11 = bf16[1024,1920]{1,0:T(8,128)(2,1)S(1)} copy-done((bf16[1024,1920]{1,0:T(8,128)(2,1)S(1)}, bf16[1024,1920]{1,0:T(8,128)(2,1)}, u32[]{:S(2)}) %copy-start.11) | copy-done | bytes 3932184
  93.5 6.5 %terms.5 = (f32[128,1920]{1,0:T(8,128)S(1)}, bf16[128,1920]{1,0:T(8,128)(2,1)S(1)}, bf16[128,1920]{1,0:T(8,128)(2,1)S(1)}, bf16[128,1920]{1,0:T(8,128)(2,1)S(1)}, s32[8,128]{1,0:T(8,128)S(1)}) custom-call(s32[4]{0:T(128)S(1)} %pad_add_fusion.1.refs_0_, bf16[256,1920]{1,0:T(8,128)(2,1)} %collective-permute-done.13.refs_1_, ...), custom_call_target="tpu_custom_call" | custom-call | flops 4026531840 | bytes 1024 | tf_op jit(solution)/shard_map/terms/pallas_call | solution.py:81
  103.9 4.4 %collective-permute-done.11.refs_2_ = bf16[256,1920]{1,0:T(8,128)(2,1)} collective-permute-done((bf16[256,1920]{1,0:T(8,128)(2,1)}, bf16[256,1920]{1,0:T(8,128)(2,1)}, u32[]{:S(2)}, u32[]{:S(2)}) %collective-permute-start.11) | collective-permute-done | bytes 983072 | tf_op jit(solution)/shard_map/ppermute | solution.py:203
  108.4 1.9 %sums.4 = (bf16[128,1920]{1,0:T(8,128)(2,1)S(1)}, bf16[128,1920]{1,0:T(8,128)(2,1)S(1)}, s32[8,128]{1,0:T(8,128)S(1)}) custom-call(f32[256,1920]{1,0:T(8,128)S(1)} %get-tuple-element.39.refs_0_, bf16[256,1920]{1,0:T(8,128)(2,1)S(1)} %collective-permute-done.10.refs_1_, bf16[256,1920]{1,0:T(8,128)(2,1)} %collective-permute-done.11.refs_2_, ...), custom_call_target="tpu_custom_call" | custom-call | bytes 1024 | tf_op jit(solution)/shard_map/sums/pallas_call | solution.py:81
  110.4 2.0 %collective-permute-start.16 = (bf16[128,1920]{1,0:T(8,128)(2,1)S(1)}, bf16[128,1920]{1,0:T(8,128)(2,1)S(1)}, u32[]{:S(2)}, u32[]{:S(2)}) collective-permute-start(bf16[128,1920]{1,0:T(8,128)(2,1)S(1)} %get-tuple-element.46), channel_id=1, source_target_pairs={{0,4},{1,5},{2,6},{3,7},{4,8},{5,9},{6,10},{7,11},{8,12},{9,13},{1... | collective-permute-start | bytes 1474568 | tf_op jit(solution)/shard_map/ppermute | solution.py:206
  112.4 2.7 %collective-permute-done.17.refs_1_ = bf16[128,1920]{1,0:T(8,128)(2,1)S(1)} collective-permute-done((bf16[128,1920]{1,0:T(8,128)(2,1)S(1)}, bf16[128,1920]{1,0:T(8,128)(2,1)S(1)}, u32[]{:S(2)}, u32[]{:S(2)}) %collective-permute-start.17) | collective-permute-done | bytes 491552 | tf_op jit(solution)/shard_map/ppermute | solution.py:203
  115.1 8.8 %collective-permute-done.18.refs_2_ = bf16[128,1920]{1,0:T(8,128)(2,1)S(1)} collective-permute-done((bf16[128,1920]{1,0:T(8,128)(2,1)S(1)}, bf16[128,1920]{1,0:T(8,128)(2,1)S(1)}, u32[]{:S(2)}, u32[]{:S(2)}) %collective-permute-start.18) | collective-permute-done | bytes 491552 | tf_op jit(solution)/shard_map/ppermute | solution.py:203
  124.6 10.3 %collective-permute-done.20 = bf16[128,1920]{1,0:T(8,128)(2,1)S(1)} collective-permute-done((bf16[128,1920]{1,0:T(8,128)(2,1)S(1)}, bf16[128,1920]{1,0:T(8,128)(2,1)S(1)}, u32[]{:S(2)}, u32[]{:S(2)}) %collective-permute-start.20) | collective-permute-done | bytes 491552 | tf_op jit(solution)/shard_map/ppermute | solution.py:206
  (59 shorter events, 23.1 us)
Async XLA Ops:
  6.5 45.3 %all-gather.2.cloned.1.call-start = ((), (), s32[]{:S(2)}) async-start(), calls=%async_computation | async-start | bytes 4423680 | tf_op jit(solution)/shard_map/all_gather | solution.py:220
  13.1 10.3 %collective-permute-start = (bf16[128,1920]{1,0:T(8,128)(2,1)}, bf16[128,1920]{1,0:T(8,128)(2,1)S(1)}, u32[]{:S(2)}, u32[]{:S(2)}) collective-permute-start(bf16[128,1920]{1,0:T(8,128)(2,1)} %pick.1.refs_0_), channel_id=1, source_target_pairs={{0,1},{1,2},{2,3},{3,0},{4,5},{5,6},{6,7},{7,4},{8,9},{9,10},{10,1... | collective-permute-start | bytes 1474568 | tf_op jit(solution)/shard_map/ppermute | solution.py:203
  14.7 13.7 %collective-permute-start.1 = (bf16[128,1920]{1,0:T(8,128)(2,1)}, bf16[128,1920]{1,0:T(8,128)(2,1)S(1)}, u32[]{:S(2)}, u32[]{:S(2)}) collective-permute-start(bf16[128,1920]{1,0:T(8,128)(2,1)} %pick.1.refs_0_), channel_id=1, source_target_pairs={{0,3},{1,0},{2,1},{3,2},{4,7},{5,4},{6,5},{7,6},{8,11},{9,8},{10,9... | collective-permute-start | bytes 1474568 | tf_op jit(solution)/shard_map/ppermute | solution.py:203
  16.4 14.4 %collective-permute-start.2 = (bf16[128,1920]{1,0:T(8,128)(2,1)}, bf16[128,1920]{1,0:T(8,128)(2,1)S(1)}, u32[]{:S(2)}, u32[]{:S(2)}) collective-permute-start(bf16[128,1920]{1,0:T(8,128)(2,1)} %pick.1.refs_0_), channel_id=1, source_target_pairs={{0,2},{1,3},{2,0},{3,1},{4,6},{5,7},{6,4},{7,5},{8,10},{9,11},{10,... | collective-permute-start | bytes 1474568 | tf_op jit(solution)/shard_map/ppermute | solution.py:203
  24.6 22.3 %collective-permute-start.6 = (bf16[256,1920]{1,0:T(8,128)(2,1)S(1)}, bf16[256,1920]{1,0:T(8,128)(2,1)}, u32[]{:S(2)}, u32[]{:S(2)}) collective-permute-start(bf16[256,1920]{1,0:T(8,128)(2,1)S(1)} %get-tuple-element.29.refs_1_), channel_id=1, source_target_pairs={{0,4},{1,5},{2,6},{3,7},{4,8},{5,9},{6,10},{7,11},{8,12},{9,13},{1... | collective-permute-start | bytes 2949128 | tf_op jit(solution)/shard_map/ppermute | solution.py:206
  31.9 16.3 %collective-permute-start.9 = (bf16[256,1920]{1,0:T(8,128)(2,1)}, bf16[256,1920]{1,0:T(8,128)(2,1)}, u32[]{:S(2)}, u32[]{:S(2)}) collective-permute-start(bf16[256,1920]{1,0:T(8,128)(2,1)} %get-tuple-element.31.refs_2_), channel_id=1, source_target_pairs={{0,12},{1,13},{2,14},{3,15},{4,0},{5,1},{6,2},{7,3},{8,4},{9,5},{1... | collective-permute-start | bytes 2949128 | tf_op jit(solution)/shard_map/ppermute | solution.py:206
  36.2 27.2 %collective-permute-start.7 = (bf16[256,1920]{1,0:T(8,128)(2,1)}, bf16[256,1920]{1,0:T(8,128)(2,1)}, u32[]{:S(2)}, u32[]{:S(2)}) collective-permute-start(bf16[256,1920]{1,0:T(8,128)(2,1)} %get-tuple-element.31.refs_2_), channel_id=1, source_target_pairs={{0,4},{1,5},{2,6},{3,7},{4,8},{5,9},{6,10},{7,11},{8,12},{9,13},{1... | collective-permute-start | bytes 2949128 | tf_op jit(solution)/shard_map/ppermute | solution.py:206
  36.2 29.2 %collective-permute-start.8 = (bf16[256,1920]{1,0:T(8,128)(2,1)S(1)}, bf16[256,1920]{1,0:T(8,128)(2,1)}, u32[]{:S(2)}, u32[]{:S(2)}) collective-permute-start(bf16[256,1920]{1,0:T(8,128)(2,1)S(1)} %get-tuple-element.29.refs_1_), channel_id=1, source_target_pairs={{0,12},{1,13},{2,14},{3,15},{4,0},{5,1},{6,2},{7,3},{8,4},{9,5},{1... | collective-permute-start | bytes 2949128 | tf_op jit(solution)/shard_map/ppermute | solution.py:206
  46.9 42.3 %collective-permute-start.13 = (bf16[256,1920]{1,0:T(8,128)(2,1)}, bf16[256,1920]{1,0:T(8,128)(2,1)}, u32[]{:S(2)}, u32[]{:S(2)}) collective-permute-start(bf16[256,1920]{1,0:T(8,128)(2,1)} %collective-permute-done.6.refs_1_), channel_id=1, source_target_pairs={{0,4},{1,5},{2,6},{3,7},{4,8},{5,9},{6,10},{7,11},{8,12},{9,13},{1... | collective-permute-start | bytes 2949128 | tf_op jit(solution)/shard_map/ppermute | solution.py:206
  48.1 41.1 %collective-permute-start.14 = (bf16[256,1920]{1,0:T(8,128)(2,1)}, bf16[256,1920]{1,0:T(8,128)(2,1)}, u32[]{:S(2)}, u32[]{:S(2)}) collective-permute-start(bf16[256,1920]{1,0:T(8,128)(2,1)} %collective-permute-done.9.refs_4_), channel_id=1, source_target_pairs={{0,12},{1,13},{2,14},{3,15},{4,0},{5,1},{6,2},{7,3},{8,4},{9,5},{1... | collective-permute-start | bytes 2949128 | tf_op jit(solution)/shard_map/ppermute | solution.py:206
  56.1 10.1 %copy-start.2 = (bf16[16,128,1024]{2,1,0:T(8,128)(2,1)S(1)}, bf16[16,128,1024]{2,1,0:T(8,128)(2,1)}, u32[]{:S(2)}) copy-start(bf16[16,128,1024]{2,1,0:T(8,128)(2,1)} %reshape.10.refs_4_.refs_6_) | copy-start | bytes 12582916
  63.4 15.9 %collective-permute-start.3 = (bf16[128,1920]{1,0:T(8,128)(2,1)S(1)}, bf16[128,1920]{1,0:T(8,128)(2,1)S(1)}, u32[]{:S(2)}, u32[]{:S(2)}) collective-permute-start(bf16[128,1920]{1,0:T(8,128)(2,1)S(1)} %get-tuple-element.33), channel_id=1, source_target_pairs={{0,3},{1,0},{2,1},{3,2},{4,7},{5,4},{6,5},{7,6},{8,11},{9,8},{10,9... | collective-permute-start | bytes 1474568 | tf_op jit(solution)/shard_map/ppermute | solution.py:203
  63.4 18.0 %collective-permute-start.4 = (bf16[128,1920]{1,0:T(8,128)(2,1)S(1)}, bf16[128,1920]{1,0:T(8,128)(2,1)S(1)}, u32[]{:S(2)}, u32[]{:S(2)}) collective-permute-start(bf16[128,1920]{1,0:T(8,128)(2,1)S(1)} %get-tuple-element.34), channel_id=1, source_target_pairs={{0,1},{1,2},{2,3},{3,0},{4,5},{5,6},{6,7},{7,4},{8,9},{9,10},{10,1... | collective-permute-start | bytes 1474568 | tf_op jit(solution)/shard_map/ppermute | solution.py:203
  65.4 16.8 %collective-permute-start.5 = (bf16[128,1920]{1,0:T(8,128)(2,1)S(1)}, bf16[128,1920]{1,0:T(8,128)(2,1)S(1)}, u32[]{:S(2)}, u32[]{:S(2)}) collective-permute-start(bf16[128,1920]{1,0:T(8,128)(2,1)S(1)} %get-tuple-element.35), channel_id=1, source_target_pairs={{0,2},{1,3},{2,0},{3,1},{4,6},{5,7},{6,4},{7,5},{8,10},{9,11},{10,... | collective-permute-start | bytes 1474568 | tf_op jit(solution)/shard_map/ppermute | solution.py:203
  79.3 24.6 %collective-permute-start.10 = (bf16[256,1920]{1,0:T(8,128)(2,1)}, bf16[256,1920]{1,0:T(8,128)(2,1)S(1)}, u32[]{:S(2)}, u32[]{:S(2)}) collective-permute-start(bf16[256,1920]{1,0:T(8,128)(2,1)} %get-tuple-element.40), channel_id=1, source_target_pairs={{0,3},{1,0},{2,1},{3,2},{4,7},{5,4},{6,5},{7,6},{8,11},{9,8},{10,9... | collective-permute-start | bytes 2949128 | tf_op jit(solution)/shard_map/ppermute | solution.py:203
  82.2 26.1 %collective-permute-start.11 = (bf16[256,1920]{1,0:T(8,128)(2,1)}, bf16[256,1920]{1,0:T(8,128)(2,1)}, u32[]{:S(2)}, u32[]{:S(2)}) collective-permute-start(bf16[256,1920]{1,0:T(8,128)(2,1)} %get-tuple-element.41), channel_id=1, source_target_pairs={{0,1},{1,2},{2,3},{3,0},{4,5},{5,6},{6,7},{7,4},{8,9},{9,10},{10,1... | collective-permute-start | bytes 2949128 | tf_op jit(solution)/shard_map/ppermute | solution.py:203
  83.0 25.4 %collective-permute-start.12 = (bf16[256,1920]{1,0:T(8,128)(2,1)}, bf16[256,1920]{1,0:T(8,128)(2,1)}, u32[]{:S(2)}, u32[]{:S(2)}) collective-permute-start(bf16[256,1920]{1,0:T(8,128)(2,1)} %get-tuple-element.42), channel_id=1, source_target_pairs={{0,2},{1,3},{2,0},{3,1},{4,6},{5,7},{6,4},{7,5},{8,10},{9,11},{10,... | collective-permute-start | bytes 2949128 | tf_op jit(solution)/shard_map/ppermute | solution.py:203
  89.2 2.2 %copy-start.3 = (bf16[16,128,1024]{2,1,0:T(8,128)(2,1)S(1)}, bf16[16,128,1024]{2,1,0:T(8,128)(2,1)}, u32[]{:S(2)}) copy-start(bf16[16,128,1024]{2,1,0:T(8,128)(2,1)} %reshape.10.refs_4_.refs_6_) | copy-start | bytes 12582916
  100.0 15.1 %collective-permute-start.17 = (bf16[128,1920]{1,0:T(8,128)(2,1)S(1)}, bf16[128,1920]{1,0:T(8,128)(2,1)S(1)}, u32[]{:S(2)}, u32[]{:S(2)}) collective-permute-start(bf16[128,1920]{1,0:T(8,128)(2,1)S(1)} %get-tuple-element.48), channel_id=1, source_target_pairs={{0,3},{1,0},{2,1},{3,2},{4,7},{5,4},{6,5},{7,6},{8,11},{9,8},{10,9... | collective-permute-start | bytes 1474568 | tf_op jit(solution)/shard_map/ppermute | solution.py:203
  101.3 22.6 %collective-permute-start.18 = (bf16[128,1920]{1,0:T(8,128)(2,1)S(1)}, bf16[128,1920]{1,0:T(8,128)(2,1)S(1)}, u32[]{:S(2)}, u32[]{:S(2)}) collective-permute-start(bf16[128,1920]{1,0:T(8,128)(2,1)S(1)} %get-tuple-element.49), channel_id=1, source_target_pairs={{0,1},{1,2},{2,3},{3,0},{4,5},{5,6},{6,7},{7,4},{8,9},{9,10},{10,1... | collective-permute-start | bytes 1474568 | tf_op jit(solution)/shard_map/ppermute | solution.py:203
  103.9 20.0 %collective-permute-start.19 = (bf16[128,1920]{1,0:T(8,128)(2,1)S(1)}, bf16[128,1920]{1,0:T(8,128)(2,1)S(1)}, u32[]{:S(2)}, u32[]{:S(2)}) collective-permute-start(bf16[128,1920]{1,0:T(8,128)(2,1)S(1)} %get-tuple-element.50), channel_id=1, source_target_pairs={{0,2},{1,3},{2,0},{3,1},{4,6},{5,7},{6,4},{7,5},{8,10},{9,11},{10,... | collective-permute-start | bytes 1474568 | tf_op jit(solution)/shard_map/ppermute | solution.py:203
  110.3 13.6 %collective-permute-start.15 = (bf16[128,1920]{1,0:T(8,128)(2,1)S(1)}, bf16[128,1920]{1,0:T(8,128)(2,1)S(1)}, u32[]{:S(2)}, u32[]{:S(2)}) collective-permute-start(bf16[128,1920]{1,0:T(8,128)(2,1)S(1)} %get-tuple-element.45), channel_id=1, source_target_pairs={{0,12},{1,13},{2,14},{3,15},{4,0},{5,1},{6,2},{7,3},{8,4},{9,5},{1... | collective-permute-start | bytes 1474568 | tf_op jit(solution)/shard_map/ppermute | solution.py:206
  110.4 13.5 %collective-permute-start.16 = (bf16[128,1920]{1,0:T(8,128)(2,1)S(1)}, bf16[128,1920]{1,0:T(8,128)(2,1)S(1)}, u32[]{:S(2)}, u32[]{:S(2)}) collective-permute-start(bf16[128,1920]{1,0:T(8,128)(2,1)S(1)} %get-tuple-element.46), channel_id=1, source_target_pairs={{0,4},{1,5},{2,6},{3,7},{4,8},{5,9},{6,10},{7,11},{8,12},{9,13},{1... | collective-permute-start | bytes 1474568 | tf_op jit(solution)/shard_map/ppermute | solution.py:206
  124.6 10.3 %collective-permute-start.20 = (bf16[128,1920]{1,0:T(8,128)(2,1)S(1)}, bf16[128,1920]{1,0:T(8,128)(2,1)S(1)}, u32[]{:S(2)}, u32[]{:S(2)}) collective-permute-start(bf16[128,1920]{1,0:T(8,128)(2,1)S(1)} %get-tuple-element.52), channel_id=1, source_target_pairs={{0,8},{1,9},{2,10},{3,11},{4,12},{5,13},{6,14},{7,15},{8,0},{9,1},... | collective-permute-start | bytes 1474568 | tf_op jit(solution)/shard_map/ppermute | solution.py:206
  (10 other events, 13.3 us)
Sparse Core Ops, SparseCore 0:
  13.2 30.3 all-gather.1

commit v3 on v2

--- a/solution.py
+++ b/solution.py
@@ -11,7 +11,7 @@
 VMEM = 60 * 1024 * 1024
 
 
-def pick_body(slab, count_ref, cell_ref, orb_ref, out_ref, acc_ref):
+def pick_body(slab, count_ref, order_ref, cell_ref, orb_ref, out_ref, acc_ref):
     step = pl.program_id(0)
     part = orb_ref.shape[0]
     slots = out_ref.shape[0]
@@ -41,7 +41,7 @@
         out_ref[...] = acc_ref[...].astype(out_ref.dtype)
 
 
-def pick(orbitals, cells, count):
+def pick(orbitals, cells, count, order):
     slab, width = orbitals.shape
     slots = cells.shape[1]
     part = 512
@@ -49,19 +49,19 @@
     return pl.pallas_call(
         functools.partial(pick_body, slab),
         grid_spec=pltpu.PrefetchScalarGridSpec(
-            num_scalar_prefetch=1,
+            num_scalar_prefetch=2,
             grid=(slab // part,),
             in_specs=[
-                pl.BlockSpec((1, slots), lambda i, n: (0, 0)),
-                pl.BlockSpec((part, width), lambda i, n: (i, 0)),
+                pl.BlockSpec((1, slots), lambda i, n, o: (0, 0)),
+                pl.BlockSpec((part, width), lambda i, n, o: (i, 0)),
             ],
-            out_specs=pl.BlockSpec((slots, width), lambda i, n: (0, 0)),
+            out_specs=pl.BlockSpec((slots, width), lambda i, n, o: (0, 0)),
             scratch_shapes=[pltpu.VMEM((slots, width), jnp.float32)],
         ),
         out_shape=jax.ShapeDtypeStruct((slots, width), orbitals.dtype),
         compiler_params=pltpu.CompilerParams(vmem_limit_bytes=VMEM),
         name="pick",
-    )(count, cells, orbitals)
+    )(count, order, cells, orbitals)
 
 
 def whole_arrays(body, ins, outs, after=(), behind=(), scalars=(), scratch=(), flops=0, name=None):
@@ -84,48 +84,44 @@
         out_specs=[vmem] * (len(outs) + 1),
         out_shape=[jax.ShapeDtypeStruct(shape, dtype) for shape, dtype in outs + marks],
         scratch_shapes=scratch,
-        compiler_params=pltpu.CompilerParams(vmem_limit_bytes=30 * 1024 * 1024),
+        compiler_params=pltpu.CompilerParams(vmem_limit_bytes=16 * 1024 * 1024),
         cost_estimate=pl.CostEstimate(flops=flops, bytes_accessed=1024, transcendentals=0),
         name=name,
     )(*scalars, *ins, *after, *behind)
 
 
-def terms(groups, order, panels, tile, outs, after=()):
+def terms(groups, order, first_block, panels, tile, outs, after=()):
     width = panels[0].shape[1]
     depth = panels[0].shape[0]
     cols = depth * len(panels)
     slots = tile.shape[1]
     sizes = [g.shape[0] for g in groups]
-    blocks = sum(sizes) // slots
     col_part, out_part = 256, 640
     n_groups, n_panels = len(groups), len(panels)
-    batch = 512
 
     def body(order_ref, *refs):
         ins, refs = refs[:n_groups], refs[n_groups:]
         panel_refs, refs = refs[:n_panels], refs[n_panels:]
         tile_ref, refs = refs[0], refs[1:]
-        out_refs, (weighted, rows) = refs[: len(outs)], refs[len(outs) :]
-        top = 0
-        for ref, size in zip(ins, sizes):
-            rows[pl.ds(top, size), :] = ref[...]
-            top += size
+        out_refs, (weighted,) = refs[: len(outs)], refs[len(outs) :]
         for k in range(cols // col_part):
             panel_ref = panel_refs[k * col_part // depth]
-            for top in range(0, sum(sizes), batch):
+            top = 0
+            for ref, size in zip(ins, sizes):
                 gram = lax.dot_general(
-                    rows[pl.ds(top, batch), :],
+                    ref[...],
                     panel_ref[pl.ds(k * col_part % depth, col_part), :],
                     (((1,), (1,)), ((), ())),
                     preferred_element_type=jnp.float32,
                 )
-                for j in range(batch // slots):
+                for j in range(size // slots):
                     span = pl.ds(k * col_part, col_part)
                     part = gram[j * slots : (j + 1) * slots, :]
-                    kern = tile_ref[order_ref[top // slots + j], :, span].astype(jnp.float32)
+                    kern = tile_ref[order_ref[first_block + top // slots + j], :, span].astype(jnp.float32)
                     weighted[pl.ds(top + j * slots, slots), span] = (part * kern).astype(
                         jnp.bfloat16
                     )
+                top += size
         for k in range(width // out_part):
             span = pl.ds(k * out_part, out_part)
             term = None
@@ -149,22 +145,42 @@
         [((sum(p[2] for p in parts), width), dtype) for dtype, parts in outs],
         after=after,
         scalars=(order,),
-        scratch=[pltpu.VMEM((sum(sizes), n), jnp.bfloat16) for n in (cols, width)],
+        scratch=[pltpu.VMEM((sum(sizes), cols), jnp.bfloat16)],
         flops=4 * sum(sizes) * cols * width,
         name="terms",
     )
 
 
-def stack(*ins, after=()):
+def stacks(pieces, after=(), behind=()):
+    ins = [a for parts in pieces for a in parts]
+    rows = [sum(a.shape[0] for a in parts) for parts in pieces]
+
+    def body(*refs):
+        i = 0
+        for out, parts in zip(refs[len(ins) :], pieces):
+            top = 0
+            for a in parts:
+                out[pl.ds(top, a.shape[0]), :] = refs[i][...]
+                top += a.shape[0]
+                i += 1
+
+    outs = [((n, ins[0].shape[1]), ins[0].dtype) for n in rows]
+    return whole_arrays(body, ins, outs, after=after, behind=behind, name="stacks")
+
+
+def place(ins, order, first_place, slots, after=(), behind=()):
     rows, width = sum(a.shape[0] for a in ins), ins[0].shape[1]
 
-    def body(*refs):
-        top = 0
-        for ref in refs[: len(ins)]:
-            refs[len(ins)][pl.ds(top, ref.shape[0]), :] = ref[...]
-            top += ref.shape[0]
-
-    return whole_arrays(body, ins, [((rows, width), ins[0].dtype)], after=after, name="stack")
+    def body(order_ref, *refs):
+        i = 0
+        for ref, a in zip(refs, ins):
+            for start in range(0, a.shape[0], slots):
+                at = pl.multiple_of(order_ref[first_place + i] * slots, slots)
+                refs[len(ins)][pl.ds(at, slots), :] = ref[pl.ds(start, slots), :]
+                i += 1
+
+    outs = [((rows, width), ins[0].dtype)]
+    return whole_arrays(body, ins, outs, after=after, behind=behind, scalars=(order,), name="place")
 
 
 def sums(mine, got, cuts, dtype, after=(), behind=()):
@@ -205,43 +221,63 @@
     def second(a, by):
         return lax.ppermute(a, ("row", "col"), plane_perm(n_row, n_col, 0, by))
 
+    def other_core(a):
+        return lax.ppermute(a, "row", [(r, r ^ 1) for r in range(n_row)])
+
+    def around_z(a):
+        to = [(r + 2 - 4 * (r % 2)) % n_row for r in range(n_row)]
+        return lax.ppermute(a, "row", list(enumerate(to)))
+
     def on_device(orbitals, point_cell, point_count, kernel):
         slab, width = orbitals.shape
         slots = point_cell.shape[2]
-        own = pick(orbitals, point_cell.reshape(1, slots), point_count)
+
+        offsets = (0, -1, 1, 2)
+        row, col = lax.axis_index("row"), lax.axis_index("col")
+        z, core, y, x = row // 2, row % 2, col // SIDE, col % SIDE
+        order = []
+        for b in offsets:
+            for a in offsets:
+                dx, dy = jnp.where(core == 0, a, b), jnp.where(core == 0, b, a)
+                order.append(((y + dy) % SIDE) * SIDE + (x + dx) % SIDE)
+        for of in (core, 1 - core):
+            order += [2 * ((z + (2 * of - 1) * step + SIDE) % SIDE) + of for step in range(SIDE)]
+        order = jnp.stack(order).astype(jnp.int32)
+
+        own = pick(orbitals, point_cell.reshape(1, slots), point_count, order)
         tile = kernel.reshape(n_col, slots, -1)
-
-        offsets = (0, -1, 1, 2)
         low, high, far = first(own, 1), first(own, -1), first(own, 2)
-        near, mark = stack(own, low)
-        near_low, near_high = second(near, 1), second(near, -1)
-        wide, _ = stack(high, far, after=(mark,))
-        wide_low, wide_high = second(wide, 1), second(wide, -1)
-        panels = (lax.all_gather(own, "row", axis=0, tiled=True),)
-
-        row, col = lax.axis_index("row"), lax.axis_index("col")
-        core, y, x = row % 2, col // SIDE, col % SIDE
+        along = [own]
+        for _ in range(SIDE - 1):
+            along.append(around_z(along[-1]))
+        near, wide, mark = stacks(((own, low), (high, far)))
+        near_low, wide_high = second(near, 1), second(wide, -1)
+        wide_low, near_high = second(wide, 1), second(near, -1)
+        mine, mark = stacks((along,), after=(mark,), behind=(near_low, wide_high, tile))
+        panel, mark = place(
+            (mine, other_core(mine)),
+            order,
+            SIDE * SIDE,
+            slots,
+            after=(mark,),
+        )
 
         def terms_of(groups, bs, after=()):
-            blocks = []
-            for b in bs:
-                for a in offsets:
-                    dx, dy = jnp.where(core == 0, a, b), jnp.where(core == 0, b, a)
-                    blocks.append(((y + dy) % SIDE) * SIDE + (x + dx) % SIDE)
-            order = jnp.stack(blocks).astype(jnp.int32)
             outs = [
                 (f32 if k == 0 else bf, [(4 * i + k, 0, slots) for i in range(len(bs))])
                 for k in range(4)
             ]
-            return terms(groups, order, panels, tile, outs, after=after)
+            at = SIDE * offsets.index(bs[0])
+            return terms(groups, order, at, (panel,), tile, outs, after=after)
 
         def over_first(t):
-            return first(t[1], -1), first(t[2], 1), first(t[3], 2)
+            far = first(t[3], 2)
+            return far, first(t[1], -1), first(t[2], 1)
 
         def total(mine, got):
             return mine + sum(a.astype(f32) for a in got)
 
-        *t_here, mark = terms_of((near, wide), (0,))
+        *t_here, mark = terms_of((near, wide), (0,), after=(mark,))
         got_here = over_first(t_here)
         near_far, wide_far = second(near_low, 1), second(wide_high, -1)
         *t_near, mark = terms_of((near_low, wide_low, near_high, wide_high), (-1, 1), after=(mark,))

time: 144 us -> 136 us (0.944)
  the two profiles are of different devices: /device:TPU:96 before, /device:TPU:6 now
where the time goes in v3:
time: 136 us; the launch traced here: 135 us
  waiting for transfers between devices  46.4 us (34%)
  starting transfers between devices  42 us (31%)
  Pallas kernels  33.1 us (24%)
  local copies, waits for them, and re-layouts  11.2 us (8%)
    ppermute x12, waiting for transfers between devices, first(): return lax.ppermute(a, ('row', 'col'), plane_perm(n_row, n_col, by, 0))  27.6 us
    pallas_call x9, Pallas kernels, whole_arrays(): pl.pallas_call(run, in_specs=[smem] * len(scalars) + [vmem] * (len(ins) +...  26.6 us
    ppermute x12, starting transfers between devices, first(): return lax.ppermute(a, ('row', 'col'), plane_perm(n_row, n_col, by, 0))  24.1 us
    ppermute x9, starting transfers between devices, second(): return lax.ppermute(a, ('row', 'col'), plane_perm(n_row, n_col, 0, by))  13.9 us
    ppermute x9, waiting for transfers between devices, second(): return lax.ppermute(a, ('row', 'col'), plane_perm(n_row, n_col, 0, by))  12.2 us
    reshape x1, local copies, waits for them, and re-layouts, on_device(): tile = kernel.reshape(n_col, slots, -1)  7.3 us
    ppermute x3, waiting for transfers between devices, around_z(): return lax.ppermute(a, 'row', list(enumerate(to)))  6.64 us
    pallas_call x1, Pallas kernels, pick(): pl.pallas_call(functools.partial(pick_body, slab), grid_spec=pltpu.Prefet...  6.55 us
  transfers between devices with their start and end apart: 25, of which 13 were waited for; matrix products, arithmetic and copies ran while one was open for 5% of the time, Pallas kernels for 18%

profile of v3, /device:TPU:6, one launch (start us, length us, event | category | flops | bytes accessed | tf_op | source)
XLA Modules:
  0.0 135.0 jit_solution(13299293790596617230)
XLA Ops:
  1.7 6.5 %pick.1.refs_0_ = bf16[128,1920]{1,0:T(8,128)(2,1)} custom-call(s32[1,1]{1,0:T(1,128)S(6)} %copy.5.count_ref, s32[24]{0:T(128)} %stack.99.order_ref.refs_0_, s32[1,128]{1,0:T(1,128)} %bitcast.31, bf16[2048,1920]{1,0:T(8,128)(2,1)} %orb_ref.1), custom_call_target="tpu_custom_call" | custom-call | tf_op jit(solution)/shard_map/pick/pallas_call | solution.py:49
  8.3 1.9 %collective-permute-start.3 = (bf16[128,1920]{1,0:T(8,128)(2,1)}, bf16[128,1920]{1,0:T(8,128)(2,1)S(1)}, u32[]{:S(2)}, u32[]{:S(2)}) collective-permute-start(bf16[128,1920]{1,0:T(8,128)(2,1)} %pick.1.refs_0_), channel_id=1, source_target_pairs={{0,32},{16,112},{32,64},{48,16},{64,96},{80,48},{96,0},{112,80},{1... | collective-permute-start | bytes 1474568 | tf_op jit(solution)/shard_map/ppermute | solution.py:229
  13.6 5.7 %collective-permute-done.3.refs_1_ = bf16[128,1920]{1,0:T(8,128)(2,1)S(1)} collective-permute-done((bf16[128,1920]{1,0:T(8,128)(2,1)}, bf16[128,1920]{1,0:T(8,128)(2,1)S(1)}, u32[]{:S(2)}, u32[]{:S(2)}) %collective-permute-start.3) | collective-permute-done | bytes 491552 | tf_op jit(solution)/shard_map/ppermute | solution.py:229
  19.3 6.9 %collective-permute-done.1.refs_2_ = bf16[128,1920]{1,0:T(8,128)(2,1)S(1)} collective-permute-done((bf16[128,1920]{1,0:T(8,128)(2,1)}, bf16[128,1920]{1,0:T(8,128)(2,1)S(1)}, u32[]{:S(2)}, u32[]{:S(2)}) %collective-permute-start.1) | collective-permute-done | bytes 491552 | tf_op jit(solution)/shard_map/ppermute | solution.py:219
  31.9 1.9 %collective-permute-start.5 = (bf16[128,1920]{1,0:T(8,128)(2,1)S(1)}, bf16[128,1920]{1,0:T(8,128)(2,1)}, u32[]{:S(2)}, u32[]{:S(2)}) collective-permute-start(bf16[128,1920]{1,0:T(8,128)(2,1)S(1)} %collective-permute-done.4.refs_2_), channel_id=1, source_target_pairs={{0,32},{16,112},{32,64},{48,16},{64,96},{80,48},{96,0},{112,80},{1... | collective-permute-start | bytes 1474568 | tf_op jit(solution)/shard_map/ppermute | solution.py:229
  33.8 7.3 %reshape.10.refs_7_.refs_4_.refs_6_ = bf16[16,128,1024]{2,1,0:T(8,128)(2,1)} reshape(bf16[1,16,128,8,1,128]{5,3,4,2,1,0:T(8,128)(2,1)} %param.7) | data formatting | bytes 8388608 | tf_op jit(solution)/shard_map/reshape | solution.py:248
  42.1 2.1 %collective-permute-done.6.refs_5_.refs_1_ = bf16[256,1920]{1,0:T(8,128)(2,1)S(1)} collective-permute-done((bf16[256,1920]{1,0:T(8,128)(2,1)}, bf16[256,1920]{1,0:T(8,128)(2,1)S(1)}, u32[]{:S(2)}, u32[]{:S(2)}) %collective-permute-start.6) | collective-permute-done | bytes 983072 | tf_op jit(solution)/shard_map/ppermute | solution.py:222
  44.6 2.2 %copy-done = bf16[16,128,1024]{2,1,0:T(8,128)(2,1)S(1)} copy-done((bf16[16,128,1024]{2,1,0:T(8,128)(2,1)S(1)}, bf16[16,128,1024]{2,1,0:T(8,128)(2,1)}, u32[]{:S(2)}) %copy-start) | copy-done | bytes 4194328
  51.9 2.9 %collective-permute-start.18 = (bf16[256,1920]{1,0:T(8,128)(2,1)S(1)}, bf16[256,1920]{1,0:T(8,128)(2,1)S(1)}, u32[]{:S(2)}, u32[]{:S(2)}) collective-permute-start(bf16[256,1920]{1,0:T(8,128)(2,1)S(1)} %collective-permute-done.7.refs_6_.refs_4_), channel_id=1, source_target_pairs={{0,12},{1,13},{2,14},{3,15},{4,0},{5,1},{6,2},{7,3},{8,4},{9,5},{1... | collective-permute-start | bytes 2949128 | tf_op jit(solution)/shard_map/ppermute | solution.py:222
  55.6 6.3 %terms.3 = (f32[128,1920]{1,0:T(8,128)S(1)}, bf16[128,1920]{1,0:T(8,128)(2,1)S(1)}, bf16[128,1920]{1,0:T(8,128)(2,1)S(1)}, bf16[128,1920]{1,0:T(8,128)(2,1)S(1)}, s32[8,128]{1,0:T(8,128)S(1)}) custom-call(s32[24]{0:T(128)S(1)} %copy-done.4, bf16[256,1920]{1,0:T(8,128)(2,1)} %get-tuple-element.33.refs_1_, bf16[256,1920]{1,0:T(8,128)(2,1)} %get-tuple-element.34.refs_2_, ...), custom_call_target="tpu_custom_call" | custom-call | flops 4026531840 | bytes 1024 | tf_op jit(solution)/shard_map/terms/pallas_call | solution.py:81
  61.9 1.9 %collective-permute-start.9 = (bf16[128,1920]{1,0:T(8,128)(2,1)S(1)}, bf16[128,1920]{1,0:T(8,128)(2,1)S(1)}, u32[]{:S(2)}, u32[]{:S(2)}) collective-permute-start(bf16[128,1920]{1,0:T(8,128)(2,1)S(1)} %get-tuple-element.41), channel_id=1, source_target_pairs={{0,2},{1,3},{2,0},{3,1},{4,6},{5,7},{6,4},{7,5},{8,10},{9,11},{10,... | collective-permute-start | bytes 1474568 | tf_op jit(solution)/shard_map/ppermute | solution.py:219
  64.4 2.7 %collective-permute-start.11 = (bf16[128,1920]{1,0:T(8,128)(2,1)S(1)}, bf16[128,1920]{1,0:T(8,128)(2,1)S(1)}, u32[]{:S(2)}, u32[]{:S(2)}) collective-permute-start(bf16[128,1920]{1,0:T(8,128)(2,1)S(1)} %get-tuple-element.43), channel_id=1, source_target_pairs={{0,1},{1,2},{2,3},{3,0},{4,5},{5,6},{6,7},{7,4},{8,9},{9,10},{10,1... | collective-permute-start | bytes 1474568 | tf_op jit(solution)/shard_map/ppermute | solution.py:219
  67.1 10.0 %terms.4 = (f32[256,1920]{1,0:T(8,128)S(1)}, bf16[256,1920]{1,0:T(8,128)(2,1)S(1)}, bf16[256,1920]{1,0:T(8,128)(2,1)S(1)}, bf16[256,1920]{1,0:T(8,128)(2,1)S(1)}, s32[8,128]{1,0:T(8,128)S(1)}) custom-call(s32[24]{0:T(128)S(1)} %copy-done.4, bf16[256,1920]{1,0:T(8,128)(2,1)S(1)} %collective-permute-done.6.refs_5_.refs_1_, ...), custom_call_target="tpu_custom_call" | custom-call | flops 8053063680 | bytes 1024 | tf_op jit(solution)/shard_map/terms/pallas_call | solution.py:81
  77.6 1.8 %collective-permute-start.14 = (bf16[256,1920]{1,0:T(8,128)(2,1)S(1)}, bf16[256,1920]{1,0:T(8,128)(2,1)S(1)}, u32[]{:S(2)}, u32[]{:S(2)}) collective-permute-start(bf16[256,1920]{1,0:T(8,128)(2,1)S(1)} %get-tuple-element.48), channel_id=1, source_target_pairs={{0,2},{1,3},{2,0},{3,1},{4,6},{5,7},{6,4},{7,5},{8,10},{9,11},{10,... | collective-permute-start | bytes 2949128 | tf_op jit(solution)/shard_map/ppermute | solution.py:219
  79.5 4.2 %collective-permute-done.10.refs_2_ = bf16[128,1920]{1,0:T(8,128)(2,1)S(1)} collective-permute-done((bf16[128,1920]{1,0:T(8,128)(2,1)S(1)}, bf16[128,1920]{1,0:T(8,128)(2,1)S(1)}, u32[]{:S(2)}, u32[]{:S(2)}) %collective-permute-start.10) | collective-permute-done | bytes 491552 | tf_op jit(solution)/shard_map/ppermute | solution.py:219
  84.8 2.1 %collective-permute-start.16 = (bf16[256,1920]{1,0:T(8,128)(2,1)S(1)}, bf16[256,1920]{1,0:T(8,128)(2,1)S(1)}, u32[]{:S(2)}, u32[]{:S(2)}) collective-permute-start(bf16[256,1920]{1,0:T(8,128)(2,1)S(1)} %get-tuple-element.50), channel_id=1, source_target_pairs={{0,1},{1,2},{2,3},{3,0},{4,5},{5,6},{6,7},{7,4},{8,9},{9,10},{10,1... | collective-permute-start | bytes 2949128 | tf_op jit(solution)/shard_map/ppermute | solution.py:219
  87.2 5.4 %terms.5 = (f32[128,1920]{1,0:T(8,128)S(1)}, bf16[128,1920]{1,0:T(8,128)(2,1)S(1)}, bf16[128,1920]{1,0:T(8,128)(2,1)S(1)}, bf16[128,1920]{1,0:T(8,128)(2,1)S(1)}, s32[8,128]{1,0:T(8,128)S(1)}) custom-call(s32[24]{0:T(128)S(1)} %copy-done.4, bf16[256,1920]{1,0:T(8,128)(2,1)S(1)} %collective-permute-done.17.refs_1_, ...), custom_call_target="tpu_custom_call" | custom-call | flops 4026531840 | bytes 1024 | tf_op jit(solution)/shard_map/terms/pallas_call | solution.py:81
  92.7 8.0 %collective-permute-start.22 = (bf16[128,1920]{1,0:T(8,128)(2,1)S(1)}, bf16[128,1920]{1,0:T(8,128)(2,1)S(1)}, u32[]{:S(2)}, u32[]{:S(2)}) collective-permute-start(bf16[128,1920]{1,0:T(8,128)(2,1)S(1)} %get-tuple-element.57), channel_id=1, source_target_pairs={{0,3},{1,0},{2,1},{3,2},{4,7},{5,4},{6,5},{7,6},{8,11},{9,8},{10,9... | collective-permute-start | bytes 1474568 | tf_op jit(solution)/shard_map/ppermute | solution.py:219
  100.7 2.6 %collective-permute-start.23 = (bf16[128,1920]{1,0:T(8,128)(2,1)S(1)}, bf16[128,1920]{1,0:T(8,128)(2,1)S(1)}, u32[]{:S(2)}, u32[]{:S(2)}) collective-permute-start(bf16[128,1920]{1,0:T(8,128)(2,1)S(1)} %get-tuple-element.58), channel_id=1, source_target_pairs={{0,1},{1,2},{2,3},{3,0},{4,5},{5,6},{6,7},{7,4},{8,9},{9,10},{10,1... | collective-permute-start | bytes 1474568 | tf_op jit(solution)/shard_map/ppermute | solution.py:219
  103.3 7.9 %collective-permute-done.15.refs_2_ = bf16[256,1920]{1,0:T(8,128)(2,1)S(1)} collective-permute-done((bf16[256,1920]{1,0:T(8,128)(2,1)S(1)}, bf16[256,1920]{1,0:T(8,128)(2,1)S(1)}, u32[]{:S(2)}, u32[]{:S(2)}) %collective-permute-start.15) | collective-permute-done | bytes 983072 | tf_op jit(solution)/shard_map/ppermute | solution.py:219
  111.7 2.0 %collective-permute-start.20 = (bf16[128,1920]{1,0:T(8,128)(2,1)S(1)}, bf16[128,1920]{1,0:T(8,128)(2,1)S(1)}, u32[]{:S(2)}, u32[]{:S(2)}) collective-permute-start(bf16[128,1920]{1,0:T(8,128)(2,1)S(1)} %get-tuple-element.54), channel_id=1, source_target_pairs={{0,4},{1,5},{2,6},{3,7},{4,8},{5,9},{6,10},{7,11},{8,12},{9,13},{1... | collective-permute-start | bytes 1474568 | tf_op jit(solution)/shard_map/ppermute | solution.py:222
  113.7 8.0 %collective-permute-done.22.refs_2_ = bf16[128,1920]{1,0:T(8,128)(2,1)S(1)} collective-permute-done((bf16[128,1920]{1,0:T(8,128)(2,1)S(1)}, bf16[128,1920]{1,0:T(8,128)(2,1)S(1)}, u32[]{:S(2)}, u32[]{:S(2)}) %collective-permute-start.22) | collective-permute-done | bytes 491552 | tf_op jit(solution)/shard_map/ppermute | solution.py:219
  123.5 2.1 %collective-permute-start.24 = (bf16[128,1920]{1,0:T(8,128)(2,1)S(1)}, bf16[128,1920]{1,0:T(8,128)(2,1)S(1)}, u32[]{:S(2)}, u32[]{:S(2)}) collective-permute-start(bf16[128,1920]{1,0:T(8,128)(2,1)S(1)} %get-tuple-element.60), channel_id=1, source_target_pairs={{0,8},{1,9},{2,10},{3,11},{4,12},{5,13},{6,14},{7,15},{8,0},{9,1},... | collective-permute-start | bytes 1474568 | tf_op jit(solution)/shard_map/ppermute | solution.py:222
  125.6 8.3 %collective-permute-done.24 = bf16[128,1920]{1,0:T(8,128)(2,1)S(1)} collective-permute-done((bf16[128,1920]{1,0:T(8,128)(2,1)S(1)}, bf16[128,1920]{1,0:T(8,128)(2,1)S(1)}, u32[]{:S(2)}, u32[]{:S(2)}) %collective-permute-start.24) | collective-permute-done | bytes 491552 | tf_op jit(solution)/shard_map/ppermute | solution.py:222
  (49 shorter events, 23.1 us)
Async XLA Ops:
  8.3 11.1 %collective-permute-start.3 = (bf16[128,1920]{1,0:T(8,128)(2,1)}, bf16[128,1920]{1,0:T(8,128)(2,1)S(1)}, u32[]{:S(2)}, u32[]{:S(2)}) collective-permute-start(bf16[128,1920]{1,0:T(8,128)(2,1)} %pick.1.refs_0_), channel_id=1, source_target_pairs={{0,32},{16,112},{32,64},{48,16},{64,96},{80,48},{96,0},{112,80},{1... | collective-permute-start | bytes 1474568 | tf_op jit(solution)/shard_map/ppermute | solution.py:229
  10.2 9.1 %collective-permute-start = (bf16[128,1920]{1,0:T(8,128)(2,1)}, bf16[128,1920]{1,0:T(8,128)(2,1)S(1)}, u32[]{:S(2)}, u32[]{:S(2)}) collective-permute-start(bf16[128,1920]{1,0:T(8,128)(2,1)} %pick.1.refs_0_), channel_id=1, source_target_pairs={{0,1},{1,2},{2,3},{3,0},{4,5},{5,6},{6,7},{7,4},{8,9},{9,10},{10,1... | collective-permute-start | bytes 1474568 | tf_op jit(solution)/shard_map/ppermute | solution.py:219
  10.7 15.5 %collective-permute-start.1 = (bf16[128,1920]{1,0:T(8,128)(2,1)}, bf16[128,1920]{1,0:T(8,128)(2,1)S(1)}, u32[]{:S(2)}, u32[]{:S(2)}) collective-permute-start(bf16[128,1920]{1,0:T(8,128)(2,1)} %pick.1.refs_0_), channel_id=1, source_target_pairs={{0,3},{1,0},{2,1},{3,2},{4,7},{5,4},{6,5},{7,6},{8,11},{9,8},{10,9... | collective-permute-start | bytes 1474568 | tf_op jit(solution)/shard_map/ppermute | solution.py:219
  12.2 14.0 %collective-permute-start.2 = (bf16[128,1920]{1,0:T(8,128)(2,1)}, bf16[128,1920]{1,0:T(8,128)(2,1)S(1)}, u32[]{:S(2)}, u32[]{:S(2)}) collective-permute-start(bf16[128,1920]{1,0:T(8,128)(2,1)} %pick.1.refs_0_), channel_id=1, source_target_pairs={{0,2},{1,3},{2,0},{3,1},{4,6},{5,7},{6,4},{7,5},{8,10},{9,11},{10,... | collective-permute-start | bytes 1474568 | tf_op jit(solution)/shard_map/ppermute | solution.py:219
  19.3 12.6 %collective-permute-start.4 = (bf16[128,1920]{1,0:T(8,128)(2,1)S(1)}, bf16[128,1920]{1,0:T(8,128)(2,1)S(1)}, u32[]{:S(2)}, u32[]{:S(2)}) collective-permute-start(bf16[128,1920]{1,0:T(8,128)(2,1)S(1)} %collective-permute-done.3.refs_1_), channel_id=1, source_target_pairs={{0,32},{16,112},{32,64},{48,16},{64,96},{80,48},{96,0},{112,80},{1... | collective-permute-start | bytes 1474568 | tf_op jit(solution)/shard_map/ppermute | solution.py:229
  28.7 15.5 %collective-permute-start.6 = (bf16[256,1920]{1,0:T(8,128)(2,1)}, bf16[256,1920]{1,0:T(8,128)(2,1)S(1)}, u32[]{:S(2)}, u32[]{:S(2)}) collective-permute-start(bf16[256,1920]{1,0:T(8,128)(2,1)} %get-tuple-element.33.refs_1_), channel_id=1, source_target_pairs={{0,4},{1,5},{2,6},{3,7},{4,8},{5,9},{6,10},{7,11},{8,12},{9,13},{1... | collective-permute-start | bytes 2949128 | tf_op jit(solution)/shard_map/ppermute | solution.py:222
  30.3 14.3 %collective-permute-start.7 = (bf16[256,1920]{1,0:T(8,128)(2,1)}, bf16[256,1920]{1,0:T(8,128)(2,1)S(1)}, u32[]{:S(2)}, u32[]{:S(2)}) collective-permute-start(bf16[256,1920]{1,0:T(8,128)(2,1)} %get-tuple-element.34.refs_2_), channel_id=1, source_target_pairs={{0,12},{1,13},{2,14},{3,15},{4,0},{5,1},{6,2},{7,3},{8,4},{9,5},{1... | collective-permute-start | bytes 2949128 | tf_op jit(solution)/shard_map/ppermute | solution.py:222
  31.9 10.1 %collective-permute-start.5 = (bf16[128,1920]{1,0:T(8,128)(2,1)S(1)}, bf16[128,1920]{1,0:T(8,128)(2,1)}, u32[]{:S(2)}, u32[]{:S(2)}) collective-permute-start(bf16[128,1920]{1,0:T(8,128)(2,1)S(1)} %collective-permute-done.4.refs_2_), channel_id=1, source_target_pairs={{0,32},{16,112},{32,64},{48,16},{64,96},{80,48},{96,0},{112,80},{1... | collective-permute-start | bytes 1474568 | tf_op jit(solution)/shard_map/ppermute | solution.py:229
  48.2 15.7 %collective-permute-start.12 = (bf16[256,1920]{1,0:T(8,128)(2,1)}, bf16[256,1920]{1,0:T(8,128)(2,1)S(1)}, u32[]{:S(2)}, u32[]{:S(2)}) collective-permute-start(bf16[256,1920]{1,0:T(8,128)(2,1)} %get-tuple-element.34.refs_2_), channel_id=1, source_target_pairs={{0,4},{1,5},{2,6},{3,7},{4,8},{5,9},{6,10},{7,11},{8,12},{9,13},{1... | collective-permute-start | bytes 2949128 | tf_op jit(solution)/shard_map/ppermute | solution.py:222
  49.8 14.6 %collective-permute-start.13 = (bf16[256,1920]{1,0:T(8,128)(2,1)}, bf16[256,1920]{1,0:T(8,128)(2,1)S(1)}, u32[]{:S(2)}, u32[]{:S(2)}) collective-permute-start(bf16[256,1920]{1,0:T(8,128)(2,1)} %get-tuple-element.33.refs_1_), channel_id=1, source_target_pairs={{0,12},{1,13},{2,14},{3,15},{4,0},{5,1},{6,2},{7,3},{8,4},{9,5},{1... | collective-permute-start | bytes 2949128 | tf_op jit(solution)/shard_map/ppermute | solution.py:222
  51.5 35.7 %collective-permute-start.17 = (bf16[256,1920]{1,0:T(8,128)(2,1)S(1)}, bf16[256,1920]{1,0:T(8,128)(2,1)S(1)}, u32[]{:S(2)}, u32[]{:S(2)}) collective-permute-start(bf16[256,1920]{1,0:T(8,128)(2,1)S(1)} %collective-permute-done.6.refs_5_.refs_1_), channel_id=1, source_target_pairs={{0,4},{1,5},{2,6},{3,7},{4,8},{5,9},{6,10},{7,11},{8,12},{9,13},{1... | collective-permute-start | bytes 2949128 | tf_op jit(solution)/shard_map/ppermute | solution.py:222
  51.9 35.3 %collective-permute-start.18 = (bf16[256,1920]{1,0:T(8,128)(2,1)S(1)}, bf16[256,1920]{1,0:T(8,128)(2,1)S(1)}, u32[]{:S(2)}, u32[]{:S(2)}) collective-permute-start(bf16[256,1920]{1,0:T(8,128)(2,1)S(1)} %collective-permute-done.7.refs_6_.refs_4_), channel_id=1, source_target_pairs={{0,12},{1,13},{2,14},{3,15},{4,0},{5,1},{6,2},{7,3},{8,4},{9,5},{1... | collective-permute-start | bytes 2949128 | tf_op jit(solution)/shard_map/ppermute | solution.py:222
  61.9 15.7 %collective-permute-start.9 = (bf16[128,1920]{1,0:T(8,128)(2,1)S(1)}, bf16[128,1920]{1,0:T(8,128)(2,1)S(1)}, u32[]{:S(2)}, u32[]{:S(2)}) collective-permute-start(bf16[128,1920]{1,0:T(8,128)(2,1)S(1)} %get-tuple-element.41), channel_id=1, source_target_pairs={{0,2},{1,3},{2,0},{3,1},{4,6},{5,7},{6,4},{7,5},{8,10},{9,11},{10,... | collective-permute-start | bytes 1474568 | tf_op jit(solution)/shard_map/ppermute | solution.py:219
  63.8 19.9 %collective-permute-start.10 = (bf16[128,1920]{1,0:T(8,128)(2,1)S(1)}, bf16[128,1920]{1,0:T(8,128)(2,1)S(1)}, u32[]{:S(2)}, u32[]{:S(2)}) collective-permute-start(bf16[128,1920]{1,0:T(8,128)(2,1)S(1)} %get-tuple-element.42), channel_id=1, source_target_pairs={{0,3},{1,0},{2,1},{3,2},{4,7},{5,4},{6,5},{7,6},{8,11},{9,8},{10,9... | collective-permute-start | bytes 1474568 | tf_op jit(solution)/shard_map/ppermute | solution.py:219
  64.4 20.4 %collective-permute-start.11 = (bf16[128,1920]{1,0:T(8,128)(2,1)S(1)}, bf16[128,1920]{1,0:T(8,128)(2,1)S(1)}, u32[]{:S(2)}, u32[]{:S(2)}) collective-permute-start(bf16[128,1920]{1,0:T(8,128)(2,1)S(1)} %get-tuple-element.43), channel_id=1, source_target_pairs={{0,1},{1,2},{2,3},{3,0},{4,5},{5,6},{6,7},{7,4},{8,9},{9,10},{10,1... | collective-permute-start | bytes 1474568 | tf_op jit(solution)/shard_map/ppermute | solution.py:219
  77.6 23.1 %collective-permute-start.14 = (bf16[256,1920]{1,0:T(8,128)(2,1)S(1)}, bf16[256,1920]{1,0:T(8,128)(2,1)S(1)}, u32[]{:S(2)}, u32[]{:S(2)}) collective-permute-start(bf16[256,1920]{1,0:T(8,128)(2,1)S(1)} %get-tuple-element.48), channel_id=1, source_target_pairs={{0,2},{1,3},{2,0},{3,1},{4,6},{5,7},{6,4},{7,5},{8,10},{9,11},{10,... | collective-permute-start | bytes 2949128 | tf_op jit(solution)/shard_map/ppermute | solution.py:219
  83.7 27.5 %collective-permute-start.15 = (bf16[256,1920]{1,0:T(8,128)(2,1)S(1)}, bf16[256,1920]{1,0:T(8,128)(2,1)S(1)}, u32[]{:S(2)}, u32[]{:S(2)}) collective-permute-start(bf16[256,1920]{1,0:T(8,128)(2,1)S(1)} %get-tuple-element.49), channel_id=1, source_target_pairs={{0,3},{1,0},{2,1},{3,2},{4,7},{5,4},{6,5},{7,6},{8,11},{9,8},{10,9... | collective-permute-start | bytes 2949128 | tf_op jit(solution)/shard_map/ppermute | solution.py:219
  84.8 26.4 %collective-permute-start.16 = (bf16[256,1920]{1,0:T(8,128)(2,1)S(1)}, bf16[256,1920]{1,0:T(8,128)(2,1)S(1)}, u32[]{:S(2)}, u32[]{:S(2)}) collective-permute-start(bf16[256,1920]{1,0:T(8,128)(2,1)S(1)} %get-tuple-element.50), channel_id=1, source_target_pairs={{0,1},{1,2},{2,3},{3,0},{4,5},{5,6},{6,7},{7,4},{8,9},{9,10},{10,1... | collective-permute-start | bytes 2949128 | tf_op jit(solution)/shard_map/ppermute | solution.py:219
  92.6 21.2 %collective-permute-start.21 = (bf16[128,1920]{1,0:T(8,128)(2,1)S(1)}, bf16[128,1920]{1,0:T(8,128)(2,1)S(1)}, u32[]{:S(2)}, u32[]{:S(2)}) collective-permute-start(bf16[128,1920]{1,0:T(8,128)(2,1)S(1)} %get-tuple-element.56), channel_id=1, source_target_pairs={{0,2},{1,3},{2,0},{3,1},{4,6},{5,7},{6,4},{7,5},{8,10},{9,11},{10,... | collective-permute-start | bytes 1474568 | tf_op jit(solution)/shard_map/ppermute | solution.py:219
  92.7 29.0 %collective-permute-start.22 = (bf16[128,1920]{1,0:T(8,128)(2,1)S(1)}, bf16[128,1920]{1,0:T(8,128)(2,1)S(1)}, u32[]{:S(2)}, u32[]{:S(2)}) collective-permute-start(bf16[128,1920]{1,0:T(8,128)(2,1)S(1)} %get-tuple-element.57), channel_id=1, source_target_pairs={{0,3},{1,0},{2,1},{3,2},{4,7},{5,4},{6,5},{7,6},{8,11},{9,8},{10,9... | collective-permute-start | bytes 1474568 | tf_op jit(solution)/shard_map/ppermute | solution.py:219
  100.7 21.0 %collective-permute-start.23 = (bf16[128,1920]{1,0:T(8,128)(2,1)S(1)}, bf16[128,1920]{1,0:T(8,128)(2,1)S(1)}, u32[]{:S(2)}, u32[]{:S(2)}) collective-permute-start(bf16[128,1920]{1,0:T(8,128)(2,1)S(1)} %get-tuple-element.58), channel_id=1, source_target_pairs={{0,1},{1,2},{2,3},{3,0},{4,5},{5,6},{6,7},{7,4},{8,9},{9,10},{10,1... | collective-permute-start | bytes 1474568 | tf_op jit(solution)/shard_map/ppermute | solution.py:219
  111.6 10.5 %collective-permute-start.19 = (bf16[128,1920]{1,0:T(8,128)(2,1)S(1)}, bf16[128,1920]{1,0:T(8,128)(2,1)S(1)}, u32[]{:S(2)}, u32[]{:S(2)}) collective-permute-start(bf16[128,1920]{1,0:T(8,128)(2,1)S(1)} %get-tuple-element.53), channel_id=1, source_target_pairs={{0,12},{1,13},{2,14},{3,15},{4,0},{5,1},{6,2},{7,3},{8,4},{9,5},{1... | collective-permute-start | bytes 1474568 | tf_op jit(solution)/shard_map/ppermute | solution.py:222
  111.7 11.1 %collective-permute-start.20 = (bf16[128,1920]{1,0:T(8,128)(2,1)S(1)}, bf16[128,1920]{1,0:T(8,128)(2,1)S(1)}, u32[]{:S(2)}, u32[]{:S(2)}) collective-permute-start(bf16[128,1920]{1,0:T(8,128)(2,1)S(1)} %get-tuple-element.54), channel_id=1, source_target_pairs={{0,4},{1,5},{2,6},{3,7},{4,8},{5,9},{6,10},{7,11},{8,12},{9,13},{1... | collective-permute-start | bytes 1474568 | tf_op jit(solution)/shard_map/ppermute | solution.py:222
  123.5 10.3 %collective-permute-start.24 = (bf16[128,1920]{1,0:T(8,128)(2,1)S(1)}, bf16[128,1920]{1,0:T(8,128)(2,1)S(1)}, u32[]{:S(2)}, u32[]{:S(2)}) collective-permute-start(bf16[128,1920]{1,0:T(8,128)(2,1)S(1)} %get-tuple-element.60), channel_id=1, source_target_pairs={{0,8},{1,9},{2,10},{3,11},{4,12},{5,13},{6,14},{7,15},{8,0},{9,1},... | collective-permute-start | bytes 1474568 | tf_op jit(solution)/shard_map/ppermute | solution.py:222
  (6 other events, 40.9 us)

commit v4 on v3

--- a/solution.py
+++ b/solution.py
@@ -44,7 +44,7 @@
 def pick(orbitals, cells, count, order):
     slab, width = orbitals.shape
     slots = cells.shape[1]
-    part = 512
+    part = 1024
     assert slab & (slab - 1) == 0
     return pl.pallas_call(
         functools.partial(pick_body, slab),
@@ -88,6 +88,35 @@
         cost_estimate=pl.CostEstimate(flops=flops, bytes_accessed=1024, transcendentals=0),
         name=name,
     )(*scalars, *ins, *after, *behind)
+
+
+def relayout(kernel):
+    rows, outer, inner = kernel.shape
+    part = 512
+
+    def body(in_ref, out_ref, mark_ref, wide_ref):
+        mark_ref[...] = jnp.zeros_like(mark_ref)
+        wide_ref[...] = in_ref[...].astype(jnp.float32).reshape(wide_ref.shape)
+        span = pl.ds(pl.multiple_of(pl.program_id(0) * part, part), part)
+        for r in range(outer):
+            piece = wide_ref[pl.ds(r, part, stride=outer), :]
+            out_ref[span, pl.ds(r * inner, inner)] = piece.astype(out_ref.dtype)
+
+    vmem = pl.BlockSpec(memory_space=pltpu.VMEM)
+    return pl.pallas_call(
+        body,
+        grid=(rows // part,),
+        in_specs=[pl.BlockSpec((part, outer, inner), lambda i: (i, 0, 0))],
+        out_specs=[vmem, vmem],
+        out_shape=[
+            jax.ShapeDtypeStruct((rows, outer * inner), kernel.dtype),
+            jax.ShapeDtypeStruct((8, 128), jnp.int32),
+        ],
+        scratch_shapes=[pltpu.VMEM((part * outer, inner), jnp.float32)],
+        compiler_params=pltpu.CompilerParams(vmem_limit_bytes=16 * 1024 * 1024),
+        cost_estimate=pl.CostEstimate(flops=0, bytes_accessed=1024, transcendentals=0),
+        name="relayout",
+    )(kernel)
 
 
 def terms(groups, order, first_block, panels, tile, outs, after=()):
@@ -232,11 +261,11 @@
         slab, width = orbitals.shape
         slots = point_cell.shape[2]
 
-        offsets = (0, -1, 1, 2)
+        offsets, b_offsets = (2, 1, -1, 0), (0, -1, 1, 2)
         row, col = lax.axis_index("row"), lax.axis_index("col")
         z, core, y, x = row // 2, row % 2, col // SIDE, col % SIDE
         order = []
-        for b in offsets:
+        for b in b_offsets:
             for a in offsets:
                 dx, dy = jnp.where(core == 0, a, b), jnp.where(core == 0, b, a)
                 order.append(((y + dy) % SIDE) * SIDE + (x + dx) % SIDE)
@@ -245,15 +274,17 @@
         order = jnp.stack(order).astype(jnp.int32)
 
         own = pick(orbitals, point_cell.reshape(1, slots), point_count, order)
-        tile = kernel.reshape(n_col, slots, -1)
-        low, high, far = first(own, 1), first(own, -1), first(own, 2)
+        tile, mark = relayout(kernel.reshape(n_col * slots, n_row, slots))
+        tile = tile.reshape(n_col, slots, -1)
+        far = first(own, 2)
+        low, high = first(own, 1), first(own, -1)
         along = [own]
         for _ in range(SIDE - 1):
             along.append(around_z(along[-1]))
-        near, wide, mark = stacks(((own, low), (high, far)))
+        wide, near, mark = stacks(((far, high), (low, own)), after=(mark,))
         near_low, wide_high = second(near, 1), second(wide, -1)
         wide_low, near_high = second(wide, 1), second(near, -1)
-        mine, mark = stacks((along,), after=(mark,), behind=(near_low, wide_high, tile))
+        mine, mark = stacks((along,), after=(mark,), behind=(near_low, wide_high))
         panel, mark = place(
             (mine, other_core(mine)),
             order,
@@ -264,30 +295,29 @@
 
         def terms_of(groups, bs, after=()):
             outs = [
-                (f32 if k == 0 else bf, [(4 * i + k, 0, slots) for i in range(len(bs))])
-                for k in range(4)
+                (f32 if a == 0 else bf, [(4 * i + k, 0, slots) for i in range(len(bs))])
+                for k, a in enumerate(offsets)
             ]
-            at = SIDE * offsets.index(bs[0])
+            at = SIDE * b_offsets.index(bs[0])
             return terms(groups, order, at, (panel,), tile, outs, after=after)
 
         def over_first(t):
-            far = first(t[3], 2)
-            return far, first(t[1], -1), first(t[2], 1)
+            return first(t[0], 2), first(t[1], 1), first(t[2], -1)
 
         def total(mine, got):
             return mine + sum(a.astype(f32) for a in got)
 
-        *t_here, mark = terms_of((near, wide), (0,), after=(mark,))
+        *t_here, mark = terms_of((wide, near), (0,), after=(mark,))
         got_here = over_first(t_here)
         near_far, wide_far = second(near_low, 1), second(wide_high, -1)
-        *t_near, mark = terms_of((near_low, wide_low, near_high, wide_high), (-1, 1), after=(mark,))
-        here, mark = sums(t_here[0], got_here, 1, f32, after=(mark,))
+        *t_near, mark = terms_of((wide_low, near_low, wide_high, near_high), (-1, 1), after=(mark,))
+        here, mark = sums(t_here[3], got_here, 1, f32, after=(mark,))
         got_near = over_first(t_near)
-        *t_far, mark = terms_of((near_far, wide_far), (2,), after=(mark,))
+        *t_far, mark = terms_of((wide_far, near_far), (2,), after=(mark,))
         got_far = over_first(t_far)
-        to_low, to_high, mark = sums(t_near[0], got_near, 2, bf, after=(mark,))
+        to_low, to_high, mark = sums(t_near[3], got_near, 2, bf, after=(mark,))
         got = second(to_low, -1), second(to_high, 1)
-        to_far, _ = sums(t_far[0], got_far, 1, bf, after=(mark,), behind=got)
+        to_far, _ = sums(t_far[3], got_far, 1, bf, after=(mark,), behind=got)
         result = total(here, (*got, second(to_far, 2)))
         return result.reshape(1, 1, slots, width)
 

time: 136 us -> 128 us (0.941)
  waiting for transfers between devices: 46.4 us -> 56.5 us
  local copies, waits for them, and re-layouts: 11.2 us -> 2.79 us
  starting transfers between devices: 42 us -> 34.9 us
  Pallas kernels: 33.1 us -> 31.2 us
    ppermute x12, starting transfers between devices: 24.1 us -> 16.5 us  [first(): return lax.ppermute(a, ('row', 'col'), plane_perm(n_row, n_col, by, 0))]
    reshape x1 -> x0, local copies, waits for them, and re-layouts: 7.3 us -> none  [on_device(): tile = kernel.reshape(n_col, slots, -1)]
    ppermute x12, waiting for transfers between devices: 27.6 us -> 32.8 us  [first(): return lax.ppermute(a, ('row', 'col'), plane_perm(n_row, n_col, by, 0))]
    pallas_call x9, Pallas kernels: 26.6 us -> 23 us  [whole_arrays(): pl.pallas_call(run, in_specs=[smem] * len(scalars) + [vmem] * (len(ins) +...]
    ppermute x9, waiting for transfers between devices: 12.2 us -> 15.1 us  [second(): return lax.ppermute(a, ('row', 'col'), plane_perm(n_row, n_col, 0, by))]
    pallas_call x0 -> x1, Pallas kernels: none -> 2.55 us  [relayout(): pl.pallas_call(body, grid=(rows // part,), in_specs=[pl.BlockSpec((part,...]
    ppermute x3, waiting for transfers between devices: 6.64 us -> 8.63 us  [around_z(): return lax.ppermute(a, 'row', list(enumerate(to)))]
    ppermute x3, starting transfers between devices: 3.84 us -> 5.57 us  [around_z(): return lax.ppermute(a, 'row', list(enumerate(to)))]
  transfers between devices with their start and end apart: 25 -> 25, of which waited for: 13 -> 15; matrix products, arithmetic and copies ran while one was open for 5% -> 0% of each run, Pallas kernels for 18% -> 19%
where the time goes in v4:
time: 128 us
  waiting for transfers between devices  56.5 us (44%)
  starting transfers between devices  34.9 us (27%)
  Pallas kernels  31.2 us (24%)
  local copies, waits for them, and re-layouts  2.79 us (2%)
    ppermute x12, waiting for transfers between devices, first(): return lax.ppermute(a, ('row', 'col'), plane_perm(n_row, n_col, by, 0))  32.8 us
    pallas_call x9, Pallas kernels, whole_arrays(): pl.pallas_call(run, in_specs=[smem] * len(scalars) + [vmem] * (len(ins) +...  23 us
    ppermute x12, starting transfers between devices, first(): return lax.ppermute(a, ('row', 'col'), plane_perm(n_row, n_col, by, 0))  16.5 us
    ppermute x9, waiting for transfers between devices, second(): return lax.ppermute(a, ('row', 'col'), plane_perm(n_row, n_col, 0, by))  15.1 us
    ppermute x9, starting transfers between devices, second(): return lax.ppermute(a, ('row', 'col'), plane_perm(n_row, n_col, 0, by))  12.8 us
    ppermute x3, waiting for transfers between devices, around_z(): return lax.ppermute(a, 'row', list(enumerate(to)))  8.63 us
    pallas_call x1, Pallas kernels, pick(): pl.pallas_call(functools.partial(pick_body, slab), grid_spec=pltpu.Prefet...  5.69 us
    ppermute x3, starting transfers between devices, around_z(): return lax.ppermute(a, 'row', list(enumerate(to)))  5.57 us
  transfers between devices with their start and end apart: 25, of which 15 were waited for; matrix products, arithmetic and copies ran while one was open for 0% of the time, Pallas kernels for 19%

profile of v4, /device:TPU:6, one launch (start us, length us, event | category | flops | bytes accessed | tf_op | source)
XLA Modules:
  0.0 127.8 jit_solution(10984426363200197964)
XLA Ops:
  1.7 5.7 %pick.1.refs_3_.refs_0_ = bf16[128,1920]{1,0:T(8,128)(2,1)} custom-call(s32[1,1]{1,0:T(1,128)S(6)} %copy.5.count_ref, s32[24]{0:T(128)} %stack.99.order_ref.refs_0_, s32[1,128]{1,0:T(1,128)} %bitcast.33, bf16[2048,1920]{1,0:T(8,128)(2,1)} %orb_ref.1), custom_call_target="tpu_custom_call" | custom-call | tf_op jit(solution)/shard_map/pick/pallas_call | solution.py:49
  7.4 1.9 %collective-permute-start.3 = (bf16[128,1920]{1,0:T(8,128)(2,1)}, bf16[128,1920]{1,0:T(8,128)(2,1)S(1)}, u32[]{:S(2)}, u32[]{:S(2)}) collective-permute-start(bf16[128,1920]{1,0:T(8,128)(2,1)} %pick.1.refs_3_.refs_0_), channel_id=1, source_target_pairs={{0,32},{16,112},{32,64},{48,16},{64,96},{80,48},{96,0},{112,80},{1... | collective-permute-start | bytes 1474568 | tf_op jit(solution)/shard_map/ppermute | solution.py:258
  10.7 3.2 %collective-permute-start.2 = (bf16[128,1920]{1,0:T(8,128)(2,1)}, bf16[128,1920]{1,0:T(8,128)(2,1)S(1)}, u32[]{:S(2)}, u32[]{:S(2)}) collective-permute-start(bf16[128,1920]{1,0:T(8,128)(2,1)} %pick.1.refs_3_.refs_0_), channel_id=1, source_target_pairs={{0,1},{1,2},{2,3},{3,0},{4,5},{5,6},{6,7},{7,4},{8,9},{9,10},{10,1... | collective-permute-start | bytes 1474568 | tf_op jit(solution)/shard_map/ppermute | solution.py:248
  13.9 2.2 %copy-done.1 = bf16[1,16,128,8,1,128]{5,3,4,2,1,0:T(8,128)(2,1)S(1)} copy-done((bf16[1,16,128,8,1,128]{5,3,4,2,1,0:T(8,128)(2,1)S(1)}, bf16[1,16,128,8,1,128]{5,3,4,2,1,0:T(8,128)(2,1)}, u32[]{:S(2)}) %copy-start.1) | copy-done | bytes 4194328
  16.1 2.5 %relayout.1 = (bf16[2048,1024]{1,0:T(8,128)(2,1)S(1)}, s32[8,128]{1,0:T(8,128)S(1)}) custom-call(bf16[2048,8,128]{2,1,0:T(8,128)(2,1)S(1)} %bitcast.29), custom_call_target="tpu_custom_call" | custom-call | bytes 1024 | tf_op jit(solution)/shard_map/relayout/pallas_call | solution.py:106
  18.7 2.0 %collective-permute-start.4 = (bf16[128,1920]{1,0:T(8,128)(2,1)S(1)}, bf16[128,1920]{1,0:T(8,128)(2,1)S(1)}, u32[]{:S(2)}, u32[]{:S(2)}) collective-permute-start(bf16[128,1920]{1,0:T(8,128)(2,1)S(1)} %collective-permute-done.3.refs_1_), channel_id=1, source_target_pairs={{0,32},{16,112},{32,64},{48,16},{64,96},{80,48},{96,0},{112,80},{1... | collective-permute-start | bytes 1474568 | tf_op jit(solution)/shard_map/ppermute | solution.py:258
  20.7 4.4 %collective-permute-done.1.refs_1_ = bf16[128,1920]{1,0:T(8,128)(2,1)S(1)} collective-permute-done((bf16[128,1920]{1,0:T(8,128)(2,1)}, bf16[128,1920]{1,0:T(8,128)(2,1)S(1)}, u32[]{:S(2)}, u32[]{:S(2)}) %collective-permute-start.1) | collective-permute-done | bytes 491552 | tf_op jit(solution)/shard_map/ppermute | solution.py:248
  30.5 8.4 %collective-permute-done.5.refs_3_ = bf16[128,1920]{1,0:T(8,128)(2,1)S(1)} collective-permute-done((bf16[128,1920]{1,0:T(8,128)(2,1)S(1)}, bf16[128,1920]{1,0:T(8,128)(2,1)S(1)}, u32[]{:S(2)}, u32[]{:S(2)}) %collective-permute-start.5) | collective-permute-done | bytes 491552 | tf_op jit(solution)/shard_map/ppermute | solution.py:258
  38.8 1.8 %collective-permute-done.6.refs_5_.refs_2_ = bf16[256,1920]{1,0:T(8,128)(2,1)S(1)} collective-permute-done((bf16[256,1920]{1,0:T(8,128)(2,1)S(1)}, bf16[256,1920]{1,0:T(8,128)(2,1)S(1)}, u32[]{:S(2)}, u32[]{:S(2)}) %collective-permute-start.6) | collective-permute-done | bytes 983072 | tf_op jit(solution)/shard_map/ppermute | solution.py:251
  47.4 5.3 %terms.3 = (bf16[128,1920]{1,0:T(8,128)(2,1)S(1)}, bf16[128,1920]{1,0:T(8,128)(2,1)S(1)}, bf16[128,1920]{1,0:T(8,128)(2,1)S(1)}, f32[128,1920]{1,0:T(8,128)S(1)}, s32[8,128]{1,0:T(8,128)S(1)}) custom-call(s32[24]{0:T(128)S(1)} %copy-done.2, bf16[256,1920]{1,0:T(8,128)(2,1)S(1)} %get-tuple-element.36.refs_1_, ...), custom_call_target="tpu_custom_call" | custom-call | flops 4026531840 | bytes 1024 | tf_op jit(solution)/shard_map/terms/pallas_call | solution.py:81
  54.3 2.6 %collective-permute-done.12.refs_1_ = bf16[256,1920]{1,0:T(8,128)(2,1)S(1)} collective-permute-done((bf16[256,1920]{1,0:T(8,128)(2,1)S(1)}, bf16[256,1920]{1,0:T(8,128)(2,1)S(1)}, u32[]{:S(2)}, u32[]{:S(2)}) %collective-permute-start.12) | collective-permute-done | bytes 983072 | tf_op jit(solution)/shard_map/ppermute | solution.py:251
  58.9 10.0 %terms.4 = (bf16[256,1920]{1,0:T(8,128)(2,1)S(1)}, bf16[256,1920]{1,0:T(8,128)(2,1)S(1)}, bf16[256,1920]{1,0:T(8,128)(2,1)S(1)}, f32[256,1920]{1,0:T(8,128)S(1)}, s32[8,128]{1,0:T(8,128)S(1)}) custom-call(s32[24]{0:T(128)S(1)} %copy-done.2, bf16[256,1920]{1,0:T(8,128)(2,1)S(1)} %collective-permute-done.12.refs_1_, ...), custom_call_target="tpu_custom_call" | custom-call | flops 8053063680 | bytes 1024 | tf_op jit(solution)/shard_map/terms/pallas_call | solution.py:81
  68.9 2.1 %collective-permute-start.14 = (bf16[256,1920]{1,0:T(8,128)(2,1)S(1)}, bf16[256,1920]{1,0:T(8,128)(2,1)S(1)}, u32[]{:S(2)}, u32[]{:S(2)}) collective-permute-start(bf16[256,1920]{1,0:T(8,128)(2,1)S(1)} %get-tuple-element.52), channel_id=1, source_target_pairs={{0,2},{1,3},{2,0},{3,1},{4,6},{5,7},{6,4},{7,5},{8,10},{9,11},{10,... | collective-permute-start | bytes 2949128 | tf_op jit(solution)/shard_map/ppermute | solution.py:248
  71.0 4.9 %collective-permute-done.10.refs_2_ = bf16[128,1920]{1,0:T(8,128)(2,1)S(1)} collective-permute-done((bf16[128,1920]{1,0:T(8,128)(2,1)S(1)}, bf16[128,1920]{1,0:T(8,128)(2,1)S(1)}, u32[]{:S(2)}, u32[]{:S(2)}) %collective-permute-start.10) | collective-permute-done | bytes 491552 | tf_op jit(solution)/shard_map/ppermute | solution.py:248
  78.5 5.3 %terms.5 = (bf16[128,1920]{1,0:T(8,128)(2,1)S(1)}, bf16[128,1920]{1,0:T(8,128)(2,1)S(1)}, bf16[128,1920]{1,0:T(8,128)(2,1)S(1)}, f32[128,1920]{1,0:T(8,128)S(1)}, s32[8,128]{1,0:T(8,128)S(1)}) custom-call(s32[24]{0:T(128)S(1)} %copy-done.2, bf16[256,1920]{1,0:T(8,128)(2,1)S(1)} %collective-permute-done.17.refs_1_, ...), custom_call_target="tpu_custom_call" | custom-call | flops 4026531840 | bytes 1024 | tf_op jit(solution)/shard_map/terms/pallas_call | solution.py:81
  83.9 2.1 %collective-permute-start.21 = (bf16[128,1920]{1,0:T(8,128)(2,1)S(1)}, bf16[128,1920]{1,0:T(8,128)(2,1)S(1)}, u32[]{:S(2)}, u32[]{:S(2)}) collective-permute-start(bf16[128,1920]{1,0:T(8,128)(2,1)S(1)} %get-tuple-element.60), channel_id=1, source_target_pairs={{0,2},{1,3},{2,0},{3,1},{4,6},{5,7},{6,4},{7,5},{8,10},{9,11},{10,... | collective-permute-start | bytes 1474568 | tf_op jit(solution)/shard_map/ppermute | solution.py:248
  86.0 2.0 %collective-permute-start.22 = (bf16[128,1920]{1,0:T(8,128)(2,1)S(1)}, bf16[128,1920]{1,0:T(8,128)(2,1)S(1)}, u32[]{:S(2)}, u32[]{:S(2)}) collective-permute-start(bf16[128,1920]{1,0:T(8,128)(2,1)S(1)} %get-tuple-element.61), channel_id=1, source_target_pairs={{0,1},{1,2},{2,3},{3,0},{4,5},{5,6},{6,7},{7,4},{8,9},{9,10},{10,1... | collective-permute-start | bytes 1474568 | tf_op jit(solution)/shard_map/ppermute | solution.py:248
  88.0 9.0 %collective-permute-done.15.refs_2_ = bf16[256,1920]{1,0:T(8,128)(2,1)S(1)} collective-permute-done((bf16[256,1920]{1,0:T(8,128)(2,1)S(1)}, bf16[256,1920]{1,0:T(8,128)(2,1)S(1)}, u32[]{:S(2)}, u32[]{:S(2)}) %collective-permute-start.15) | collective-permute-done | bytes 983072 | tf_op jit(solution)/shard_map/ppermute | solution.py:248
  97.0 6.3 %collective-permute-done.16.refs_3_ = bf16[256,1920]{1,0:T(8,128)(2,1)S(1)} collective-permute-done((bf16[256,1920]{1,0:T(8,128)(2,1)S(1)}, bf16[256,1920]{1,0:T(8,128)(2,1)S(1)}, u32[]{:S(2)}, u32[]{:S(2)}) %collective-permute-start.16) | collective-permute-done | bytes 983072 | tf_op jit(solution)/shard_map/ppermute | solution.py:248
  103.8 2.0 %collective-permute-start.20 = (bf16[128,1920]{1,0:T(8,128)(2,1)S(1)}, bf16[128,1920]{1,0:T(8,128)(2,1)S(1)}, u32[]{:S(2)}, u32[]{:S(2)}) collective-permute-start(bf16[128,1920]{1,0:T(8,128)(2,1)S(1)} %get-tuple-element.58), channel_id=1, source_target_pairs={{0,4},{1,5},{2,6},{3,7},{4,8},{5,9},{6,10},{7,11},{8,12},{9,13},{1... | collective-permute-start | bytes 1474568 | tf_op jit(solution)/shard_map/ppermute | solution.py:251
  105.8 6.4 %collective-permute-done.22.refs_2_ = bf16[128,1920]{1,0:T(8,128)(2,1)S(1)} collective-permute-done((bf16[128,1920]{1,0:T(8,128)(2,1)S(1)}, bf16[128,1920]{1,0:T(8,128)(2,1)S(1)}, u32[]{:S(2)}, u32[]{:S(2)}) %collective-permute-start.22) | collective-permute-done | bytes 491552 | tf_op jit(solution)/shard_map/ppermute | solution.py:248
  112.2 1.7 %collective-permute-done.23.refs_3_ = bf16[128,1920]{1,0:T(8,128)(2,1)S(1)} collective-permute-done((bf16[128,1920]{1,0:T(8,128)(2,1)S(1)}, bf16[128,1920]{1,0:T(8,128)(2,1)S(1)}, u32[]{:S(2)}, u32[]{:S(2)}) %collective-permute-start.23) | collective-permute-done | bytes 491552 | tf_op jit(solution)/shard_map/ppermute | solution.py:248
  116.3 2.1 %collective-permute-start.24 = (bf16[128,1920]{1,0:T(8,128)(2,1)S(1)}, bf16[128,1920]{1,0:T(8,128)(2,1)S(1)}, u32[]{:S(2)}, u32[]{:S(2)}) collective-permute-start(bf16[128,1920]{1,0:T(8,128)(2,1)S(1)} %get-tuple-element.64), channel_id=1, source_target_pairs={{0,8},{1,9},{2,10},{3,11},{4,12},{5,13},{6,14},{7,15},{8,0},{9,1},... | collective-permute-start | bytes 1474568 | tf_op jit(solution)/shard_map/ppermute | solution.py:251
  118.4 8.3 %collective-permute-done.24 = bf16[128,1920]{1,0:T(8,128)(2,1)S(1)} collective-permute-done((bf16[128,1920]{1,0:T(8,128)(2,1)S(1)}, bf16[128,1920]{1,0:T(8,128)(2,1)S(1)}, u32[]{:S(2)}, u32[]{:S(2)}) %collective-permute-start.24) | collective-permute-done | bytes 491552 | tf_op jit(solution)/shard_map/ppermute | solution.py:251
  (45 shorter events, 24.4 us)
Async XLA Ops:
  7.4 11.3 %collective-permute-start.3 = (bf16[128,1920]{1,0:T(8,128)(2,1)}, bf16[128,1920]{1,0:T(8,128)(2,1)S(1)}, u32[]{:S(2)}, u32[]{:S(2)}) collective-permute-start(bf16[128,1920]{1,0:T(8,128)(2,1)} %pick.1.refs_3_.refs_0_), channel_id=1, source_target_pairs={{0,32},{16,112},{32,64},{48,16},{64,96},{80,48},{96,0},{112,80},{1... | collective-permute-start | bytes 1474568 | tf_op jit(solution)/shard_map/ppermute | solution.py:258
  9.3 11.4 %collective-permute-start = (bf16[128,1920]{1,0:T(8,128)(2,1)}, bf16[128,1920]{1,0:T(8,128)(2,1)S(1)}, u32[]{:S(2)}, u32[]{:S(2)}) collective-permute-start(bf16[128,1920]{1,0:T(8,128)(2,1)} %pick.1.refs_3_.refs_0_), channel_id=1, source_target_pairs={{0,2},{1,3},{2,0},{3,1},{4,6},{5,7},{6,4},{7,5},{8,10},{9,11},{10,... | collective-permute-start | bytes 1474568 | tf_op jit(solution)/shard_map/ppermute | solution.py:248
  10.7 14.4 %collective-permute-start.1 = (bf16[128,1920]{1,0:T(8,128)(2,1)}, bf16[128,1920]{1,0:T(8,128)(2,1)S(1)}, u32[]{:S(2)}, u32[]{:S(2)}) collective-permute-start(bf16[128,1920]{1,0:T(8,128)(2,1)} %pick.1.refs_3_.refs_0_), channel_id=1, source_target_pairs={{0,3},{1,0},{2,1},{3,2},{4,7},{5,4},{6,5},{7,6},{8,11},{9,8},{10,9... | collective-permute-start | bytes 1474568 | tf_op jit(solution)/shard_map/ppermute | solution.py:248
  10.7 14.4 %collective-permute-start.2 = (bf16[128,1920]{1,0:T(8,128)(2,1)}, bf16[128,1920]{1,0:T(8,128)(2,1)S(1)}, u32[]{:S(2)}, u32[]{:S(2)}) collective-permute-start(bf16[128,1920]{1,0:T(8,128)(2,1)} %pick.1.refs_3_.refs_0_), channel_id=1, source_target_pairs={{0,1},{1,2},{2,3},{3,0},{4,5},{5,6},{6,7},{7,4},{8,9},{9,10},{10,1... | collective-permute-start | bytes 1474568 | tf_op jit(solution)/shard_map/ppermute | solution.py:248
  18.7 10.1 %collective-permute-start.4 = (bf16[128,1920]{1,0:T(8,128)(2,1)S(1)}, bf16[128,1920]{1,0:T(8,128)(2,1)S(1)}, u32[]{:S(2)}, u32[]{:S(2)}) collective-permute-start(bf16[128,1920]{1,0:T(8,128)(2,1)S(1)} %collective-permute-done.3.refs_1_), channel_id=1, source_target_pairs={{0,32},{16,112},{32,64},{48,16},{64,96},{80,48},{96,0},{112,80},{1... | collective-permute-start | bytes 1474568 | tf_op jit(solution)/shard_map/ppermute | solution.py:258
  25.2 15.4 %collective-permute-start.6 = (bf16[256,1920]{1,0:T(8,128)(2,1)S(1)}, bf16[256,1920]{1,0:T(8,128)(2,1)S(1)}, u32[]{:S(2)}, u32[]{:S(2)}) collective-permute-start(bf16[256,1920]{1,0:T(8,128)(2,1)S(1)} %get-tuple-element.37.refs_2_), channel_id=1, source_target_pairs={{0,4},{1,5},{2,6},{3,7},{4,8},{5,9},{6,10},{7,11},{8,12},{9,13},{1... | collective-permute-start | bytes 2949128 | tf_op jit(solution)/shard_map/ppermute | solution.py:251
  26.9 14.1 %collective-permute-start.7 = (bf16[256,1920]{1,0:T(8,128)(2,1)S(1)}, bf16[256,1920]{1,0:T(8,128)(2,1)S(1)}, u32[]{:S(2)}, u32[]{:S(2)}) collective-permute-start(bf16[256,1920]{1,0:T(8,128)(2,1)S(1)} %get-tuple-element.36.refs_1_), channel_id=1, source_target_pairs={{0,12},{1,13},{2,14},{3,15},{4,0},{5,1},{6,2},{7,3},{8,4},{9,5},{1... | collective-permute-start | bytes 2949128 | tf_op jit(solution)/shard_map/ppermute | solution.py:251
  28.8 10.0 %collective-permute-start.5 = (bf16[128,1920]{1,0:T(8,128)(2,1)S(1)}, bf16[128,1920]{1,0:T(8,128)(2,1)S(1)}, u32[]{:S(2)}, u32[]{:S(2)}) collective-permute-start(bf16[128,1920]{1,0:T(8,128)(2,1)S(1)} %collective-permute-done.4.refs_2_), channel_id=1, source_target_pairs={{0,32},{16,112},{32,64},{48,16},{64,96},{80,48},{96,0},{112,80},{1... | collective-permute-start | bytes 1474568 | tf_op jit(solution)/shard_map/ppermute | solution.py:258
  41.2 15.7 %collective-permute-start.12 = (bf16[256,1920]{1,0:T(8,128)(2,1)S(1)}, bf16[256,1920]{1,0:T(8,128)(2,1)S(1)}, u32[]{:S(2)}, u32[]{:S(2)}) collective-permute-start(bf16[256,1920]{1,0:T(8,128)(2,1)S(1)} %get-tuple-element.36.refs_1_), channel_id=1, source_target_pairs={{0,4},{1,5},{2,6},{3,7},{4,8},{5,9},{6,10},{7,11},{8,12},{9,13},{1... | collective-permute-start | bytes 2949128 | tf_op jit(solution)/shard_map/ppermute | solution.py:251
  42.9 14.7 %collective-permute-start.13 = (bf16[256,1920]{1,0:T(8,128)(2,1)S(1)}, bf16[256,1920]{1,0:T(8,128)(2,1)S(1)}, u32[]{:S(2)}, u32[]{:S(2)}) collective-permute-start(bf16[256,1920]{1,0:T(8,128)(2,1)S(1)} %get-tuple-element.37.refs_2_), channel_id=1, source_target_pairs={{0,12},{1,13},{2,14},{3,15},{4,0},{5,1},{6,2},{7,3},{8,4},{9,5},{1... | collective-permute-start | bytes 2949128 | tf_op jit(solution)/shard_map/ppermute | solution.py:251
  44.5 34.0 %collective-permute-start.17 = (bf16[256,1920]{1,0:T(8,128)(2,1)S(1)}, bf16[256,1920]{1,0:T(8,128)(2,1)S(1)}, u32[]{:S(2)}, u32[]{:S(2)}) collective-permute-start(bf16[256,1920]{1,0:T(8,128)(2,1)S(1)} %collective-permute-done.7.refs_6_.refs_3_), channel_id=1, source_target_pairs={{0,12},{1,13},{2,14},{3,15},{4,0},{5,1},{6,2},{7,3},{8,4},{9,5},{1... | collective-permute-start | bytes 2949128 | tf_op jit(solution)/shard_map/ppermute | solution.py:251
  46.2 32.3 %collective-permute-start.18 = (bf16[256,1920]{1,0:T(8,128)(2,1)S(1)}, bf16[256,1920]{1,0:T(8,128)(2,1)S(1)}, u32[]{:S(2)}, u32[]{:S(2)}) collective-permute-start(bf16[256,1920]{1,0:T(8,128)(2,1)S(1)} %collective-permute-done.6.refs_5_.refs_2_), channel_id=1, source_target_pairs={{0,4},{1,5},{2,6},{3,7},{4,8},{5,9},{6,10},{7,11},{8,12},{9,13},{1... | collective-permute-start | bytes 2949128 | tf_op jit(solution)/shard_map/ppermute | solution.py:251
  52.7 16.2 %collective-permute-start.9 = (bf16[128,1920]{1,0:T(8,128)(2,1)S(1)}, bf16[128,1920]{1,0:T(8,128)(2,1)S(1)}, u32[]{:S(2)}, u32[]{:S(2)}) collective-permute-start(bf16[128,1920]{1,0:T(8,128)(2,1)S(1)} %get-tuple-element.45), channel_id=1, source_target_pairs={{0,2},{1,3},{2,0},{3,1},{4,6},{5,7},{6,4},{7,5},{8,10},{9,11},{10,... | collective-permute-start | bytes 1474568 | tf_op jit(solution)/shard_map/ppermute | solution.py:248
  56.9 19.0 %collective-permute-start.10 = (bf16[128,1920]{1,0:T(8,128)(2,1)S(1)}, bf16[128,1920]{1,0:T(8,128)(2,1)S(1)}, u32[]{:S(2)}, u32[]{:S(2)}) collective-permute-start(bf16[128,1920]{1,0:T(8,128)(2,1)S(1)} %get-tuple-element.46), channel_id=1, source_target_pairs={{0,1},{1,2},{2,3},{3,0},{4,5},{5,6},{6,7},{7,4},{8,9},{9,10},{10,1... | collective-permute-start | bytes 1474568 | tf_op jit(solution)/shard_map/ppermute | solution.py:248
  57.5 18.8 %collective-permute-start.11 = (bf16[128,1920]{1,0:T(8,128)(2,1)S(1)}, bf16[128,1920]{1,0:T(8,128)(2,1)S(1)}, u32[]{:S(2)}, u32[]{:S(2)}) collective-permute-start(bf16[128,1920]{1,0:T(8,128)(2,1)S(1)} %get-tuple-element.47), channel_id=1, source_target_pairs={{0,3},{1,0},{2,1},{3,2},{4,7},{5,4},{6,5},{7,6},{8,11},{9,8},{10,9... | collective-permute-start | bytes 1474568 | tf_op jit(solution)/shard_map/ppermute | solution.py:248
  68.9 19.1 %collective-permute-start.14 = (bf16[256,1920]{1,0:T(8,128)(2,1)S(1)}, bf16[256,1920]{1,0:T(8,128)(2,1)S(1)}, u32[]{:S(2)}, u32[]{:S(2)}) collective-permute-start(bf16[256,1920]{1,0:T(8,128)(2,1)S(1)} %get-tuple-element.52), channel_id=1, source_target_pairs={{0,2},{1,3},{2,0},{3,1},{4,6},{5,7},{6,4},{7,5},{8,10},{9,11},{10,... | collective-permute-start | bytes 2949128 | tf_op jit(solution)/shard_map/ppermute | solution.py:248
  75.9 21.1 %collective-permute-start.15 = (bf16[256,1920]{1,0:T(8,128)(2,1)S(1)}, bf16[256,1920]{1,0:T(8,128)(2,1)S(1)}, u32[]{:S(2)}, u32[]{:S(2)}) collective-permute-start(bf16[256,1920]{1,0:T(8,128)(2,1)S(1)} %get-tuple-element.53), channel_id=1, source_target_pairs={{0,1},{1,2},{2,3},{3,0},{4,5},{5,6},{6,7},{7,4},{8,9},{9,10},{10,1... | collective-permute-start | bytes 2949128 | tf_op jit(solution)/shard_map/ppermute | solution.py:248
  76.3 27.0 %collective-permute-start.16 = (bf16[256,1920]{1,0:T(8,128)(2,1)S(1)}, bf16[256,1920]{1,0:T(8,128)(2,1)S(1)}, u32[]{:S(2)}, u32[]{:S(2)}) collective-permute-start(bf16[256,1920]{1,0:T(8,128)(2,1)S(1)} %get-tuple-element.54), channel_id=1, source_target_pairs={{0,3},{1,0},{2,1},{3,2},{4,7},{5,4},{6,5},{7,6},{8,11},{9,8},{10,9... | collective-permute-start | bytes 2949128 | tf_op jit(solution)/shard_map/ppermute | solution.py:248
  83.9 22.0 %collective-permute-start.21 = (bf16[128,1920]{1,0:T(8,128)(2,1)S(1)}, bf16[128,1920]{1,0:T(8,128)(2,1)S(1)}, u32[]{:S(2)}, u32[]{:S(2)}) collective-permute-start(bf16[128,1920]{1,0:T(8,128)(2,1)S(1)} %get-tuple-element.60), channel_id=1, source_target_pairs={{0,2},{1,3},{2,0},{3,1},{4,6},{5,7},{6,4},{7,5},{8,10},{9,11},{10,... | collective-permute-start | bytes 1474568 | tf_op jit(solution)/shard_map/ppermute | solution.py:248
  86.0 26.3 %collective-permute-start.22 = (bf16[128,1920]{1,0:T(8,128)(2,1)S(1)}, bf16[128,1920]{1,0:T(8,128)(2,1)S(1)}, u32[]{:S(2)}, u32[]{:S(2)}) collective-permute-start(bf16[128,1920]{1,0:T(8,128)(2,1)S(1)} %get-tuple-element.61), channel_id=1, source_target_pairs={{0,1},{1,2},{2,3},{3,0},{4,5},{5,6},{6,7},{7,4},{8,9},{9,10},{10,1... | collective-permute-start | bytes 1474568 | tf_op jit(solution)/shard_map/ppermute | solution.py:248
  88.0 26.0 %collective-permute-start.23 = (bf16[128,1920]{1,0:T(8,128)(2,1)S(1)}, bf16[128,1920]{1,0:T(8,128)(2,1)S(1)}, u32[]{:S(2)}, u32[]{:S(2)}) collective-permute-start(bf16[128,1920]{1,0:T(8,128)(2,1)S(1)} %get-tuple-element.62), channel_id=1, source_target_pairs={{0,3},{1,0},{2,1},{3,2},{4,7},{5,4},{6,5},{7,6},{8,11},{9,8},{10,9... | collective-permute-start | bytes 1474568 | tf_op jit(solution)/shard_map/ppermute | solution.py:248
  103.7 11.3 %collective-permute-start.19 = (bf16[128,1920]{1,0:T(8,128)(2,1)S(1)}, bf16[128,1920]{1,0:T(8,128)(2,1)S(1)}, u32[]{:S(2)}, u32[]{:S(2)}) collective-permute-start(bf16[128,1920]{1,0:T(8,128)(2,1)S(1)} %get-tuple-element.57), channel_id=1, source_target_pairs={{0,12},{1,13},{2,14},{3,15},{4,0},{5,1},{6,2},{7,3},{8,4},{9,5},{1... | collective-permute-start | bytes 1474568 | tf_op jit(solution)/shard_map/ppermute | solution.py:251
  103.8 11.9 %collective-permute-start.20 = (bf16[128,1920]{1,0:T(8,128)(2,1)S(1)}, bf16[128,1920]{1,0:T(8,128)(2,1)S(1)}, u32[]{:S(2)}, u32[]{:S(2)}) collective-permute-start(bf16[128,1920]{1,0:T(8,128)(2,1)S(1)} %get-tuple-element.58), channel_id=1, source_target_pairs={{0,4},{1,5},{2,6},{3,7},{4,8},{5,9},{6,10},{7,11},{8,12},{9,13},{1... | collective-permute-start | bytes 1474568 | tf_op jit(solution)/shard_map/ppermute | solution.py:251
  116.3 10.3 %collective-permute-start.24 = (bf16[128,1920]{1,0:T(8,128)(2,1)S(1)}, bf16[128,1920]{1,0:T(8,128)(2,1)S(1)}, u32[]{:S(2)}, u32[]{:S(2)}) collective-permute-start(bf16[128,1920]{1,0:T(8,128)(2,1)S(1)} %get-tuple-element.64), channel_id=1, source_target_pairs={{0,8},{1,9},{2,10},{3,11},{4,12},{5,13},{6,14},{7,15},{8,0},{9,1},... | collective-permute-start | bytes 1474568 | tf_op jit(solution)/shard_map/ppermute | solution.py:251
  (4 other events, 53.2 us)

commit v5 on v4

--- a/solution.py
+++ b/solution.py
@@ -125,7 +125,7 @@
     cols = depth * len(panels)
     slots = tile.shape[1]
     sizes = [g.shape[0] for g in groups]
-    col_part, out_part = 256, 640
+    col_part, out_part = 256, 768
     n_groups, n_panels = len(groups), len(panels)
 
     def body(order_ref, *refs):
@@ -151,8 +151,8 @@
                         jnp.bfloat16
                     )
                 top += size
-        for k in range(width // out_part):
-            span = pl.ds(k * out_part, out_part)
+        for start in range(0, width, out_part):
+            span = pl.ds(start, min(out_part, width - start))
             term = None
             for i, panel_ref in enumerate(panel_refs):
                 more = jnp.dot(

time: 128 us -> 128 us (level)
  no operation moved by 1% of the time
where the time goes in v5:
time: 128 us
  waiting for transfers between devices  57.6 us (45%)
  starting transfers between devices  35 us (27%)
  Pallas kernels  30.2 us (24%)
  local copies, waits for them, and re-layouts  2.79 us (2%)
    ppermute x12, waiting for transfers between devices, first(): return lax.ppermute(a, ('row', 'col'), plane_perm(n_row, n_col, by, 0))  33 us
    pallas_call x9, Pallas kernels, whole_arrays(): pl.pallas_call(run, in_specs=[smem] * len(scalars) + [vmem] * (len(ins) +...  21.9 us
    ppermute x12, starting transfers between devices, first(): return lax.ppermute(a, ('row', 'col'), plane_perm(n_row, n_col, by, 0))  16.5 us
    ppermute x9, waiting for transfers between devices, second(): return lax.ppermute(a, ('row', 'col'), plane_perm(n_row, n_col, 0, by))  15.9 us
    ppermute x9, starting transfers between devices, second(): return lax.ppermute(a, ('row', 'col'), plane_perm(n_row, n_col, 0, by))  12.8 us
    ppermute x3, waiting for transfers between devices, around_z(): return lax.ppermute(a, 'row', list(enumerate(to)))  8.63 us
    pallas_call x1, Pallas kernels, pick(): pl.pallas_call(functools.partial(pick_body, slab), grid_spec=pltpu.Prefet...  5.69 us
    ppermute x3, starting transfers between devices, around_z(): return lax.ppermute(a, 'row', list(enumerate(to)))  5.57 us
  transfers between devices with their start and end apart: 25, of which 15 were waited for; matrix products, arithmetic and copies ran while one was open for 0% of the time, Pallas kernels for 19%

profile of v5, /device:TPU:6, one launch (start us, length us, event | category | flops | bytes accessed | tf_op | source)
XLA Modules:
  0.0 127.8 jit_solution(15869050062894327344)
XLA Ops:
  1.7 5.7 %pick.1.refs_3_.refs_0_ = bf16[128,1920]{1,0:T(8,128)(2,1)} custom-call(s32[1,1]{1,0:T(1,128)S(6)} %copy.5.count_ref, s32[24]{0:T(128)} %stack.99.order_ref.refs_0_, s32[1,128]{1,0:T(1,128)} %bitcast.33, bf16[2048,1920]{1,0:T(8,128)(2,1)} %orb_ref.1), custom_call_target="tpu_custom_call" | custom-call | tf_op jit(solution)/shard_map/pick/pallas_call | solution.py:49
  7.4 1.9 %collective-permute-start.3 = (bf16[128,1920]{1,0:T(8,128)(2,1)}, bf16[128,1920]{1,0:T(8,128)(2,1)S(1)}, u32[]{:S(2)}, u32[]{:S(2)}) collective-permute-start(bf16[128,1920]{1,0:T(8,128)(2,1)} %pick.1.refs_3_.refs_0_), channel_id=1, source_target_pairs={{0,32},{16,112},{32,64},{48,16},{64,96},{80,48},{96,0},{112,80},{1... | collective-permute-start | bytes 1474568 | tf_op jit(solution)/shard_map/ppermute | solution.py:258
  10.7 3.2 %collective-permute-start.2 = (bf16[128,1920]{1,0:T(8,128)(2,1)}, bf16[128,1920]{1,0:T(8,128)(2,1)S(1)}, u32[]{:S(2)}, u32[]{:S(2)}) collective-permute-start(bf16[128,1920]{1,0:T(8,128)(2,1)} %pick.1.refs_3_.refs_0_), channel_id=1, source_target_pairs={{0,1},{1,2},{2,3},{3,0},{4,5},{5,6},{6,7},{7,4},{8,9},{9,10},{10,1... | collective-permute-start | bytes 1474568 | tf_op jit(solution)/shard_map/ppermute | solution.py:248
  13.9 2.2 %copy-done.1 = bf16[1,16,128,8,1,128]{5,3,4,2,1,0:T(8,128)(2,1)S(1)} copy-done((bf16[1,16,128,8,1,128]{5,3,4,2,1,0:T(8,128)(2,1)S(1)}, bf16[1,16,128,8,1,128]{5,3,4,2,1,0:T(8,128)(2,1)}, u32[]{:S(2)}) %copy-start.1) | copy-done | bytes 4194328
  16.1 2.5 %relayout.1 = (bf16[2048,1024]{1,0:T(8,128)(2,1)S(1)}, s32[8,128]{1,0:T(8,128)S(1)}) custom-call(bf16[2048,8,128]{2,1,0:T(8,128)(2,1)S(1)} %bitcast.29), custom_call_target="tpu_custom_call" | custom-call | bytes 1024 | tf_op jit(solution)/shard_map/relayout/pallas_call | solution.py:106
  18.7 2.0 %collective-permute-start.4 = (bf16[128,1920]{1,0:T(8,128)(2,1)S(1)}, bf16[128,1920]{1,0:T(8,128)(2,1)S(1)}, u32[]{:S(2)}, u32[]{:S(2)}) collective-permute-start(bf16[128,1920]{1,0:T(8,128)(2,1)S(1)} %collective-permute-done.3.refs_1_), channel_id=1, source_target_pairs={{0,32},{16,112},{32,64},{48,16},{64,96},{80,48},{96,0},{112,80},{1... | collective-permute-start | bytes 1474568 | tf_op jit(solution)/shard_map/ppermute | solution.py:258
  20.7 4.4 %collective-permute-done.1.refs_1_ = bf16[128,1920]{1,0:T(8,128)(2,1)S(1)} collective-permute-done((bf16[128,1920]{1,0:T(8,128)(2,1)}, bf16[128,1920]{1,0:T(8,128)(2,1)S(1)}, u32[]{:S(2)}, u32[]{:S(2)}) %collective-permute-start.1) | collective-permute-done | bytes 491552 | tf_op jit(solution)/shard_map/ppermute | solution.py:248
  30.5 8.4 %collective-permute-done.5.refs_3_ = bf16[128,1920]{1,0:T(8,128)(2,1)S(1)} collective-permute-done((bf16[128,1920]{1,0:T(8,128)(2,1)S(1)}, bf16[128,1920]{1,0:T(8,128)(2,1)S(1)}, u32[]{:S(2)}, u32[]{:S(2)}) %collective-permute-start.5) | collective-permute-done | bytes 491552 | tf_op jit(solution)/shard_map/ppermute | solution.py:258
  38.8 1.8 %collective-permute-done.6.refs_5_.refs_2_ = bf16[256,1920]{1,0:T(8,128)(2,1)S(1)} collective-permute-done((bf16[256,1920]{1,0:T(8,128)(2,1)S(1)}, bf16[256,1920]{1,0:T(8,128)(2,1)S(1)}, u32[]{:S(2)}, u32[]{:S(2)}) %collective-permute-start.6) | collective-permute-done | bytes 983072 | tf_op jit(solution)/shard_map/ppermute | solution.py:251
  47.4 5.1 %terms.3 = (bf16[128,1920]{1,0:T(8,128)(2,1)S(1)}, bf16[128,1920]{1,0:T(8,128)(2,1)S(1)}, bf16[128,1920]{1,0:T(8,128)(2,1)S(1)}, f32[128,1920]{1,0:T(8,128)S(1)}, s32[8,128]{1,0:T(8,128)S(1)}) custom-call(s32[24]{0:T(128)S(1)} %copy-done.2, bf16[256,1920]{1,0:T(8,128)(2,1)S(1)} %get-tuple-element.36.refs_1_, ...), custom_call_target="tpu_custom_call" | custom-call | flops 4026531840 | bytes 1024 | tf_op jit(solution)/shard_map/terms/pallas_call | solution.py:81
  54.0 3.2 %collective-permute-done.12.refs_1_ = bf16[256,1920]{1,0:T(8,128)(2,1)S(1)} collective-permute-done((bf16[256,1920]{1,0:T(8,128)(2,1)S(1)}, bf16[256,1920]{1,0:T(8,128)(2,1)S(1)}, u32[]{:S(2)}, u32[]{:S(2)}) %collective-permute-start.12) | collective-permute-done | bytes 983072 | tf_op jit(solution)/shard_map/ppermute | solution.py:251
  59.2 9.4 %terms.4 = (bf16[256,1920]{1,0:T(8,128)(2,1)S(1)}, bf16[256,1920]{1,0:T(8,128)(2,1)S(1)}, bf16[256,1920]{1,0:T(8,128)(2,1)S(1)}, f32[256,1920]{1,0:T(8,128)S(1)}, s32[8,128]{1,0:T(8,128)S(1)}) custom-call(s32[24]{0:T(128)S(1)} %copy-done.2, bf16[256,1920]{1,0:T(8,128)(2,1)S(1)} %collective-permute-done.12.refs_1_, ...), custom_call_target="tpu_custom_call" | custom-call | flops 8053063680 | bytes 1024 | tf_op jit(solution)/shard_map/terms/pallas_call | solution.py:81
  68.7 2.1 %collective-permute-start.14 = (bf16[256,1920]{1,0:T(8,128)(2,1)S(1)}, bf16[256,1920]{1,0:T(8,128)(2,1)S(1)}, u32[]{:S(2)}, u32[]{:S(2)}) collective-permute-start(bf16[256,1920]{1,0:T(8,128)(2,1)S(1)} %get-tuple-element.52), channel_id=1, source_target_pairs={{0,2},{1,3},{2,0},{3,1},{4,6},{5,7},{6,4},{7,5},{8,10},{9,11},{10,... | collective-permute-start | bytes 2949128 | tf_op jit(solution)/shard_map/ppermute | solution.py:248
  70.7 5.2 %collective-permute-done.10.refs_2_ = bf16[128,1920]{1,0:T(8,128)(2,1)S(1)} collective-permute-done((bf16[128,1920]{1,0:T(8,128)(2,1)S(1)}, bf16[128,1920]{1,0:T(8,128)(2,1)S(1)}, u32[]{:S(2)}, u32[]{:S(2)}) %collective-permute-start.10) | collective-permute-done | bytes 491552 | tf_op jit(solution)/shard_map/ppermute | solution.py:248
  78.8 5.1 %terms.5 = (bf16[128,1920]{1,0:T(8,128)(2,1)S(1)}, bf16[128,1920]{1,0:T(8,128)(2,1)S(1)}, bf16[128,1920]{1,0:T(8,128)(2,1)S(1)}, f32[128,1920]{1,0:T(8,128)S(1)}, s32[8,128]{1,0:T(8,128)S(1)}) custom-call(s32[24]{0:T(128)S(1)} %copy-done.2, bf16[256,1920]{1,0:T(8,128)(2,1)S(1)} %collective-permute-done.17.refs_1_, ...), custom_call_target="tpu_custom_call" | custom-call | flops 4026531840 | bytes 1024 | tf_op jit(solution)/shard_map/terms/pallas_call | solution.py:81
  83.9 2.1 %collective-permute-start.21 = (bf16[128,1920]{1,0:T(8,128)(2,1)S(1)}, bf16[128,1920]{1,0:T(8,128)(2,1)S(1)}, u32[]{:S(2)}, u32[]{:S(2)}) collective-permute-start(bf16[128,1920]{1,0:T(8,128)(2,1)S(1)} %get-tuple-element.60), channel_id=1, source_target_pairs={{0,2},{1,3},{2,0},{3,1},{4,6},{5,7},{6,4},{7,5},{8,10},{9,11},{10,... | collective-permute-start | bytes 1474568 | tf_op jit(solution)/shard_map/ppermute | solution.py:248
  86.0 2.0 %collective-permute-start.22 = (bf16[128,1920]{1,0:T(8,128)(2,1)S(1)}, bf16[128,1920]{1,0:T(8,128)(2,1)S(1)}, u32[]{:S(2)}, u32[]{:S(2)}) collective-permute-start(bf16[128,1920]{1,0:T(8,128)(2,1)S(1)} %get-tuple-element.61), channel_id=1, source_target_pairs={{0,1},{1,2},{2,3},{3,0},{4,5},{5,6},{6,7},{7,4},{8,9},{9,10},{10,1... | collective-permute-start | bytes 1474568 | tf_op jit(solution)/shard_map/ppermute | solution.py:248
  88.0 9.0 %collective-permute-done.15.refs_2_ = bf16[256,1920]{1,0:T(8,128)(2,1)S(1)} collective-permute-done((bf16[256,1920]{1,0:T(8,128)(2,1)S(1)}, bf16[256,1920]{1,0:T(8,128)(2,1)S(1)}, u32[]{:S(2)}, u32[]{:S(2)}) %collective-permute-start.15) | collective-permute-done | bytes 983072 | tf_op jit(solution)/shard_map/ppermute | solution.py:248
  97.0 6.1 %collective-permute-done.16.refs_3_ = bf16[256,1920]{1,0:T(8,128)(2,1)S(1)} collective-permute-done((bf16[256,1920]{1,0:T(8,128)(2,1)S(1)}, bf16[256,1920]{1,0:T(8,128)(2,1)S(1)}, u32[]{:S(2)}, u32[]{:S(2)}) %collective-permute-start.16) | collective-permute-done | bytes 983072 | tf_op jit(solution)/shard_map/ppermute | solution.py:248
  103.7 2.0 %collective-permute-start.20 = (bf16[128,1920]{1,0:T(8,128)(2,1)S(1)}, bf16[128,1920]{1,0:T(8,128)(2,1)S(1)}, u32[]{:S(2)}, u32[]{:S(2)}) collective-permute-start(bf16[128,1920]{1,0:T(8,128)(2,1)S(1)} %get-tuple-element.58), channel_id=1, source_target_pairs={{0,4},{1,5},{2,6},{3,7},{4,8},{5,9},{6,10},{7,11},{8,12},{9,13},{1... | collective-permute-start | bytes 1474568 | tf_op jit(solution)/shard_map/ppermute | solution.py:251
  105.7 6.6 %collective-permute-done.22.refs_2_ = bf16[128,1920]{1,0:T(8,128)(2,1)S(1)} collective-permute-done((bf16[128,1920]{1,0:T(8,128)(2,1)S(1)}, bf16[128,1920]{1,0:T(8,128)(2,1)S(1)}, u32[]{:S(2)}, u32[]{:S(2)}) %collective-permute-start.22) | collective-permute-done | bytes 491552 | tf_op jit(solution)/shard_map/ppermute | solution.py:248
  112.2 1.7 %collective-permute-done.23.refs_3_ = bf16[128,1920]{1,0:T(8,128)(2,1)S(1)} collective-permute-done((bf16[128,1920]{1,0:T(8,128)(2,1)S(1)}, bf16[128,1920]{1,0:T(8,128)(2,1)S(1)}, u32[]{:S(2)}, u32[]{:S(2)}) %collective-permute-start.23) | collective-permute-done | bytes 491552 | tf_op jit(solution)/shard_map/ppermute | solution.py:248
  116.3 2.1 %collective-permute-start.24 = (bf16[128,1920]{1,0:T(8,128)(2,1)S(1)}, bf16[128,1920]{1,0:T(8,128)(2,1)S(1)}, u32[]{:S(2)}, u32[]{:S(2)}) collective-permute-start(bf16[128,1920]{1,0:T(8,128)(2,1)S(1)} %get-tuple-element.64), channel_id=1, source_target_pairs={{0,8},{1,9},{2,10},{3,11},{4,12},{5,13},{6,14},{7,15},{8,0},{9,1},... | collective-permute-start | bytes 1474568 | tf_op jit(solution)/shard_map/ppermute | solution.py:251
  118.4 8.2 %collective-permute-done.24 = bf16[128,1920]{1,0:T(8,128)(2,1)S(1)} collective-permute-done((bf16[128,1920]{1,0:T(8,128)(2,1)S(1)}, bf16[128,1920]{1,0:T(8,128)(2,1)S(1)}, u32[]{:S(2)}, u32[]{:S(2)}) %collective-permute-start.24) | collective-permute-done | bytes 491552 | tf_op jit(solution)/shard_map/ppermute | solution.py:251
  (45 shorter events, 24.6 us)
Async XLA Ops:
  7.4 11.3 %collective-permute-start.3 = (bf16[128,1920]{1,0:T(8,128)(2,1)}, bf16[128,1920]{1,0:T(8,128)(2,1)S(1)}, u32[]{:S(2)}, u32[]{:S(2)}) collective-permute-start(bf16[128,1920]{1,0:T(8,128)(2,1)} %pick.1.refs_3_.refs_0_), channel_id=1, source_target_pairs={{0,32},{16,112},{32,64},{48,16},{64,96},{80,48},{96,0},{112,80},{1... | collective-permute-start | bytes 1474568 | tf_op jit(solution)/shard_map/ppermute | solution.py:258
  9.3 11.4 %collective-permute-start = (bf16[128,1920]{1,0:T(8,128)(2,1)}, bf16[128,1920]{1,0:T(8,128)(2,1)S(1)}, u32[]{:S(2)}, u32[]{:S(2)}) collective-permute-start(bf16[128,1920]{1,0:T(8,128)(2,1)} %pick.1.refs_3_.refs_0_), channel_id=1, source_target_pairs={{0,2},{1,3},{2,0},{3,1},{4,6},{5,7},{6,4},{7,5},{8,10},{9,11},{10,... | collective-permute-start | bytes 1474568 | tf_op jit(solution)/shard_map/ppermute | solution.py:248
  10.7 14.4 %collective-permute-start.1 = (bf16[128,1920]{1,0:T(8,128)(2,1)}, bf16[128,1920]{1,0:T(8,128)(2,1)S(1)}, u32[]{:S(2)}, u32[]{:S(2)}) collective-permute-start(bf16[128,1920]{1,0:T(8,128)(2,1)} %pick.1.refs_3_.refs_0_), channel_id=1, source_target_pairs={{0,3},{1,0},{2,1},{3,2},{4,7},{5,4},{6,5},{7,6},{8,11},{9,8},{10,9... | collective-permute-start | bytes 1474568 | tf_op jit(solution)/shard_map/ppermute | solution.py:248
  10.7 14.4 %collective-permute-start.2 = (bf16[128,1920]{1,0:T(8,128)(2,1)}, bf16[128,1920]{1,0:T(8,128)(2,1)S(1)}, u32[]{:S(2)}, u32[]{:S(2)}) collective-permute-start(bf16[128,1920]{1,0:T(8,128)(2,1)} %pick.1.refs_3_.refs_0_), channel_id=1, source_target_pairs={{0,1},{1,2},{2,3},{3,0},{4,5},{5,6},{6,7},{7,4},{8,9},{9,10},{10,1... | collective-permute-start | bytes 1474568 | tf_op jit(solution)/shard_map/ppermute | solution.py:248
  18.7 10.1 %collective-permute-start.4 = (bf16[128,1920]{1,0:T(8,128)(2,1)S(1)}, bf16[128,1920]{1,0:T(8,128)(2,1)S(1)}, u32[]{:S(2)}, u32[]{:S(2)}) collective-permute-start(bf16[128,1920]{1,0:T(8,128)(2,1)S(1)} %collective-permute-done.3.refs_1_), channel_id=1, source_target_pairs={{0,32},{16,112},{32,64},{48,16},{64,96},{80,48},{96,0},{112,80},{1... | collective-permute-start | bytes 1474568 | tf_op jit(solution)/shard_map/ppermute | solution.py:258
  25.2 15.4 %collective-permute-start.6 = (bf16[256,1920]{1,0:T(8,128)(2,1)S(1)}, bf16[256,1920]{1,0:T(8,128)(2,1)S(1)}, u32[]{:S(2)}, u32[]{:S(2)}) collective-permute-start(bf16[256,1920]{1,0:T(8,128)(2,1)S(1)} %get-tuple-element.37.refs_2_), channel_id=1, source_target_pairs={{0,4},{1,5},{2,6},{3,7},{4,8},{5,9},{6,10},{7,11},{8,12},{9,13},{1... | collective-permute-start | bytes 2949128 | tf_op jit(solution)/shard_map/ppermute | solution.py:251
  26.9 14.1 %collective-permute-start.7 = (bf16[256,1920]{1,0:T(8,128)(2,1)S(1)}, bf16[256,1920]{1,0:T(8,128)(2,1)S(1)}, u32[]{:S(2)}, u32[]{:S(2)}) collective-permute-start(bf16[256,1920]{1,0:T(8,128)(2,1)S(1)} %get-tuple-element.36.refs_1_), channel_id=1, source_target_pairs={{0,12},{1,13},{2,14},{3,15},{4,0},{5,1},{6,2},{7,3},{8,4},{9,5},{1... | collective-permute-start | bytes 2949128 | tf_op jit(solution)/shard_map/ppermute | solution.py:251
  28.8 10.0 %collective-permute-start.5 = (bf16[128,1920]{1,0:T(8,128)(2,1)S(1)}, bf16[128,1920]{1,0:T(8,128)(2,1)S(1)}, u32[]{:S(2)}, u32[]{:S(2)}) collective-permute-start(bf16[128,1920]{1,0:T(8,128)(2,1)S(1)} %collective-permute-done.4.refs_2_), channel_id=1, source_target_pairs={{0,32},{16,112},{32,64},{48,16},{64,96},{80,48},{96,0},{112,80},{1... | collective-permute-start | bytes 1474568 | tf_op jit(solution)/shard_map/ppermute | solution.py:258
  41.2 16.0 %collective-permute-start.12 = (bf16[256,1920]{1,0:T(8,128)(2,1)S(1)}, bf16[256,1920]{1,0:T(8,128)(2,1)S(1)}, u32[]{:S(2)}, u32[]{:S(2)}) collective-permute-start(bf16[256,1920]{1,0:T(8,128)(2,1)S(1)} %get-tuple-element.36.refs_1_), channel_id=1, source_target_pairs={{0,4},{1,5},{2,6},{3,7},{4,8},{5,9},{6,10},{7,11},{8,12},{9,13},{1... | collective-permute-start | bytes 2949128 | tf_op jit(solution)/shard_map/ppermute | solution.py:251
  42.9 14.9 %collective-permute-start.13 = (bf16[256,1920]{1,0:T(8,128)(2,1)S(1)}, bf16[256,1920]{1,0:T(8,128)(2,1)S(1)}, u32[]{:S(2)}, u32[]{:S(2)}) collective-permute-start(bf16[256,1920]{1,0:T(8,128)(2,1)S(1)} %get-tuple-element.37.refs_2_), channel_id=1, source_target_pairs={{0,12},{1,13},{2,14},{3,15},{4,0},{5,1},{6,2},{7,3},{8,4},{9,5},{1... | collective-permute-start | bytes 2949128 | tf_op jit(solution)/shard_map/ppermute | solution.py:251
  44.5 34.3 %collective-permute-start.17 = (bf16[256,1920]{1,0:T(8,128)(2,1)S(1)}, bf16[256,1920]{1,0:T(8,128)(2,1)S(1)}, u32[]{:S(2)}, u32[]{:S(2)}) collective-permute-start(bf16[256,1920]{1,0:T(8,128)(2,1)S(1)} %collective-permute-done.7.refs_6_.refs_3_), channel_id=1, source_target_pairs={{0,12},{1,13},{2,14},{3,15},{4,0},{5,1},{6,2},{7,3},{8,4},{9,5},{1... | collective-permute-start | bytes 2949128 | tf_op jit(solution)/shard_map/ppermute | solution.py:251
  46.2 32.6 %collective-permute-start.18 = (bf16[256,1920]{1,0:T(8,128)(2,1)S(1)}, bf16[256,1920]{1,0:T(8,128)(2,1)S(1)}, u32[]{:S(2)}, u32[]{:S(2)}) collective-permute-start(bf16[256,1920]{1,0:T(8,128)(2,1)S(1)} %collective-permute-done.6.refs_5_.refs_2_), channel_id=1, source_target_pairs={{0,4},{1,5},{2,6},{3,7},{4,8},{5,9},{6,10},{7,11},{8,12},{9,13},{1... | collective-permute-start | bytes 2949128 | tf_op jit(solution)/shard_map/ppermute | solution.py:251
  52.5 16.2 %collective-permute-start.9 = (bf16[128,1920]{1,0:T(8,128)(2,1)S(1)}, bf16[128,1920]{1,0:T(8,128)(2,1)S(1)}, u32[]{:S(2)}, u32[]{:S(2)}) collective-permute-start(bf16[128,1920]{1,0:T(8,128)(2,1)S(1)} %get-tuple-element.45), channel_id=1, source_target_pairs={{0,2},{1,3},{2,0},{3,1},{4,6},{5,7},{6,4},{7,5},{8,10},{9,11},{10,... | collective-permute-start | bytes 1474568 | tf_op jit(solution)/shard_map/ppermute | solution.py:248
  57.2 18.7 %collective-permute-start.10 = (bf16[128,1920]{1,0:T(8,128)(2,1)S(1)}, bf16[128,1920]{1,0:T(8,128)(2,1)S(1)}, u32[]{:S(2)}, u32[]{:S(2)}) collective-permute-start(bf16[128,1920]{1,0:T(8,128)(2,1)S(1)} %get-tuple-element.46), channel_id=1, source_target_pairs={{0,1},{1,2},{2,3},{3,0},{4,5},{5,6},{6,7},{7,4},{8,9},{9,10},{10,1... | collective-permute-start | bytes 1474568 | tf_op jit(solution)/shard_map/ppermute | solution.py:248
  57.8 18.5 %collective-permute-start.11 = (bf16[128,1920]{1,0:T(8,128)(2,1)S(1)}, bf16[128,1920]{1,0:T(8,128)(2,1)S(1)}, u32[]{:S(2)}, u32[]{:S(2)}) collective-permute-start(bf16[128,1920]{1,0:T(8,128)(2,1)S(1)} %get-tuple-element.47), channel_id=1, source_target_pairs={{0,3},{1,0},{2,1},{3,2},{4,7},{5,4},{6,5},{7,6},{8,11},{9,8},{10,9... | collective-permute-start | bytes 1474568 | tf_op jit(solution)/shard_map/ppermute | solution.py:248
  68.7 19.3 %collective-permute-start.14 = (bf16[256,1920]{1,0:T(8,128)(2,1)S(1)}, bf16[256,1920]{1,0:T(8,128)(2,1)S(1)}, u32[]{:S(2)}, u32[]{:S(2)}) collective-permute-start(bf16[256,1920]{1,0:T(8,128)(2,1)S(1)} %get-tuple-element.52), channel_id=1, source_target_pairs={{0,2},{1,3},{2,0},{3,1},{4,6},{5,7},{6,4},{7,5},{8,10},{9,11},{10,... | collective-permute-start | bytes 2949128 | tf_op jit(solution)/shard_map/ppermute | solution.py:248
  75.9 21.1 %collective-permute-start.15 = (bf16[256,1920]{1,0:T(8,128)(2,1)S(1)}, bf16[256,1920]{1,0:T(8,128)(2,1)S(1)}, u32[]{:S(2)}, u32[]{:S(2)}) collective-permute-start(bf16[256,1920]{1,0:T(8,128)(2,1)S(1)} %get-tuple-element.53), channel_id=1, source_target_pairs={{0,1},{1,2},{2,3},{3,0},{4,5},{5,6},{6,7},{7,4},{8,9},{9,10},{10,1... | collective-permute-start | bytes 2949128 | tf_op jit(solution)/shard_map/ppermute | solution.py:248
  76.3 26.9 %collective-permute-start.16 = (bf16[256,1920]{1,0:T(8,128)(2,1)S(1)}, bf16[256,1920]{1,0:T(8,128)(2,1)S(1)}, u32[]{:S(2)}, u32[]{:S(2)}) collective-permute-start(bf16[256,1920]{1,0:T(8,128)(2,1)S(1)} %get-tuple-element.54), channel_id=1, source_target_pairs={{0,3},{1,0},{2,1},{3,2},{4,7},{5,4},{6,5},{7,6},{8,11},{9,8},{10,9... | collective-permute-start | bytes 2949128 | tf_op jit(solution)/shard_map/ppermute | solution.py:248
  83.9 21.8 %collective-permute-start.21 = (bf16[128,1920]{1,0:T(8,128)(2,1)S(1)}, bf16[128,1920]{1,0:T(8,128)(2,1)S(1)}, u32[]{:S(2)}, u32[]{:S(2)}) collective-permute-start(bf16[128,1920]{1,0:T(8,128)(2,1)S(1)} %get-tuple-element.60), channel_id=1, source_target_pairs={{0,2},{1,3},{2,0},{3,1},{4,6},{5,7},{6,4},{7,5},{8,10},{9,11},{10,... | collective-permute-start | bytes 1474568 | tf_op jit(solution)/shard_map/ppermute | solution.py:248
  86.0 26.3 %collective-permute-start.22 = (bf16[128,1920]{1,0:T(8,128)(2,1)S(1)}, bf16[128,1920]{1,0:T(8,128)(2,1)S(1)}, u32[]{:S(2)}, u32[]{:S(2)}) collective-permute-start(bf16[128,1920]{1,0:T(8,128)(2,1)S(1)} %get-tuple-element.61), channel_id=1, source_target_pairs={{0,1},{1,2},{2,3},{3,0},{4,5},{5,6},{6,7},{7,4},{8,9},{9,10},{10,1... | collective-permute-start | bytes 1474568 | tf_op jit(solution)/shard_map/ppermute | solution.py:248
  88.0 26.0 %collective-permute-start.23 = (bf16[128,1920]{1,0:T(8,128)(2,1)S(1)}, bf16[128,1920]{1,0:T(8,128)(2,1)S(1)}, u32[]{:S(2)}, u32[]{:S(2)}) collective-permute-start(bf16[128,1920]{1,0:T(8,128)(2,1)S(1)} %get-tuple-element.62), channel_id=1, source_target_pairs={{0,3},{1,0},{2,1},{3,2},{4,7},{5,4},{6,5},{7,6},{8,11},{9,8},{10,9... | collective-permute-start | bytes 1474568 | tf_op jit(solution)/shard_map/ppermute | solution.py:248
  103.6 11.4 %collective-permute-start.19 = (bf16[128,1920]{1,0:T(8,128)(2,1)S(1)}, bf16[128,1920]{1,0:T(8,128)(2,1)S(1)}, u32[]{:S(2)}, u32[]{:S(2)}) collective-permute-start(bf16[128,1920]{1,0:T(8,128)(2,1)S(1)} %get-tuple-element.57), channel_id=1, source_target_pairs={{0,12},{1,13},{2,14},{3,15},{4,0},{5,1},{6,2},{7,3},{8,4},{9,5},{1... | collective-permute-start | bytes 1474568 | tf_op jit(solution)/shard_map/ppermute | solution.py:251
  103.7 12.0 %collective-permute-start.20 = (bf16[128,1920]{1,0:T(8,128)(2,1)S(1)}, bf16[128,1920]{1,0:T(8,128)(2,1)S(1)}, u32[]{:S(2)}, u32[]{:S(2)}) collective-permute-start(bf16[128,1920]{1,0:T(8,128)(2,1)S(1)} %get-tuple-element.58), channel_id=1, source_target_pairs={{0,4},{1,5},{2,6},{3,7},{4,8},{5,9},{6,10},{7,11},{8,12},{9,13},{1... | collective-permute-start | bytes 1474568 | tf_op jit(solution)/shard_map/ppermute | solution.py:251
  116.3 10.3 %collective-permute-start.24 = (bf16[128,1920]{1,0:T(8,128)(2,1)S(1)}, bf16[128,1920]{1,0:T(8,128)(2,1)S(1)}, u32[]{:S(2)}, u32[]{:S(2)}) collective-permute-start(bf16[128,1920]{1,0:T(8,128)(2,1)S(1)} %get-tuple-element.64), channel_id=1, source_target_pairs={{0,8},{1,9},{2,10},{3,11},{4,12},{5,13},{6,14},{7,15},{8,0},{9,1},... | collective-permute-start | bytes 1474568 | tf_op jit(solution)/shard_map/ppermute | solution.py:251
  (4 other events, 53.2 us)
